TPU v7x, 32 devices: a whole 2x2x4 slice. The times are simulated.
32 devices in a mesh: seq: 8 (over z, x), head: 4 (over y, core).
Axes of the slice: x: 2, y: 2, z: 4, core: 2. Of those that a mesh axis runs over, the one named last changes fastest.
Arguments:
- hidden_in: bfloat16 [2048, 2048], P('seq'), may hold values from -6 to 6
- w_qk: bfloat16 [2048, 2, 2048], P(None, None, 'head'), may hold values from -0.125 to 0.125
- w_value: bfloat16 [2048, 4096], P(None, 'head'), may hold values from -0.125 to 0.125
- w_outgate: bfloat16 [2048, 4096], P(None, 'head'), may hold values from -0.125 to 0.125
- w_ba: bfloat16 [2048, 2, 32], P(None, None, 'head'), may hold values from -0.125 to 0.125
- conv_qk: bfloat16 [4, 2, 2048], P(None, None, 'head'), may hold values from -3 to 3
- conv_value: bfloat16 [4, 4096], P(None, 'head'), may hold values from -3 to 3
- hist_qk: bfloat16 [3, 2, 2048], P(None, None, 'head'), may hold values from -6 to 6
- hist_value: bfloat16 [3, 4096], P(None, 'head'), may hold values from -6 to 6
- a_log: float32 [32], P('head'), may hold values from -11 to -3
- dt_bias: float32 [32], P('head'), may hold values from -1 to 1
- beta_bias: float32 [32], P('head'), may hold values from -1 to 1
- state_in: float32 [32, 128, 128], P('head'), may hold values from -0.6 to 0.6
- norm_gain: float32 [128], replicated, may hold values from 0.5 to 1.5
- w_out: bfloat16 [4096, 2048], P('head'), may hold values from -0.09375 to 0.09375
Outputs:
- mixed: bfloat16 [2048, 2048], P('seq', 'head')
- checkpoints: float32 [8, 32, 128, 128], P('seq', 'head')
All inputs are finite; a program needn't handle non-finite values.
Results may differ from a plain program's by a relative error of at most 0.015.
Values may be sent and summed in bfloat16 or wider, within the bound.
No kernel may reach another device: no remote copies, remote signals or barrier semaphores. Data moves between devices by JAX's collectives and lax.ppermute only.
A program may use at most 64 MiB of HBM per device.

v0:
```python
import functools

import jax
import jax.numpy as jnp
from jax import lax
from jax.experimental import pallas as pl
from jax.experimental.pallas import tpu as pltpu
from jax.sharding import PartitionSpec as P

KD = 128
DV = 128
HALF = 128
HALO = 8
F32 = jnp.float32
BF16 = jnp.bfloat16
VMEM = pl.BlockSpec(memory_space=pltpu.VMEM)
SMEM = pl.BlockSpec(memory_space=pltpu.SMEM)


def dot(left, right):
    return jnp.dot(left, right, preferred_element_type=F32)


def dot_nt(left, right):
    return lax.dot_general(left, right, (((1,), (1,)), ((), ())), preferred_element_type=F32)


def split(values):
    high = values.astype(BF16)
    return high, (values - high.astype(F32)).astype(BF16)


def fine_dot(left, right):
    left_hi, left_lo = split(left)
    right_hi, right_lo = split(right)
    return dot(left_hi, right_hi) + (dot(left_hi, right_lo) + dot(left_lo, right_hi))


def silu(values):
    return values / (1.0 + jnp.exp(-values))


def unit_rows(values):
    return values * lax.rsqrt(jnp.sum(values * values, axis=-1, keepdims=True) + 1e-06)


def conv_rows(block, history, weight, first):
    rows = block.shape[0] - HALO
    taps = weight.shape[0]
    start = HALO - (taps - 1)
    halo = jnp.where(first, history, block[:HALO])
    joined = jnp.concatenate([halo, block[HALO:]], 0)
    total = weight[0:1] * joined[start : start + rows]
    for tap in range(1, taps):
        total = total + weight[tap : tap + 1] * joined[start + tap : start + tap + rows]
    return silu(total)


def call(kernel, out_shape, in_specs, flops, moved, scratch=()):
    return pl.pallas_call(
        kernel,
        out_shape=out_shape,
        in_specs=in_specs,
        out_specs=jax.tree.map(lambda _: VMEM, out_shape),
        scratch_shapes=list(scratch),
        compiler_params=pltpu.CompilerParams(vmem_limit_bytes=40 << 20),
        cost_estimate=pl.CostEstimate(flops=flops, bytes_accessed=moved, transcendentals=0),
    )


def shape(dims, dtype):
    return jax.ShapeDtypeStruct(dims, dtype)


def prepare_kernel(
    place, qk, value, gates, hist_qk, hist_value, conv_qk, conv_value, params,
    keys_out, solved_out, maps_out, send_out, rows_out, cols_out,
):
    heads = gates.shape[1]
    rows = gates.shape[2]
    key_heads = heads // 2
    first = place[0] == 0
    bit = place[1]
    strength = jax.nn.sigmoid(gates[0].astype(F32) + params[:, 2:3])
    decay_in = gates[1].astype(F32) + params[:, 1:2]
    soft = jnp.maximum(decay_in, 0.0) + jnp.log1p(jnp.exp(-jnp.abs(decay_in)))
    log_decay = -jnp.exp(params[:, 0:1]) * soft
    line = lax.broadcasted_iota(jnp.int32, (rows, rows), 0)
    across = lax.broadcasted_iota(jnp.int32, (rows, rows), 1)
    upper = jnp.where(line <= across, 1.0, 0.0).astype(BF16)
    high, low = split(log_decay)
    lowest = (log_decay - high.astype(F32) - low.astype(F32)).astype(BF16)
    cumul = dot(high, upper) + (dot(low, upper) + dot(lowest, upper))
    fade = jnp.exp(cumul)
    to_end = jnp.exp(cumul[:, rows - 1 : rows] - cumul)
    pad = jnp.zeros((128 - 4 * heads, rows), F32)
    cols = jnp.concatenate([cumul, strength, strength * fade, fade, pad], 0).T
    rows_out[...] = cumul
    cols_out[...] = cols

    line = lax.broadcasted_iota(jnp.int32, (HALF, HALF), 0)
    across = lax.broadcasted_iota(jnp.int32, (HALF, HALF), 1)
    below = line > across
    eye = jnp.where(line == across, 1.0, 0.0)
    parts = rows // HALF
    lowers = []
    rhs = []
    ends = []
    for key_head in range(key_heads):
        lanes = slice(key_head * KD, (key_head + 1) * KD)
        key = unit_rows(
            conv_rows(
                qk[1, :, lanes].astype(F32),
                hist_qk[1, :, lanes].astype(F32),
                conv_qk[1, :, lanes].astype(F32),
                first,
            )
        )
        key_low = key.astype(BF16)
        keys_out[key_head] = key_low
        dots = dot_nt(key_low, key_low)
        key_t = key.T
        for head in (2 * key_head, 2 * key_head + 1):
            lanes = slice(head * DV, (head + 1) * DV)
            val = conv_rows(
                value[:, lanes].astype(F32),
                hist_value[:, lanes].astype(F32),
                conv_value[:, lanes].astype(F32),
                first,
            )
            col = cols[:, head : head + 1]
            beta = cols[:, heads + head : heads + head + 1]
            beta_fade = cols[:, 2 * heads + head : 2 * heads + head + 1]
            lower = {}
            for i in range(parts):
                for j in range(i + 1):
                    a = slice(i * HALF, (i + 1) * HALF)
                    b = slice(j * HALF, (j + 1) * HALF)
                    spread = jnp.exp(jnp.minimum(col[a] - cumul[head : head + 1, b], 0.0))
                    entry = beta[a] * spread * dots[a, b]
                    lower[i, j] = jnp.where(below, entry, 0.0) if i == j else entry
            lowers.append(lower)
            rhs.append(jnp.concatenate([beta_fade * key, beta * val], 1))
            ends.append((key_t * to_end[head : head + 1]).astype(BF16))

    names = [(head, i) for head in range(heads) for i in range(parts)]
    tri = {}
    for head, i in names:
        near = (line // 2) == (across // 2)
        tri[head, i] = eye - jnp.where(near, lowers[head][i, i], 0.0)
    size = 2
    while size < HALF:
        mask = ((line // (2 * size)) == (across // (2 * size))) & ((line // size) != (across // size))
        low = {n: tri[n].astype(BF16) for n in names}
        inner = {
            (head, i): dot(jnp.where(mask, lowers[head][i, i], 0.0).astype(BF16), low[head, i]).astype(BF16)
            for head, i in names
        }
        tri = {n: tri[n] - dot(low[n], inner[n]) for n in names}
        size *= 2
    tri = {n: tri[n].astype(BF16) for n in names}
    solved = [[] for _ in range(heads)]
    for i in range(parts):
        for head in range(heads):
            need = rhs[head][i * HALF : (i + 1) * HALF]
            for j in range(i):
                need = need - fine_dot(lowers[head][i, j], solved[head][j])
            solved[head].append(dot(tri[head, i], need.astype(BF16)))
    half = heads // 2
    for head in range(heads):
        both = jnp.concatenate(solved[head], 0).astype(BF16)
        solved_out[head] = both
        ended = dot(ends[head], both)
        fade_end = fade[head : head + 1, rows - 1 : rows]
        own = jnp.concatenate([eye * fade_end - ended[:, :KD], ended[:, KD:]], 1).astype(BF16)
        maps_out[head] = own
    send_out[...] = maps_out[pl.ds((1 - bit) * half, half)]


def query_kernel(
    place, qk, keys, solved, cumul, cols, hist_qk, conv_qk, gate_z, gain,
    reads_out, local_out, gate_out,
):
    heads, rows = cumul.shape
    first = place[0] == 0
    line = lax.broadcasted_iota(jnp.int32, (rows, rows), 0)
    across = lax.broadcasted_iota(jnp.int32, (rows, rows), 1)
    within = line >= across
    for key_head in range(heads // 2):
        lanes = slice(key_head * KD, (key_head + 1) * KD)
        query = unit_rows(
            conv_rows(
                qk[0, :, lanes].astype(F32),
                hist_qk[0, :, lanes].astype(F32),
                conv_qk[0, :, lanes].astype(F32),
                first,
            )
        ) * (KD**-0.5)
        dots = dot_nt(query.astype(BF16), keys[key_head])
        for head in (2 * key_head, 2 * key_head + 1):
            col = cols[:, head : head + 1]
            fade = cols[:, 3 * heads + head : 3 * heads + head + 1]
            spread = jnp.exp(jnp.minimum(col - cumul[head : head + 1], 0.0))
            attend = jnp.where(within, spread * dots, 0.0).astype(BF16)
            part = dot(attend, solved[head])
            reads_out[head] = (fade * query - part[:, :KD]).astype(BF16)
            local_out[head] = part[:, KD:]
            lanes = slice(head * DV, (head + 1) * DV)
            gate_out[head] = silu(gate_z[:, lanes].astype(F32)) * gain[...]


def join(outer, inner):
    product = dot(outer[:, :KD], inner)
    return jnp.concatenate([product[:, :KD], product[:, KD:] + outer[:, KD:].astype(F32)], 1)


def act(outer, state):
    return dot(outer[:, :KD], state) + outer[:, KD:].astype(F32)


def pair_kernel(place, maps, received, total_out):
    bit = place[1]
    half = received.shape[0]
    for j in range(half):
        mine, other = maps[bit * half + j], received[j]
        low, high = jnp.where(bit == 1, other, mine), jnp.where(bit == 1, mine, other)
        total_out[j] = join(high, low).astype(BF16)


def level_kernel(level, last, *refs):
    if level == 1:
        place, total, received, state_in, total_out, prefix_out = refs
    else:
        place, total, received, prefix, state_in, total_out, prefix_out = refs
    bit = place[level + 1]
    half = total.shape[0]
    line = lax.broadcasted_iota(jnp.int32, (KD, KD + DV), 0)
    across = lax.broadcasted_iota(jnp.int32, (KD, KD + DV), 1)
    same = jnp.where(line == across, 1.0, 0.0).astype(BF16)
    for j in range(half):
        mine, other = total[j], received[j]
        low, high = jnp.where(bit == 1, other, mine), jnp.where(bit == 1, mine, other)
        if level == 1:
            prefix_out[j] = jnp.where(bit == 1, low, same)
        else:
            prefix_out[j] = jnp.where(bit == 1, join(prefix[j], low).astype(BF16), prefix[j])
        if last:
            state = state_in[place[1] * half + j].astype(BF16)
            total_out[j] = act(high, act(low, state).astype(BF16)).astype(BF16)
        else:
            total_out[j] = join(high, low).astype(BF16)


def enter_kernel(top, place, prefix, state_in, came, maps, received, mine_out, send_out):
    bit = place[1]
    half = prefix.shape[0]
    for j in range(half):
        start = jnp.where(place[top + 1] == 1, came[j], state_in[bit * half + j].astype(BF16))
        entering = act(prefix[j], start).astype(BF16)
        low = jnp.where(bit == 1, received[j], maps[bit * half + j])
        passed = act(low, entering).astype(BF16)
        mine_out[j] = jnp.where(bit == 1, passed, entering)
        send_out[j] = jnp.where(bit == 1, entering, passed)


def output_kernel(
    place, mine, came, reads, local_reads, gate, w_out, send_out, keep_out, states_out, normed,
):
    bit = place[1]
    core = place[0]
    half = mine.shape[0]
    heads = 2 * half
    blocks = send_out.shape[0]
    width = send_out.shape[2]
    for j in range(heads):
        if j < half:
            head, state = bit * half + j, mine[j]
        else:
            head, state = (1 - bit) * half + (j - half), came[j - half]
        states_out[head] = state
        out = local_reads[head] + dot(reads[head], state)
        scale = lax.rsqrt(jnp.mean(out * out, axis=-1, keepdims=True) + 1e-06)
        lanes = pl.ds(pl.multiple_of(head * DV, DV), DV)
        normed[:, lanes] = (out * scale * gate[head]).astype(BF16)
    for j in range(blocks):
        for side, ref in ((1 - core, send_out), (core, keep_out)):
            lanes = pl.ds(pl.multiple_of((2 * j + side) * width, width), width)
            ref[j] = dot(normed[...], w_out[:, lanes]).astype(BF16)


def merge_kernel(place, keep, came, send_out, keep_out):
    bit = place[0]
    blocks = send_out.shape[0]
    for j in range(blocks):
        away, home = 2 * j + 1 - bit, 2 * j + bit
        send_out[j] = (keep[away].astype(F32) + came[away].astype(F32)).astype(BF16)
        keep_out[j] = keep[home].astype(F32) + came[home].astype(F32)


def checkpoint_kernel(maps, states, out):
    for head in range(maps.shape[0]):
        out[0, head] = act(maps[head], states[head])


def swapped(value, axis, step):
    count = lax.axis_size(axis)
    return lax.ppermute(value, axis, [(i, i ^ step) for i in range(count)])


def local(
    hidden_in, w_qk, w_value, w_outgate, w_ba, conv_qk, conv_value, hist_qk, hist_value,
    a_log, dt_bias, beta_bias, state_in, norm_gain, w_out,
):
    rows, width = hidden_in.shape
    key_cols = w_qk.shape[2]
    heads = a_log.shape[0]
    half = heads // 2
    taps = conv_value.shape[0]
    n_seq = lax.axis_size("seq")
    n_head = lax.axis_size("head")
    levels = n_seq.bit_length() - 1
    seq = lax.axis_index("seq")
    col = lax.axis_index("head")
    place = jnp.stack([seq] + [(seq >> level) & 1 for level in range(levels)]).astype(jnp.int32)

    halo = lax.ppermute(
        hidden_in[rows - HALO :], "seq", [(i, (i + 1) % n_seq) for i in range(n_seq)]
    )
    joined = jnp.concatenate([halo, hidden_in], 0)
    qk = jnp.einsum("td,dce->cte", joined, w_qk, preferred_element_type=F32).astype(BF16)
    value = jnp.dot(joined, w_value, preferred_element_type=F32).astype(BF16)
    gates = jnp.einsum("td,dch->cht", hidden_in, w_ba, preferred_element_type=F32).astype(BF16)
    params = jnp.stack([a_log, dt_bias, beta_bias], 1)
    hist_qk = jnp.pad(jnp.moveaxis(hist_qk, 1, 0), ((0, 0), (HALO - taps + 1, 0), (0, 0)))
    hist_value = jnp.pad(hist_value, ((HALO - taps + 1, 0), (0, 0)))
    conv_qk = jnp.moveaxis(conv_qk, 1, 0)

    keys, solved, maps, send, cumul, cols = call(
        prepare_kernel,
        (
            shape((half, rows, KD), BF16),
            shape((heads, rows, KD + DV), BF16),
            shape((heads, KD, KD + DV), BF16),
            shape((half, KD, KD + DV), BF16),
            shape((heads, rows), F32),
            shape((rows, 128), F32),
        ),
        [SMEM] + [VMEM] * 8,
        10**10,
        4 << 20,
    )(place, qk, value, gates, hist_qk, hist_value, conv_qk, conv_value, params)

    received = swapped(send, "seq", 1)
    gate_z = jnp.dot(hidden_in, w_outgate, preferred_element_type=F32).astype(BF16)
    reads, local_reads, gate = call(
        query_kernel,
        (
            shape((heads, rows, KD), BF16),
            shape((heads, rows, DV), F32),
            shape((heads, rows, DV), F32),
        ),
        [SMEM] + [VMEM] * 9,
        4 * 10**9,
        6 << 20,
    )(place, qk, keys, solved, cumul, cols, hist_qk, conv_qk, gate_z, norm_gain.reshape(1, DV))

    map_shape = shape((half, KD, KD + DV), BF16)
    state_shape = shape((half, KD, DV), BF16)
    total = call(pair_kernel, map_shape, [SMEM, VMEM, VMEM], 10**8, 1 << 20)(place, maps, received)
    prefix = ()
    for level in range(1, levels - 1):
        other = swapped(total, "seq", 1 << level)
        last = level == levels - 2
        total, prefix = call(
            functools.partial(level_kernel, level, last),
            (state_shape if last else map_shape, map_shape),
            [SMEM] + [VMEM] * (3 if level == 1 else 4),
            10**8,
            1 << 20,
        )(place, total, other, *prefix, state_in)
        prefix = (prefix,)
    came = swapped(total, "seq", 1 << (levels - 1))
    mine, send_state = call(
        functools.partial(enter_kernel, levels - 1),
        (state_shape, state_shape),
        [SMEM] + [VMEM] * 5,
        10**8,
        1 << 20,
    )(place, prefix[0], state_in, came, maps, received)
    other_state = swapped(send_state, "seq", 1)

    out_width = w_out.shape[1] // n_head
    blocks = n_head // 2
    side = jnp.stack([col & 1, place[1]]).astype(jnp.int32)
    send_out, keep, states = call(
        output_kernel,
        (
            shape((blocks, rows, out_width), BF16),
            shape((blocks, rows, out_width), BF16),
            shape((heads, KD, DV), BF16),
        ),
        [SMEM] + [VMEM] * 6,
        10**9,
        8 << 20,
        [pltpu.VMEM((rows, heads * DV), BF16)],
    )(side, mine, other_state, reads, local_reads, gate, w_out)
    came_out = swapped(send_out, "head", 1)
    step = 2
    while step < n_head:
        blocks //= 2
        send_out, keep = call(
            merge_kernel,
            (shape((blocks, rows, out_width), BF16), shape((blocks, rows, out_width), F32)),
            [SMEM, VMEM, VMEM],
            10**6,
            2 << 20,
        )(((col // step) & 1).astype(jnp.int32).reshape(1), keep, came_out)
        came_out = swapped(send_out, "head", step)
        step *= 2
    checkpoint = call(
        checkpoint_kernel, shape((1, heads, KD, DV), F32), [VMEM, VMEM], 10**8, 2 << 20
    )(maps, states)
    mixed = (keep[0].astype(F32) + came_out[0].astype(F32)).astype(BF16)
    return (mixed, checkpoint)


def solution(mesh):
    return jax.shard_map(
        local,
        mesh=mesh,
        in_specs=(
            P("seq", None),
            P(None, None, "head"),
            P(None, "head"),
            P(None, "head"),
            P(None, None, "head"),
            P(None, None, "head"),
            P(None, "head"),
            P(None, None, "head"),
            P(None, "head"),
            P("head"),
            P("head"),
            P("head"),
            P("head", None, None),
            P(),
            P("head", None),
        ),
        out_specs=(P("seq", "head"), P("seq", "head", None, None)),
        check_vma=False,
    )
```

profile of v0, /device:TPU:0, one launch (start us, length us, event | category | flops | bytes accessed | tf_op | source)
XLA Modules:
  0.0 66.8 jit_solution(6312968530382937099)
XLA Ops:
  0.6 0.8 %slice.3 = bf16[8,2048]{1,0:T(8,128)(2,1)S(1)} slice(bf16[256,2048]{1,0:T(8,128)(2,1)} %param.15), slice={[248:256], [0:2048]} | slice | bytes 65536 | tf_op jit(solution)/shard_map/slice | solution.py:327
  1.4 2.9 %collective-permute-start = (bf16[8,2048]{1,0:T(8,128)(2,1)S(1)}, bf16[8,2048]{1,0:T(8,128)(2,1)S(1)}, u32[]{:S(2)}, u32[]{:S(2)}) collective-permute-start(bf16[8,2048]{1,0:T(8,128)(2,1)S(1)} %slice.3), channel_id=1, source_target_pairs={{0,4},{4,8},{8,12},{12,16},{16,20},{20,24},{24,28},{28,0},{1,5},{5... | collective-permute-start | bytes 98312 | tf_op jit(solution)/shard_map/ppermute | solution.py:326
  4.4 1.6 %convolution_convert_fusion.2.gates = bf16[2,8,256]{2,1,0:T(8,128)(2,1)S(1)} fusion(bf16[2048,2,8]{0,2,1:T(8,128)(2,1)S(1)} %copy-done, bf16[256,2048]{1,0:T(8,128)(2,1)} %param.15), kind=kOutput, calls=%fused_computation.6 | convolution fusion | flops 16781312 | bytes 1122304 | tf_op jit(solution)/shard_map/td,dch->cht/dot_general | solution.py:332
  6.0 0.7 %copy.22 = f32[8,1]{1,0:T(8,128)S(1)} copy(f32[8,1]{0,1:T(1,128)} %bitcast.35) | data formatting | bytes 64 | tf_op jit(solution)/shard_map/stack | solution.py:333
  6.7 0.7 %copy.21 = f32[8,1]{1,0:T(8,128)S(1)} copy(f32[8,1]{0,1:T(1,128)} %bitcast.36) | data formatting | bytes 64 | tf_op jit(solution)/shard_map/stack | solution.py:333
  7.5 0.7 %copy.20 = f32[8,1]{1,0:T(8,128)S(1)} copy(f32[8,1]{0,1:T(1,128)} %bitcast.37) | data formatting | bytes 64 | tf_op jit(solution)/shard_map/stack | solution.py:333
  8.3 0.7 %copy.32 = bf16[3,2,512]{2,0,1:T(4,128)(2,1)S(1)} copy(bf16[3,2,512]{2,1,0:T(2,128)(2,1)} %param.22) | data formatting | bytes 12288 | tf_op args[7]
  9.1 0.7 %pad.9.hist_value = bf16[8,1024]{1,0:T(8,128)(2,1)S(1)} pad(bf16[3,1024]{1,0:T(4,128)(2,1)} %param.23, bf16[]{:T(256)} %constant.27.clone.1), padding=5_0x0_0 | pad | bytes 22530 | tf_op jit(solution)/shard_map/jit(_pad)/pad | solution.py:335
  9.8 0.7 %copy.31 = bf16[4,2,512]{2,0,1:T(4,128)(2,1)S(1)} copy(bf16[4,2,512]{2,1,0:T(2,128)(2,1)} %param.20) | data formatting | bytes 16384 | tf_op args[5]
  10.5 1.3 %constant_dynamic-update-slice_fusion = bf16[264,2048]{1,0:T(8,128)(2,1)S(1)} fusion(bf16[264,2048]{1,0:T(8,128)(2,1)S(1)} %constant_dynamic-update-slice_fusion.1, bf16[256,2048]{1,0:T(8,128)(2,1)} %param.15), kind=kLoop, calls=%fused_computation.13 | loop fusion | bytes 2097152 | tf_op jit(solution)/shard_map/concatenate | solution.py:329
  11.8 3.7 %fusion.5.qk = bf16[2,264,512]{2,1,0:T(8,128)(2,1)S(1)} fusion(bf16[2048,2,512]{2,1,0:T(2,128)(2,1)} %param.16, bf16[264,2048]{1,0:T(8,128)(2,1)S(1)} %constant_dynamic-update-slice_fusion), kind=kOutput, calls=%fused_computation.5 | convolution fusion | flops 1107566592 | bytes 5816320 | tf_op jit(solution)/shard_map/td,dce->cte/dot_general | solution.py:330
  15.5 1.3 %convolution_convert_fusion.value = bf16[264,1024]{1,0:T(8,128)(2,1)S(1)} fusion(bf16[264,2048]{1,0:T(8,128)(2,1)S(1)} %constant_dynamic-update-slice_fusion, bf16[2048,1024]{1,0:T(8,128)(2,1)S(1)} %copy-done.8), kind=kOutput, calls=%fused_computation.3 | convolution fusion | flops 1107566592 | bytes 5816320 | tf_op jit(solution)/shard_map/dot_general | solution.py:331
  16.9 6.4 %shard_map.158 = (bf16[4,256,128]{2,1,0:T(8,128)(2,1)S(1)}, bf16[8,256,256]{2,1,0:T(8,128)(2,1)S(1)}, bf16[8,128,256]{2,1,0:T(8,128)(2,1)S(1)}, bf16[4,128,256]{...) custom-call(s32[4]{0:T(128)S(1)} %pad_add_fusion.1.place.refs_0_, ...), custom_call_target="tpu_custom_call" | custom-call | flops 10000000000 | bytes 4194304 | tf_op jit(solution)/shard_map/pallas_call | solution.py:338
  23.3 1.6 %collective-permute-start.1 = (bf16[4,128,256]{2,1,0:T(8,128)(2,1)S(1)}, bf16[4,128,256]{2,1,0:T(8,128)(2,1)S(1)}, u32[]{:S(2)}, u32[]{:S(2)}) collective-permute-start(bf16[4,128,256]{2,1,0:T(8,128)(2,1)S(1)} %get-tuple-element.21), channel_id=1, source_target_pairs={{0,4},{4,0},{8,12},{12,8},{16,20},{20,16},{24,28},{28,24},{1,5},{5... | collective-permute-start | bytes 786440 | tf_op jit(solution)/shard_map/ppermute | solution.py:307
  25.0 6.2 %collective-permute-done.1.received = bf16[4,128,256]{2,1,0:T(8,128)(2,1)S(1)} collective-permute-done((bf16[4,128,256]{2,1,0:T(8,128)(2,1)S(1)}, bf16[4,128,256]{2,1,0:T(8,128)(2,1)S(1)}, u32[]{:S(2)}, u32[]{:S(2)}) %collective-permute-start.1) | collective-permute-done | bytes 262176 | tf_op jit(solution)/shard_map/ppermute | solution.py:307
  31.2 0.8 %shard_map.159.refs_1_ = bf16[4,128,256]{2,1,0:T(8,128)(2,1)S(1)} custom-call(s32[4]{0:T(128)S(1)} %pad_add_fusion.1.place.refs_0_, bf16[8,128,256]{2,1,0:T(8,128)(2,1)S(1)} %get-tuple-element.20.maps, bf16[4,128,256]{2,1,0:T(8,128)(2,1)S(1)} %collective-permute-done.1.received), custom_call_target="tpu_custom_call" | custom-call | flops 100000000 | bytes 1048576 | tf_op jit(solution)/shard_map/pallas_call | solution.py:369
  31.9 1.6 %collective-permute-start.2 = (bf16[4,128,256]{2,1,0:T(8,128)(2,1)S(1)}, bf16[4,128,256]{2,1,0:T(8,128)(2,1)S(1)}, u32[]{:S(2)}, u32[]{:S(2)}) collective-permute-start(bf16[4,128,256]{2,1,0:T(8,128)(2,1)S(1)} %shard_map.159.refs_1_), channel_id=1, source_target_pairs={{0,8},{4,12},{8,0},{12,4},{16,24},{20,28},{24,16},{28,20},{1,9},{5... | collective-permute-start | bytes 786440 | tf_op jit(solution)/shard_map/ppermute | solution.py:307
  33.6 5.3 %collective-permute-done.2.refs_2_ = bf16[4,128,256]{2,1,0:T(8,128)(2,1)S(1)} collective-permute-done((bf16[4,128,256]{2,1,0:T(8,128)(2,1)S(1)}, bf16[4,128,256]{2,1,0:T(8,128)(2,1)S(1)}, u32[]{:S(2)}, u32[]{:S(2)}) %collective-permute-start.2) | collective-permute-done | bytes 262176 | tf_op jit(solution)/shard_map/ppermute | solution.py:307
  38.9 0.9 %shard_map.160 = (bf16[4,128,128]{2,1,0:T(8,128)(2,1)S(1)}, bf16[4,128,256]{2,1,0:T(8,128)(2,1)S(1)}) custom-call(s32[4]{0:T(128)S(1)} %pad_add_fusion.1.place.refs_0_, bf16[4,128,256]{2,1,0:T(8,128)(2,1)S(1)} %shard_map.159.refs_1_, bf16[4,128,256]{2,1,0:T(8,128)(2,1)S(1)} %collective-permute-done.2.refs_2_, f32[8,128,128]{2,1,0:T(8,128)S(1)} %copy-done.2), custom_call_target="tpu_custom_call" | custom-call | flops 100000000 | bytes 1048576 | tf_op jit(solution)/shard_map/pallas_call | solution.py:374
  39.8 2.6 %collective-permute-start.3 = (bf16[4,128,128]{2,1,0:T(8,128)(2,1)S(1)}, bf16[4,128,128]{2,1,0:T(8,128)(2,1)S(1)}, u32[]{:S(2)}, u32[]{:S(2)}) collective-permute-start(bf16[4,128,128]{2,1,0:T(8,128)(2,1)S(1)} %get-tuple-element.23), channel_id=1, source_target_pairs={{0,16},{4,20},{8,24},{12,28},{16,0},{20,4},{24,8},{28,12},{1,17},{... | collective-permute-start | bytes 393224 | tf_op jit(solution)/shard_map/ppermute | solution.py:307
  42.4 1.3 %convolution_convert_fusion.1.gate_z = bf16[256,1024]{1,0:T(8,128)(2,1)S(1)} fusion(bf16[256,2048]{1,0:T(8,128)(2,1)S(1)} %copy-done.7, bf16[2048,1024]{1,0:T(8,128)(2,1)S(1)} %copy-done.9), kind=kOutput, calls=%fused_computation.4 | convolution fusion | flops 1074003968 | bytes 5767168 | tf_op jit(solution)/shard_map/dot_general | solution.py:354
  43.8 3.3 %collective-permute-done.3.came = bf16[4,128,128]{2,1,0:T(8,128)(2,1)S(1)} collective-permute-done((bf16[4,128,128]{2,1,0:T(8,128)(2,1)S(1)}, bf16[4,128,128]{2,1,0:T(8,128)(2,1)S(1)}, u32[]{:S(2)}, u32[]{:S(2)}) %collective-permute-start.3) | collective-permute-done | bytes 131104 | tf_op jit(solution)/shard_map/ppermute | solution.py:307
  47.1 0.9 %shard_map.161 = (bf16[4,128,128]{2,1,0:T(8,128)(2,1)S(1)}, bf16[4,128,128]{2,1,0:T(8,128)(2,1)S(1)}) custom-call(s32[4]{0:T(128)S(1)} %pad_add_fusion.1.place.refs_0_, bf16[4,128,256]{2,1,0:T(8,128)(2,1)S(1)} %get-tuple-element.22.prefix, f32[8,128,128]{2,1,0:T(8,128)S(1)} %copy-done.2, bf16[4,128,128]{2,1,0:T(8,128)(2,1)S(1)} %collective-permute-done.3.came, ...), custom_call_target="tpu_custom_call" | custom-call | flops 100000000 | bytes 1048576 | tf_op jit(solution)/shard_map/pallas_call | solution.py:383
  48.0 1.6 %collective-permute-start.4 = (bf16[4,128,128]{2,1,0:T(8,128)(2,1)S(1)}, bf16[4,128,128]{2,1,0:T(8,128)(2,1)S(1)}, u32[]{:S(2)}, u32[]{:S(2)}) collective-permute-start(bf16[4,128,128]{2,1,0:T(8,128)(2,1)S(1)} %get-tuple-element.25), channel_id=1, source_target_pairs={{0,4},{4,0},{8,12},{12,8},{16,20},{20,16},{24,28},{28,24},{1,5},{5... | collective-permute-start | bytes 393224 | tf_op jit(solution)/shard_map/ppermute | solution.py:307
  49.6 1.2 %copy-done.6 = bf16[8,256,256]{2,1,0:T(8,128)(2,1)S(1)} copy-done((bf16[8,256,256]{2,1,0:T(8,128)(2,1)S(1)}, bf16[8,256,256]{2,1,0:T(8,128)(2,1)}, u32[]{:S(2)}) %copy-start.6) | copy-done | bytes 1048600
  50.8 2.3 %shard_map.162 = (bf16[8,256,128]{2,1,0:T(8,128)(2,1)S(1)}, f32[8,256,128]{2,1,0:T(8,128)S(1)}, f32[8,256,128]{2,1,0:T(8,128)S(1)}) custom-call(s32[4]{0:T(128)S(1)} %pad_add_fusion.1.place.refs_0_, bf16[2,264,512]{2,1,0:T(8,128)(2,1)S(1)} %fusion.5.qk, bf16[4,256,128]{2,1,0:T(8,128)(2,1)S(1)} %get-tuple-element.26.keys, bf16[8,256,256]{2,1,0:T(8,128)(2,1)S(1)} %copy-done.6, ...), custom_call_target="tpu_custom_call" | custom-call | flops 4000000000 | bytes 6291456 | tf_op jit(solution)/shard_map/pallas_call | solution.py:355
  53.2 2.4 %shard_map.163 = (bf16[2,256,512]{2,1,0:T(8,128)(2,1)S(1)}, bf16[2,256,512]{2,1,0:T(8,128)(2,1)S(1)}, bf16[8,128,128]{2,1,0:T(8,128)(2,1)S(1)}) custom-call(s32[2]{0:T(128)S(1)} %pad_add_fusion.place, bf16[4,128,128]{2,1,0:T(8,128)(2,1)S(1)} %get-tuple-element.24.mine, bf16[4,128,128]{2,1,0:T(8,128)(2,1)S(1)} %collective-permute-done.4.came, ...), custom_call_target="tpu_custom_call" | custom-call | flops 1000000000 | bytes 8388608 | tf_op jit(solution)/shard_map/pallas_call | solution.py:395
  55.6 1.9 %collective-permute-done.5.came = bf16[2,256,512]{2,1,0:T(8,128)(2,1)S(1)} collective-permute-done((bf16[2,256,512]{2,1,0:T(8,128)(2,1)S(1)}, bf16[2,256,512]{2,1,0:T(8,128)(2,1)S(1)}, u32[]{:S(2)}, u32[]{:S(2)}) %collective-permute-start.5) | collective-permute-done | bytes 524320 | tf_op jit(solution)/shard_map/ppermute | solution.py:307
  57.6 1.6 %collective-permute-start.6 = (bf16[1,256,512]{2,1,0:T(8,128)(2,1)S(1)}, bf16[1,256,512]{2,1,0:T(8,128)(2,1)S(1)}, u32[]{:S(2)}, u32[]{:S(2)}) collective-permute-start(bf16[1,256,512]{2,1,0:T(8,128)(2,1)S(1)} %get-tuple-element.36), channel_id=1, source_target_pairs={{0,2},{1,3},{2,0},{3,1},{4,6},{5,7},{6,4},{7,5},{8,10},{9,11},{10,... | collective-permute-start | bytes 786440 | tf_op jit(solution)/shard_map/ppermute | solution.py:307
  59.2 1.0 %shard_map.165 = f32[1,8,128,128]{3,2,1,0:T(8,128)} custom-call(bf16[8,128,256]{2,1,0:T(8,128)(2,1)S(1)} %get-tuple-element.20.maps, bf16[8,128,128]{2,1,0:T(8,128)(2,1)S(1)} %get-tuple-element.37.states), custom_call_target="tpu_custom_call" | custom-call | flops 100000000 | bytes 2097152 | tf_op jit(solution)/shard_map/pallas_call | solution.py:420
  60.2 5.8 %collective-permute-done.6 = bf16[1,256,512]{2,1,0:T(8,128)(2,1)S(1)} collective-permute-done((bf16[1,256,512]{2,1,0:T(8,128)(2,1)S(1)}, bf16[1,256,512]{2,1,0:T(8,128)(2,1)S(1)}, u32[]{:S(2)}, u32[]{:S(2)}) %collective-permute-start.6) | collective-permute-done | bytes 262176 | tf_op jit(solution)/shard_map/ppermute | solution.py:307
  66.1 0.8 %fusion.10 = bf16[256,512]{1,0:T(8,128)(2,1)} fusion(f32[1,256,512]{2,1,0:T(8,128)S(1)} %get-tuple-element.35, bf16[1,256,512]{2,1,0:T(8,128)(2,1)S(1)} %collective-permute-done.6), kind=kLoop, calls=%fused_computation.10 | loop fusion | flops 393216 | bytes 1048576 | tf_op jit(solution)/shard_map/convert_element_type | solution.py:423
  (28 shorter events, 0.5 us)
Async XLA Ops:
  0.6 3.8 %copy-start = (bf16[2048,2,8]{0,2,1:T(8,128)(2,1)S(1)}, bf16[2048,2,8]{0,2,1:T(8,128)(2,1)}, u32[]{:S(2)}) copy-start(bf16[2048,2,8]{0,2,1:T(8,128)(2,1)} %param.19) | copy-start | bytes 196612
  1.4 9.0 %collective-permute-start = (bf16[8,2048]{1,0:T(8,128)(2,1)S(1)}, bf16[8,2048]{1,0:T(8,128)(2,1)S(1)}, u32[]{:S(2)}, u32[]{:S(2)}) collective-permute-start(bf16[8,2048]{1,0:T(8,128)(2,1)S(1)} %slice.3), channel_id=1, source_target_pairs={{0,4},{4,8},{8,12},{12,16},{16,20},{20,24},{24,28},{28,0},{1,5},{5... | collective-permute-start | bytes 98312 | tf_op jit(solution)/shard_map/ppermute | solution.py:326
  11.8 3.7 %copy-start.8 = (bf16[2048,1024]{1,0:T(8,128)(2,1)S(1)}, bf16[2048,1024]{1,0:T(8,128)(2,1)}, u32[]{:S(2)}) copy-start(bf16[2048,1024]{1,0:T(8,128)(2,1)} %param.17) | copy-start | bytes 12582916
  15.5 1.3 %copy-start.3 = (bf16[4,1024]{1,0:T(4,128)(2,1)S(1)}, bf16[4,1024]{1,0:T(4,128)(2,1)}, u32[]{:S(2)}) copy-start(bf16[4,1024]{1,0:T(4,128)(2,1)} %conv_value.1) | copy-start | bytes 24580
  16.9 22.0 %copy-start.2 = (f32[8,128,128]{2,1,0:T(8,128)S(1)}, f32[8,128,128]{2,1,0:T(8,128)}, u32[]{:S(2)}) copy-start(f32[8,128,128]{2,1,0:T(8,128)} %state_in.1) | copy-start | bytes 1572868
  16.9 25.5 %copy-start.7 = (bf16[256,2048]{1,0:T(8,128)(2,1)S(1)}, bf16[256,2048]{1,0:T(8,128)(2,1)}, u32[]{:S(2)}) copy-start(bf16[256,2048]{1,0:T(8,128)(2,1)} %param.15) | copy-start | bytes 3145732
  16.9 25.5 %copy-start.9 = (bf16[2048,1024]{1,0:T(8,128)(2,1)S(1)}, bf16[2048,1024]{1,0:T(8,128)(2,1)}, u32[]{:S(2)}) copy-start(bf16[2048,1024]{1,0:T(8,128)(2,1)} %param.18) | copy-start | bytes 12582916
  23.3 19.1 %copy-start.5 = (bf16[8,256,256]{2,1,0:T(8,128)(2,1)}, bf16[8,256,256]{2,1,0:T(8,128)(2,1)S(1)}, u32[]{:S(2)}) copy-start(bf16[8,256,256]{2,1,0:T(8,128)(2,1)S(1)} %get-tuple-element.27.solved) | copy-start | bytes 3145732
  23.3 7.8 %collective-permute-start.1 = (bf16[4,128,256]{2,1,0:T(8,128)(2,1)S(1)}, bf16[4,128,256]{2,1,0:T(8,128)(2,1)S(1)}, u32[]{:S(2)}, u32[]{:S(2)}) collective-permute-start(bf16[4,128,256]{2,1,0:T(8,128)(2,1)S(1)} %get-tuple-element.21), channel_id=1, source_target_pairs={{0,4},{4,0},{8,12},{12,8},{16,20},{20,16},{24,28},{28,24},{1,5},{5... | collective-permute-start | bytes 786440 | tf_op jit(solution)/shard_map/ppermute | solution.py:307
  31.9 6.9 %collective-permute-start.2 = (bf16[4,128,256]{2,1,0:T(8,128)(2,1)S(1)}, bf16[4,128,256]{2,1,0:T(8,128)(2,1)S(1)}, u32[]{:S(2)}, u32[]{:S(2)}) collective-permute-start(bf16[4,128,256]{2,1,0:T(8,128)(2,1)S(1)} %shard_map.159.refs_1_), channel_id=1, source_target_pairs={{0,8},{4,12},{8,0},{12,4},{16,24},{20,28},{24,16},{28,20},{1,9},{5... | collective-permute-start | bytes 786440 | tf_op jit(solution)/shard_map/ppermute | solution.py:307
  39.7 9.9 %copy-start.4 = (f32[128]{0:T(128)S(1)}, f32[128]{0:T(128)}, u32[]{:S(2)}) copy-start(f32[128]{0:T(128)} %param.28) | copy-start | bytes 1540
  39.8 7.3 %collective-permute-start.3 = (bf16[4,128,128]{2,1,0:T(8,128)(2,1)S(1)}, bf16[4,128,128]{2,1,0:T(8,128)(2,1)S(1)}, u32[]{:S(2)}, u32[]{:S(2)}) collective-permute-start(bf16[4,128,128]{2,1,0:T(8,128)(2,1)S(1)} %get-tuple-element.23), channel_id=1, source_target_pairs={{0,16},{4,20},{8,24},{12,28},{16,0},{20,4},{24,8},{28,12},{1,17},{... | collective-permute-start | bytes 393224 | tf_op jit(solution)/shard_map/ppermute | solution.py:307
  48.0 5.2 %collective-permute-start.4 = (bf16[4,128,128]{2,1,0:T(8,128)(2,1)S(1)}, bf16[4,128,128]{2,1,0:T(8,128)(2,1)S(1)}, u32[]{:S(2)}, u32[]{:S(2)}) collective-permute-start(bf16[4,128,128]{2,1,0:T(8,128)(2,1)S(1)} %get-tuple-element.25), channel_id=1, source_target_pairs={{0,4},{4,0},{8,12},{12,8},{16,20},{20,16},{24,28},{28,24},{1,5},{5... | collective-permute-start | bytes 393224 | tf_op jit(solution)/shard_map/ppermute | solution.py:307
  49.6 1.2 %copy-start.6 = (bf16[8,256,256]{2,1,0:T(8,128)(2,1)S(1)}, bf16[8,256,256]{2,1,0:T(8,128)(2,1)}, u32[]{:S(2)}) copy-start(bf16[8,256,256]{2,1,0:T(8,128)(2,1)} %copy-done.5) | copy-start | bytes 3145732
  50.8 2.3 %copy-start.1 = (bf16[1024,2048]{1,0:T(8,128)(2,1)S(1)}, bf16[1024,2048]{1,0:T(8,128)(2,1)}, u32[]{:S(2)}) copy-start(bf16[1024,2048]{1,0:T(8,128)(2,1)} %w_out.1) | copy-start | bytes 12582916
  55.5 2.0 %collective-permute-start.5 = (bf16[2,256,512]{2,1,0:T(8,128)(2,1)S(1)}, bf16[2,256,512]{2,1,0:T(8,128)(2,1)S(1)}, u32[]{:S(2)}, u32[]{:S(2)}) collective-permute-start(bf16[2,256,512]{2,1,0:T(8,128)(2,1)S(1)} %get-tuple-element.34), channel_id=1, source_target_pairs={{0,1},{1,0},{2,3},{3,2},{4,5},{5,4},{6,7},{7,6},{8,9},{9,8},{10,11... | collective-permute-start | bytes 1572872 | tf_op jit(solution)/shard_map/ppermute | solution.py:307
  57.6 8.4 %collective-permute-start.6 = (bf16[1,256,512]{2,1,0:T(8,128)(2,1)S(1)}, bf16[1,256,512]{2,1,0:T(8,128)(2,1)S(1)}, u32[]{:S(2)}, u32[]{:S(2)}) collective-permute-start(bf16[1,256,512]{2,1,0:T(8,128)(2,1)S(1)} %get-tuple-element.36), channel_id=1, source_target_pairs={{0,2},{1,3},{2,0},{3,1},{4,6},{5,7},{6,4},{7,5},{8,10},{9,11},{10,... | collective-permute-start | bytes 786440 | tf_op jit(solution)/shard_map/ppermute | solution.py:307
where the time goes:
time: 67.3 us; the launch traced here: 66.8 us
  waiting for transfers between devices  22.5 us (33%)
  Pallas kernels  14.8 us (22%)
  starting transfers between devices  12.1 us (18%)
  matrix products  7.86 us (12%)
  local copies, waits for them, and re-layouts  7.73 us (11%)
  other arithmetic  1 us (1%)
  between operations  0.85 us (1%)
    ppermute x6, waiting for transfers between devices, swapped(): return lax.ppermute(value, axis, [(i, i ^ step) for i in range(count)])  22.5 us
    ppermute x6, starting transfers between devices, swapped(): return lax.ppermute(value, axis, [(i, i ^ step) for i in range(count)])  9.16 us
    pallas_call x1, Pallas kernels, local(): call(prepare_kernel, (shape((half, rows, KD), BF16), shape((heads, rows,...  6.43 us
    dot_general x1, matrix products, local(): jnp.einsum('td,dce->cte', joined, w_qk, preferred_element_type=F32)  3.66 us
    ppermute x1, starting transfers between devices, local(): lax.ppermute(hidden_in[rows - HALO:], 'seq', [(i, (i + 1) % n_seq) for i...  2.94 us
    unnamed x23, local copies, waits for them, and re-layouts  2.69 us
    pallas_call x1, Pallas kernels, local(): call(output_kernel, (shape((blocks, rows, out_width), BF16), shape((block...  2.36 us
    pallas_call x1, Pallas kernels, local(): call(query_kernel, (shape((heads, rows, KD), BF16), shape((heads, rows, D...  2.32 us
  transfers between devices with their start and end apart: 7, of which 5 were waited for; matrix products, arithmetic and copies ran while one was open for 11% of the time, Pallas kernels for 5%

commit v1 on v0

--- a/solution.py
+++ b/solution.py
@@ -44,12 +44,11 @@
     return values * lax.rsqrt(jnp.sum(values * values, axis=-1, keepdims=True) + 1e-06)
 
 
-def conv_rows(block, history, weight, first):
-    rows = block.shape[0] - HALO
+def conv_rows(block, halo, history, weight, first):
+    rows = block.shape[0]
     taps = weight.shape[0]
     start = HALO - (taps - 1)
-    halo = jnp.where(first, history, block[:HALO])
-    joined = jnp.concatenate([halo, block[HALO:]], 0)
+    joined = jnp.concatenate([jnp.where(first, history, halo), block], 0)
     total = weight[0:1] * joined[start : start + rows]
     for tap in range(1, taps):
         total = total + weight[tap : tap + 1] * joined[start + tap : start + tap + rows]
@@ -63,7 +62,7 @@
         in_specs=in_specs,
         out_specs=jax.tree.map(lambda _: VMEM, out_shape),
         scratch_shapes=list(scratch),
-        compiler_params=pltpu.CompilerParams(vmem_limit_bytes=40 << 20),
+        compiler_params=pltpu.CompilerParams(vmem_limit_bytes=12 << 20),
         cost_estimate=pl.CostEstimate(flops=flops, bytes_accessed=moved, transcendentals=0),
     )
 
@@ -72,19 +71,64 @@
     return jax.ShapeDtypeStruct(dims, dtype)
 
 
+def lane_block(index, width):
+    return pl.ds(pl.multiple_of(index * width, width), width)
+
+
+def picked(flag, values):
+    count = values.shape[0] // 2
+    return jnp.where(flag == 1, values[count:], values[:count])
+
+
+def scalar_column(ref, start, count):
+    index = lax.broadcasted_iota(jnp.int32, (count, 1), 0)
+    column = jnp.zeros((count, 1), F32)
+    for i in range(count):
+        column = jnp.where(index == i, ref[start + i], column)
+    return column
+
+
+def load_small(hist_qk, conv_qk, part, hist_s, conv_s):
+    taps = conv_qk.shape[0]
+    hist_s[HALO - taps + 1 :, :] = hist_qk[...].astype(F32)[:, part, :]
+    conv_s[...] = conv_qk[...].astype(F32)[:, part, :]
+
+
+def key_block(qk, halo, hist_s, conv_s, part, index, first):
+    key_cols = qk.shape[2]
+    lanes = lane_block(index, KD)
+    halo_lanes = lane_block(part * (key_cols // KD) + index, KD)
+    return unit_rows(
+        conv_rows(
+            qk[part, :, lanes].astype(F32),
+            halo[:, halo_lanes].astype(F32),
+            hist_s[:, lanes],
+            conv_s[:, lanes],
+            first,
+        )
+    )
+
+
 def prepare_kernel(
-    place, qk, value, gates, hist_qk, hist_value, conv_qk, conv_value, params,
-    keys_out, solved_out, maps_out, send_out, rows_out, cols_out,
+    own, place, a_log, dt_bias, beta_bias, qk, value, gates, halo, hist_qk, hist_value,
+    conv_qk, conv_value, keys_out, solved_out, maps_out, rows_out, cols_out,
+    hist_s, conv_s, hist_v,
 ):
-    heads = gates.shape[1]
+    heads = gates.shape[1] // 2
     rows = gates.shape[2]
     key_heads = heads // 2
+    key_cols = qk.shape[2]
+    taps = conv_value.shape[0]
     first = place[0] == 0
-    bit = place[1]
-    strength = jax.nn.sigmoid(gates[0].astype(F32) + params[:, 2:3])
-    decay_in = gates[1].astype(F32) + params[:, 1:2]
+    side = place[1] if own else 1 - place[1]
+    load_small(hist_qk, conv_qk, 1, hist_s, conv_s)
+    hist_v[HALO - taps + 1 :, :] = hist_value[...].astype(F32)
+    strength = jax.nn.sigmoid(
+        picked(side, gates[0].astype(F32)) + scalar_column(beta_bias, side * heads, heads)
+    )
+    decay_in = picked(side, gates[1].astype(F32)) + scalar_column(dt_bias, side * heads, heads)
     soft = jnp.maximum(decay_in, 0.0) + jnp.log1p(jnp.exp(-jnp.abs(decay_in)))
-    log_decay = -jnp.exp(params[:, 0:1]) * soft
+    log_decay = -jnp.exp(scalar_column(a_log, side * heads, heads)) * soft
     line = lax.broadcasted_iota(jnp.int32, (rows, rows), 0)
     across = lax.broadcasted_iota(jnp.int32, (rows, rows), 1)
     upper = jnp.where(line <= across, 1.0, 0.0).astype(BF16)
@@ -107,24 +151,18 @@
     rhs = []
     ends = []
     for key_head in range(key_heads):
-        lanes = slice(key_head * KD, (key_head + 1) * KD)
-        key = unit_rows(
-            conv_rows(
-                qk[1, :, lanes].astype(F32),
-                hist_qk[1, :, lanes].astype(F32),
-                conv_qk[1, :, lanes].astype(F32),
-                first,
-            )
-        )
+        key = key_block(qk, halo, hist_s, conv_s, 1, side * key_heads + key_head, first)
         key_low = key.astype(BF16)
         keys_out[key_head] = key_low
         dots = dot_nt(key_low, key_low)
         key_t = key.T
         for head in (2 * key_head, 2 * key_head + 1):
-            lanes = slice(head * DV, (head + 1) * DV)
+            index = side * heads + head
+            lanes = lane_block(index, DV)
             val = conv_rows(
                 value[:, lanes].astype(F32),
-                hist_value[:, lanes].astype(F32),
+                halo[:, lane_block(2 * key_cols // DV + index, DV)].astype(F32),
+                hist_v[:, lanes],
                 conv_value[:, lanes].astype(F32),
                 first,
             )
@@ -166,7 +204,6 @@
             for j in range(i):
                 need = need - fine_dot(lowers[head][i, j], solved[head][j])
             solved[head].append(dot(tri[head, i], need.astype(BF16)))
-    half = heads // 2
     for head in range(heads):
         both = jnp.concatenate(solved[head], 0).astype(BF16)
         solved_out[head] = both
@@ -174,28 +211,23 @@
         fade_end = fade[head : head + 1, rows - 1 : rows]
         own = jnp.concatenate([eye * fade_end - ended[:, :KD], ended[:, KD:]], 1).astype(BF16)
         maps_out[head] = own
-    send_out[...] = maps_out[pl.ds((1 - bit) * half, half)]
 
 
 def query_kernel(
-    place, qk, keys, solved, cumul, cols, hist_qk, conv_qk, gate_z, gain,
-    reads_out, local_out, gate_out,
+    own, place, qk, halo, hist_qk, conv_qk, keys, solved, cumul, cols, gate_z, gain,
+    reads_out, local_out, gate_out, hist_s, conv_s,
 ):
     heads, rows = cumul.shape
+    key_heads = heads // 2
     first = place[0] == 0
+    side = place[1] if own else 1 - place[1]
+    load_small(hist_qk, conv_qk, 0, hist_s, conv_s)
     line = lax.broadcasted_iota(jnp.int32, (rows, rows), 0)
     across = lax.broadcasted_iota(jnp.int32, (rows, rows), 1)
     within = line >= across
-    for key_head in range(heads // 2):
-        lanes = slice(key_head * KD, (key_head + 1) * KD)
-        query = unit_rows(
-            conv_rows(
-                qk[0, :, lanes].astype(F32),
-                hist_qk[0, :, lanes].astype(F32),
-                conv_qk[0, :, lanes].astype(F32),
-                first,
-            )
-        ) * (KD**-0.5)
+    for key_head in range(key_heads):
+        query = key_block(qk, halo, hist_s, conv_s, 0, side * key_heads + key_head, first)
+        query = query * (KD**-0.5)
         dots = dot_nt(query.astype(BF16), keys[key_head])
         for head in (2 * key_head, 2 * key_head + 1):
             col = cols[:, head : head + 1]
@@ -205,7 +237,7 @@
             part = dot(attend, solved[head])
             reads_out[head] = (fade * query - part[:, :KD]).astype(BF16)
             local_out[head] = part[:, KD:]
-            lanes = slice(head * DV, (head + 1) * DV)
+            lanes = lane_block(side * heads + head, DV)
             gate_out[head] = silu(gate_z[:, lanes].astype(F32)) * gain[...]
 
 
@@ -220,9 +252,8 @@
 
 def pair_kernel(place, maps, received, total_out):
     bit = place[1]
-    half = received.shape[0]
-    for j in range(half):
-        mine, other = maps[bit * half + j], received[j]
+    for j in range(received.shape[0]):
+        mine, other = maps[j], received[j]
         low, high = jnp.where(bit == 1, other, mine), jnp.where(bit == 1, mine, other)
         total_out[j] = join(high, low).astype(BF16)
 
@@ -257,49 +288,55 @@
     for j in range(half):
         start = jnp.where(place[top + 1] == 1, came[j], state_in[bit * half + j].astype(BF16))
         entering = act(prefix[j], start).astype(BF16)
-        low = jnp.where(bit == 1, received[j], maps[bit * half + j])
+        low = jnp.where(bit == 1, received[j], maps[j])
         passed = act(low, entering).astype(BF16)
         mine_out[j] = jnp.where(bit == 1, passed, entering)
         send_out[j] = jnp.where(bit == 1, entering, passed)
 
 
-def output_kernel(
-    place, mine, came, reads, local_reads, gate, w_out, send_out, keep_out, states_out, normed,
+def normed_rows(local_part, reads, gate, state):
+    out = local_part + dot(reads, state)
+    scale = lax.rsqrt(jnp.mean(out * out, axis=-1, keepdims=True) + 1e-06)
+    return (out * scale * gate).astype(BF16)
+
+
+def project(side, mine_rows, other_rows, w_out, away, send_out, keep_out):
+    core, bit, lift = side[0], side[1], side[2]
+    depth = w_out.shape[0] // 2
+    width = send_out.shape[2]
+    for j in range(send_out.shape[0]):
+        block = 2 * j + (1 - lift if away else lift)
+        for member, ref in ((1 - core, send_out), (core, keep_out)):
+            lanes = lane_block(2 * block + member, width)
+            own = w_out[pl.ds(pl.multiple_of(bit * depth, depth), depth), lanes]
+            other = w_out[pl.ds(pl.multiple_of((1 - bit) * depth, depth), depth), lanes]
+            ref[j] = (dot(mine_rows[...], own) + dot(other_rows[...], other)).astype(BF16)
+
+
+def normed_kernel(states, reads, local_reads, gate, normed_out):
+    for j in range(states.shape[0]):
+        normed_out[:, j * DV : (j + 1) * DV] = normed_rows(
+            local_reads[j], reads[j], gate[j], states[j]
+        )
+
+
+def away_kernel(
+    side, states, reads, local_reads, gate, mine_rows, w_out, other_rows, send_out, keep_out
 ):
-    bit = place[1]
-    core = place[0]
-    half = mine.shape[0]
-    heads = 2 * half
-    blocks = send_out.shape[0]
-    width = send_out.shape[2]
-    for j in range(heads):
-        if j < half:
-            head, state = bit * half + j, mine[j]
-        else:
-            head, state = (1 - bit) * half + (j - half), came[j - half]
-        states_out[head] = state
-        out = local_reads[head] + dot(reads[head], state)
-        scale = lax.rsqrt(jnp.mean(out * out, axis=-1, keepdims=True) + 1e-06)
-        lanes = pl.ds(pl.multiple_of(head * DV, DV), DV)
-        normed[:, lanes] = (out * scale * gate[head]).astype(BF16)
-    for j in range(blocks):
-        for side, ref in ((1 - core, send_out), (core, keep_out)):
-            lanes = pl.ds(pl.multiple_of((2 * j + side) * width, width), width)
-            ref[j] = dot(normed[...], w_out[:, lanes]).astype(BF16)
-
-
-def merge_kernel(place, keep, came, send_out, keep_out):
-    bit = place[0]
-    blocks = send_out.shape[0]
-    for j in range(blocks):
-        away, home = 2 * j + 1 - bit, 2 * j + bit
-        send_out[j] = (keep[away].astype(F32) + came[away].astype(F32)).astype(BF16)
-        keep_out[j] = keep[home].astype(F32) + came[home].astype(F32)
-
-
-def checkpoint_kernel(maps, states, out):
-    for head in range(maps.shape[0]):
-        out[0, head] = act(maps[head], states[head])
+    normed_kernel(states, reads, local_reads, gate, other_rows)
+    project(side, mine_rows, other_rows, w_out, True, send_out, keep_out)
+
+
+def home_kernel(
+    side, mine_rows, other_rows, w_out, maps, states, away_maps, away_states,
+    send_out, keep_out, checkpoint,
+):
+    project(side, mine_rows, other_rows, w_out, False, send_out, keep_out)
+    bit = side[1]
+    half = maps.shape[0]
+    for j in range(half):
+        checkpoint[0, bit * half + j] = act(maps[j], states[j])
+        checkpoint[0, (1 - bit) * half + j] = act(away_maps[j], away_states[j])
 
 
 def swapped(value, axis, step):
@@ -323,47 +360,59 @@
     col = lax.axis_index("head")
     place = jnp.stack([seq] + [(seq >> level) & 1 for level in range(levels)]).astype(jnp.int32)
 
-    halo = lax.ppermute(
-        hidden_in[rows - HALO :], "seq", [(i, (i + 1) % n_seq) for i in range(n_seq)]
-    )
-    joined = jnp.concatenate([halo, hidden_in], 0)
-    qk = jnp.einsum("td,dce->cte", joined, w_qk, preferred_element_type=F32).astype(BF16)
-    value = jnp.dot(joined, w_value, preferred_element_type=F32).astype(BF16)
+    qk = jnp.einsum("td,dce->cte", hidden_in, w_qk, preferred_element_type=F32).astype(BF16)
+    value = jnp.dot(hidden_in, w_value, preferred_element_type=F32).astype(BF16)
+    tail = rows - HALO
+    ends = jnp.concatenate([qk[0, tail:], qk[1, tail:], value[tail:]], 1)
+    halo = lax.ppermute(ends, "seq", [(i, (i + 1) % n_seq) for i in range(n_seq)])
     gates = jnp.einsum("td,dch->cht", hidden_in, w_ba, preferred_element_type=F32).astype(BF16)
-    params = jnp.stack([a_log, dt_bias, beta_bias], 1)
-    hist_qk = jnp.pad(jnp.moveaxis(hist_qk, 1, 0), ((0, 0), (HALO - taps + 1, 0), (0, 0)))
-    hist_value = jnp.pad(hist_value, ((HALO - taps + 1, 0), (0, 0)))
-    conv_qk = jnp.moveaxis(conv_qk, 1, 0)
-
-    keys, solved, maps, send, cumul, cols = call(
-        prepare_kernel,
-        (
-            shape((half, rows, KD), BF16),
-            shape((heads, rows, KD + DV), BF16),
-            shape((heads, KD, KD + DV), BF16),
-            shape((half, KD, KD + DV), BF16),
-            shape((heads, rows), F32),
-            shape((rows, 128), F32),
-        ),
-        [SMEM] + [VMEM] * 8,
-        10**10,
-        4 << 20,
-    )(place, qk, value, gates, hist_qk, hist_value, conv_qk, conv_value, params)
-
-    received = swapped(send, "seq", 1)
-    gate_z = jnp.dot(hidden_in, w_outgate, preferred_element_type=F32).astype(BF16)
-    reads, local_reads, gate = call(
-        query_kernel,
-        (
-            shape((heads, rows, KD), BF16),
-            shape((heads, rows, DV), F32),
-            shape((heads, rows, DV), F32),
-        ),
-        [SMEM] + [VMEM] * 9,
-        4 * 10**9,
-        6 << 20,
-    )(place, qk, keys, solved, cumul, cols, hist_qk, conv_qk, gate_z, norm_gain.reshape(1, DV))
-
+
+    def prepare(own):
+        return call(
+            functools.partial(prepare_kernel, own),
+            (
+                shape((half // 2, rows, KD), BF16),
+                shape((half, rows, KD + DV), BF16),
+                shape((half, KD, KD + DV), BF16),
+                shape((half, rows), F32),
+                shape((rows, 128), F32),
+            ),
+            [SMEM] * 4 + [VMEM] * 8,
+            4 * 10**9,
+            4 << 20,
+            [
+                pltpu.VMEM((HALO, key_cols), F32),
+                pltpu.VMEM((taps, key_cols), F32),
+                pltpu.VMEM((HALO, heads * DV), F32),
+            ],
+        )(
+            place, a_log, dt_bias, beta_bias, qk, value, gates, halo, hist_qk, hist_value,
+            conv_qk, conv_value,
+        )
+
+    def query(own, prepared):
+        keys, solved, _, cumul, cols = prepared
+        return call(
+            functools.partial(query_kernel, own),
+            (
+                shape((half, rows, KD), BF16),
+                shape((half, rows, DV), F32),
+                shape((half, rows, DV), F32),
+            ),
+            [SMEM] + [VMEM] * 10,
+            2 * 10**9,
+            4 << 20,
+            [pltpu.VMEM((HALO, key_cols), F32), pltpu.VMEM((taps, key_cols), F32)],
+        )(
+            place, qk, halo, hist_qk, conv_qk, keys, solved, cumul, cols, gate_z,
+            norm_gain.reshape(1, DV),
+        )
+
+    away = prepare(False)
+    received = swapped(away[2], "seq", 1)
+    own = prepare(True)
+    received, own = lax.optimization_barrier((received, own))
+    maps = own[2]
     map_shape = shape((half, KD, KD + DV), BF16)
     state_shape = shape((half, KD, DV), BF16)
     total = call(pair_kernel, map_shape, [SMEM, VMEM, VMEM], 10**8, 1 << 20)(place, maps, received)
@@ -380,6 +429,11 @@
         )(place, total, other, *prefix, state_in)
         prefix = (prefix,)
     came = swapped(total, "seq", 1 << (levels - 1))
+    later, _ = lax.optimization_barrier((hidden_in, total))
+    gate_z = jnp.dot(later, w_outgate, preferred_element_type=F32).astype(BF16)
+    own_reads = query(True, own)
+    away_reads = query(False, away)
+    came, own_reads, away_reads = lax.optimization_barrier((came, own_reads, away_reads))
     mine, send_state = call(
         functools.partial(enter_kernel, levels - 1),
         (state_shape, state_shape),
@@ -390,38 +444,41 @@
     other_state = swapped(send_state, "seq", 1)
 
     out_width = w_out.shape[1] // n_head
-    blocks = n_head // 2
-    side = jnp.stack([col & 1, place[1]]).astype(jnp.int32)
-    send_out, keep, states = call(
-        output_kernel,
-        (
-            shape((blocks, rows, out_width), BF16),
-            shape((blocks, rows, out_width), BF16),
-            shape((heads, KD, DV), BF16),
-        ),
+    blocks = n_head // 4
+    side = jnp.stack([col & 1, place[1], (col >> 1) & 1]).astype(jnp.int32)
+    part_shape = shape((blocks, rows, out_width), BF16)
+    rows_shape = shape((rows, half * DV), BF16)
+    own_rows = call(normed_kernel, rows_shape, [VMEM] * 4, 10**9, 4 << 20)(mine, *own_reads)
+    other_rows, send_out, keep = call(
+        away_kernel,
+        (rows_shape, part_shape, part_shape),
         [SMEM] + [VMEM] * 6,
         10**9,
-        8 << 20,
-        [pltpu.VMEM((rows, heads * DV), BF16)],
-    )(side, mine, other_state, reads, local_reads, gate, w_out)
+        4 << 20,
+    )(side, other_state, *away_reads, own_rows, w_out)
     came_out = swapped(send_out, "head", 1)
-    step = 2
+    total_out = (keep.astype(F32) + came_out.astype(F32)).astype(BF16)
+    total_out, other_rows = lax.optimization_barrier((total_out, other_rows))
+    came_far = swapped(total_out, "head", 2)
+    send_out, keep, checkpoint = call(
+        home_kernel,
+        (part_shape, part_shape, shape((1, heads, KD, DV), F32)),
+        [SMEM] + [VMEM] * 7,
+        10**9,
+        4 << 20,
+    )(side, own_rows, other_rows, w_out, maps, mine, away[2], other_state)
+    came_out = swapped(send_out, "head", 1)
+    mixed = keep.astype(F32) + came_out.astype(F32) + came_far.astype(F32)
+    step = 4
     while step < n_head:
+        here = (col // step) & 1
         blocks //= 2
-        send_out, keep = call(
-            merge_kernel,
-            (shape((blocks, rows, out_width), BF16), shape((blocks, rows, out_width), F32)),
-            [SMEM, VMEM, VMEM],
-            10**6,
-            2 << 20,
-        )(((col // step) & 1).astype(jnp.int32).reshape(1), keep, came_out)
-        came_out = swapped(send_out, "head", step)
+        pairs = mixed.reshape(blocks, 2, rows, out_width)
+        send_out = lax.dynamic_index_in_dim(pairs, 1 - here, 1, False).astype(BF16)
+        mixed = lax.dynamic_index_in_dim(pairs, here, 1, False)
+        mixed = mixed + swapped(send_out, "head", step).astype(F32)
         step *= 2
-    checkpoint = call(
-        checkpoint_kernel, shape((1, heads, KD, DV), F32), [VMEM, VMEM], 10**8, 2 << 20
-    )(maps, states)
-    mixed = (keep[0].astype(F32) + came_out[0].astype(F32)).astype(BF16)
-    return (mixed, checkpoint)
+    return (mixed[0].astype(BF16), checkpoint)
 
 
 def solution(mesh):

time: 67.3 us -> 63.4 us (0.942)
  starting transfers between devices: 12.1 us -> 7.62 us
  Pallas kernels: 14.8 us -> 18.8 us
  local copies, waits for them, and re-layouts: 7.73 us -> 5.33 us
  waiting for transfers between devices: 22.5 us -> 20.5 us
  matrix products: 7.86 us -> 8.86 us
    ppermute x6 -> x7, waiting for transfers between devices: 22.5 us -> 16 us  [swapped(): return lax.ppermute(value, axis, [(i, i ^ step) for i in range(count)])]
    ppermute x6 -> x7, starting transfers between devices: 9.16 us -> 4.62 us  [swapped(): return lax.ppermute(value, axis, [(i, i ^ step) for i in range(count)])]
    ppermute x1, waiting for transfers between devices: 0.01 us -> 4.47 us  [local(): lax.ppermute(ends, 'seq', [(i, (i + 1) % n_seq) for i in range(n_seq)])]
    pallas_call x5 -> x7, Pallas kernels: 12.2 us -> 16.3 us  [the longest x2 9.2 us: prepare(): call(functools.partial(prepare_kernel, own), (shape((half // 2, rows, KD)...]
    unnamed x23 -> x54, local copies, waits for them, and re-layouts: 2.69 us -> 5.33 us
    dot_general x3, matrix products: 6.26 us -> 8.48 us  [the longest x1 3.77 us: local(): jnp.einsum('td,dce->cte', hidden_in, w_qk, preferred_element_type=F32)]
    another operation x3 -> x0, local copies, waits for them, and re-layouts: 2.2 us -> none  [local(): params = jnp.stack([a_log, dt_bias, beta_bias], 1)]
    concatenate x1 -> x0, local copies, waits for them, and re-layouts: 1.33 us -> none  [local(): joined = jnp.concatenate([halo, hidden_in], 0)]
  transfers between devices with their start and end apart: 7 -> 8, of which waited for: 5 -> 5; matrix products, arithmetic and copies ran while one was open for 11% -> 6% of each run, Pallas kernels for 5% -> 16%
where the time goes in v1:
time: 63.4 us; the launch traced here: 63.2 us
  waiting for transfers between devices  20.5 us (32%)
  Pallas kernels  18.8 us (30%)
  matrix products  8.86 us (14%)
  starting transfers between devices  7.62 us (12%)
  local copies, waits for them, and re-layouts  5.33 us (8%)
  between operations  1.06 us (2%)
  other arithmetic  1.04 us (2%)
    ppermute x7, waiting for transfers between devices, swapped(): return lax.ppermute(value, axis, [(i, i ^ step) for i in range(count)])  16 us
    pallas_call x2, Pallas kernels, prepare(): call(functools.partial(prepare_kernel, own), (shape((half // 2, rows, KD)...  9.2 us
    unnamed x54, local copies, waits for them, and re-layouts  5.33 us
    ppermute x7, starting transfers between devices, swapped(): return lax.ppermute(value, axis, [(i, i ^ step) for i in range(count)])  4.62 us
    ppermute x1, waiting for transfers between devices, local(): lax.ppermute(ends, 'seq', [(i, (i + 1) % n_seq) for i in range(n_seq)])  4.47 us
    dot_general x1, matrix products, local(): jnp.einsum('td,dce->cte', hidden_in, w_qk, preferred_element_type=F32)  3.77 us
    dot_general x1, matrix products, local(): gate_z = jnp.dot(later, w_outgate, preferred_element_type=F32).astype(BF16)  3.43 us
    pallas_call x2, Pallas kernels, query(): call(functools.partial(query_kernel, own), (shape((half, rows, KD), BF16)...  3.06 us
  transfers between devices with their start and end apart: 8, of which 5 were waited for; matrix products, arithmetic and copies ran while one was open for 6% of the time, Pallas kernels for 16%

profile of v1, /device:TPU:0, one launch (start us, length us, event | category | flops | bytes accessed | tf_op | source)
XLA Modules:
  0.0 63.2 jit_solution(11894077533316341839)
XLA Ops:
  0.7 1.2 %copy-done = bf16[256,2048]{1,0:T(8,128)(2,1)S(1)} copy-done((bf16[256,2048]{1,0:T(8,128)(2,1)S(1)}, bf16[256,2048]{1,0:T(8,128)(2,1)}, u32[]{:S(2)}) %copy-start) | copy-done | bytes 1048600
  1.9 3.8 %fusion.5.qk = bf16[2,256,512]{2,1,0:T(8,128)(2,1)S(1)} fusion(bf16[2048,2,512]{2,1,0:T(2,128)(2,1)} %param.16, bf16[256,2048]{1,0:T(8,128)(2,1)S(1)} %copy-done), kind=kOutput, calls=%fused_computation.5 | convolution fusion | flops 1074003968 | bytes 5767168 | tf_op jit(solution)/shard_map/td,dce->cte/dot_general | solution.py:363
  5.7 1.3 %convolution_convert_fusion.1.value = bf16[256,1024]{1,0:T(8,128)(2,1)S(1)} fusion(bf16[256,2048]{1,0:T(8,128)(2,1)S(1)} %copy-done, bf16[2048,1024]{1,0:T(8,128)(2,1)S(1)} %copy-done.26), kind=kOutput, calls=%fused_computation.4 | convolution fusion | flops 1074003968 | bytes 5767168 | tf_op jit(solution)/shard_map/dot_general | solution.py:364
  7.1 3.0 %collective-permute-start = (bf16[8,2048]{1,0:T(8,128)(2,1)S(1)}, bf16[8,2048]{1,0:T(8,128)(2,1)S(1)}, u32[]{:S(2)}, u32[]{:S(2)}) collective-permute-start(bf16[8,2048]{1,0:T(8,128)(2,1)S(1)} %pad_maximum_fusion), channel_id=1, source_target_pairs={{0,4},{4,8},{8,12},{12,16},{16,20},{20,24},{24,28},{28,0},{1,5},{5... | collective-permute-start | bytes 98312 | tf_op jit(solution)/shard_map/ppermute | solution.py:367
  10.1 0.4 convolution_convert_fusion.2.gates
  10.5 0.1 pad_add_fusion.1.place.refs_0_
  10.5 4.5 %collective-permute-done.halo = bf16[8,2048]{1,0:T(8,128)(2,1)S(1)} collective-permute-done((bf16[8,2048]{1,0:T(8,128)(2,1)S(1)}, bf16[8,2048]{1,0:T(8,128)(2,1)S(1)}, u32[]{:S(2)}, u32[]{:S(2)}) %collective-permute-start) | collective-permute-done | bytes 32800 | tf_op jit(solution)/shard_map/ppermute | solution.py:367
  15.1 4.6 %shard_map.158 = (bf16[2,256,128]{2,1,0:T(8,128)(2,1)S(1)}, bf16[4,256,256]{2,1,0:T(8,128)(2,1)S(1)}, bf16[4,128,256]{2,1,0:T(8,128)(2,1)S(1)}, f32[4,256]{1,0:T(4,128)S(1)}, f32[256,128]{1,0:T(8,128)S(1)}) custom-call(s32[4]{0:T(128)S(1)} %pad_add_fusion.1.place.refs_0_, f32[8]{0:T(128)S(1)} %copy-done.9, f32[8]{0:T(128)S(1)} %copy-done.10, ...), custom_call_target="tpu_custom_call" | custom-call | flops 4000000000 | bytes 4194304 | tf_op jit(solution)/shard_map/pallas_call | solution.py:371
  19.7 0.8 %copy-done.13 = bf16[4,256,256]{2,1,0:T(8,128)(2,1)} copy-done((bf16[4,256,256]{2,1,0:T(8,128)(2,1)}, bf16[4,256,256]{2,1,0:T(8,128)(2,1)S(1)}, u32[]{:S(2)}) %copy-start.13) | copy-done | bytes 524312
  20.5 1.1 %copy-done.4 = bf16[256,1024]{1,0:T(8,128)(2,1)S(1)} copy-done((bf16[256,1024]{1,0:T(8,128)(2,1)S(1)}, bf16[256,1024]{1,0:T(8,128)(2,1)}, u32[]{:S(2)}) %copy-start.4) | copy-done | bytes 524312
  21.6 4.6 %shard_map.159 = (bf16[2,256,128]{2,1,0:T(8,128)(2,1)S(1)}, bf16[4,256,256]{2,1,0:T(8,128)(2,1)S(1)}, bf16[4,128,256]{2,1,0:T(8,128)(2,1)S(1)}, f32[4,256]{1,0:T(4,128)S(1)}, f32[256,128]{1,0:T(8,128)S(1)}) custom-call(s32[4]{0:T(128)S(1)} %pad_add_fusion.1.place.refs_0_, f32[8]{0:T(128)S(1)} %copy-done.9, f32[8]{0:T(128)S(1)} %copy-done.10, ...), custom_call_target="tpu_custom_call" | custom-call | flops 4000000000 | bytes 4194304 | tf_op jit(solution)/shard_map/pallas_call | solution.py:371
  26.3 0.8 %copy-done.15 = bf16[4,256,256]{2,1,0:T(8,128)(2,1)} copy-done((bf16[4,256,256]{2,1,0:T(8,128)(2,1)}, bf16[4,256,256]{2,1,0:T(8,128)(2,1)S(1)}, u32[]{:S(2)}) %copy-start.15) | copy-done | bytes 524312
  27.1 0.7 %copy-done.21 = bf16[2,256,128]{2,1,0:T(8,128)(2,1)} copy-done((bf16[2,256,128]{2,1,0:T(8,128)(2,1)}, bf16[2,256,128]{2,1,0:T(8,128)(2,1)S(1)}, u32[]{:S(2)}) %copy-start.21) | copy-done | bytes 131096
  27.7 0.6 %copy-done.23 = f32[256,128]{1,0:T(8,128)} copy-done((f32[256,128]{1,0:T(8,128)}, f32[256,128]{1,0:T(8,128)S(1)}, u32[]{:S(2)}) %copy-start.23) | copy-done | bytes 131096
  28.4 0.8 %shard_map.160.refs_1_ = bf16[4,128,256]{2,1,0:T(8,128)(2,1)S(1)} custom-call(s32[4]{0:T(128)S(1)} %pad_add_fusion.1.place.refs_0_, bf16[4,128,256]{2,1,0:T(8,128)(2,1)S(1)} %get-tuple-element.50.maps, bf16[4,128,256]{2,1,0:T(8,128)(2,1)S(1)} %collective-permute-done.1.received), custom_call_target="tpu_custom_call" | custom-call | flops 100000000 | bytes 1048576 | tf_op jit(solution)/shard_map/pallas_call | solution.py:418
  29.1 0.5 collective-permute-start.2
  29.7 6.7 %collective-permute-done.2.refs_2_ = bf16[4,128,256]{2,1,0:T(8,128)(2,1)S(1)} collective-permute-done((bf16[4,128,256]{2,1,0:T(8,128)(2,1)S(1)}, bf16[4,128,256]{2,1,0:T(8,128)(2,1)S(1)}, u32[]{:S(2)}, u32[]{:S(2)}) %collective-permute-start.2) | collective-permute-done | bytes 262176 | tf_op jit(solution)/shard_map/ppermute | solution.py:344
  36.4 0.9 %shard_map.161 = (bf16[4,128,128]{2,1,0:T(8,128)(2,1)S(1)}, bf16[4,128,256]{2,1,0:T(8,128)(2,1)S(1)}) custom-call(s32[4]{0:T(128)S(1)} %pad_add_fusion.1.place.refs_0_, bf16[4,128,256]{2,1,0:T(8,128)(2,1)S(1)} %shard_map.160.refs_1_, bf16[4,128,256]{2,1,0:T(8,128)(2,1)S(1)} %collective-permute-done.2.refs_2_, f32[8,128,128]{2,1,0:T(8,128)S(1)} %copy-done.2), custom_call_target="tpu_custom_call" | custom-call | flops 100000000 | bytes 1048576 | tf_op jit(solution)/shard_map/pallas_call | solution.py:423
  37.3 1.0 %collective-permute-start.3 = (bf16[4,128,128]{2,1,0:T(8,128)(2,1)S(1)}, bf16[4,128,128]{2,1,0:T(8,128)(2,1)S(1)}, u32[]{:S(2)}, u32[]{:S(2)}) collective-permute-start(bf16[4,128,128]{2,1,0:T(8,128)(2,1)S(1)} %get-tuple-element.53), channel_id=1, source_target_pairs={{0,16},{4,20},{8,24},{12,28},{16,0},{20,4},{24,8},{28,12},{1,17},{... | collective-permute-start | bytes 393224 | tf_op jit(solution)/shard_map/ppermute | solution.py:344
  38.2 3.4 %convolution_convert_fusion.gate_z = bf16[256,1024]{1,0:T(8,128)(2,1)S(1)} fusion(bf16[256,2048]{1,0:T(8,128)(2,1)S(1)} %copy-done, bf16[2048,1024]{1,0:T(8,128)(2,1)} %param.18), kind=kOutput, calls=%fused_computation.3 | convolution fusion | flops 1074003968 | bytes 5767168 | tf_op jit(solution)/shard_map/dot_general | solution.py:433
  41.8 1.5 %shard_map.162 = (bf16[4,256,128]{2,1,0:T(8,128)(2,1)S(1)}, f32[4,256,128]{2,1,0:T(8,128)S(1)}, f32[4,256,128]{2,1,0:T(8,128)S(1)}) custom-call(s32[4]{0:T(128)S(1)} %pad_add_fusion.1.place.refs_0_, bf16[2,256,512]{2,1,0:T(8,128)(2,1)S(1)} %fusion.5.qk, bf16[8,2048]{1,0:T(8,128)(2,1)S(1)} %collective-permute-done.halo, bf16[3,2,512]{2,1,0:T(2,128)(2,1)S(1)} %copy-done.8, ...), custom_call_target="tpu_custom_call" | custom-call | flops 2000000000 | bytes 4194304 | tf_op jit(solution)/shard_map/pallas_call | solution.py:395
  43.3 1.5 %shard_map.163 = (bf16[4,256,128]{2,1,0:T(8,128)(2,1)S(1)}, f32[4,256,128]{2,1,0:T(8,128)S(1)}, f32[4,256,128]{2,1,0:T(8,128)S(1)}) custom-call(s32[4]{0:T(128)S(1)} %pad_add_fusion.1.place.refs_0_, bf16[2,256,512]{2,1,0:T(8,128)(2,1)S(1)} %fusion.5.qk, bf16[8,2048]{1,0:T(8,128)(2,1)S(1)} %collective-permute-done.halo, bf16[3,2,512]{2,1,0:T(2,128)(2,1)S(1)} %copy-done.8, ...), custom_call_target="tpu_custom_call" | custom-call | flops 2000000000 | bytes 4194304 | tf_op jit(solution)/shard_map/pallas_call | solution.py:395
  44.9 0.9 %shard_map.164 = (bf16[4,128,128]{2,1,0:T(8,128)(2,1)S(1)}, bf16[4,128,128]{2,1,0:T(8,128)(2,1)S(1)}) custom-call(s32[4]{0:T(128)S(1)} %pad_add_fusion.1.place.refs_0_, bf16[4,128,256]{2,1,0:T(8,128)(2,1)S(1)} %get-tuple-element.52.prefix, f32[8,128,128]{2,1,0:T(8,128)S(1)} %copy-done.2, bf16[4,128,128]{2,1,0:T(8,128)(2,1)S(1)} %collective-permute-done.3.came, ...), custom_call_target="tpu_custom_call" | custom-call | flops 100000000 | bytes 1048576 | tf_op jit(solution)/shard_map/pallas_call | solution.py:437
  45.8 1.5 %collective-permute-start.4 = (bf16[4,128,128]{2,1,0:T(8,128)(2,1)S(1)}, bf16[4,128,128]{2,1,0:T(8,128)(2,1)S(1)}, u32[]{:S(2)}, u32[]{:S(2)}) collective-permute-start(bf16[4,128,128]{2,1,0:T(8,128)(2,1)S(1)} %get-tuple-element.74), channel_id=1, source_target_pairs={{0,4},{4,0},{8,12},{12,8},{16,20},{20,16},{24,28},{28,24},{1,5},{5... | collective-permute-start | bytes 393224 | tf_op jit(solution)/shard_map/ppermute | solution.py:344
  47.3 0.4 shard_map.165.mine_rows
  47.7 3.1 %collective-permute-done.4.states.away_states = bf16[4,128,128]{2,1,0:T(8,128)(2,1)S(1)} collective-permute-done((bf16[4,128,128]{2,1,0:T(8,128)(2,1)S(1)}, bf16[4,128,128]{2,1,0:T(8,128)(2,1)S(1)}, u32[]{:S(2)}, u32[]{:S(2)}) %collective-permute-start.4) | collective-permute-done | bytes 131104 | tf_op jit(solution)/shard_map/ppermute | solution.py:344
  50.8 1.5 %shard_map.166 = (bf16[256,512]{1,0:T(8,128)(2,1)S(1)}, bf16[1,256,512]{2,1,0:T(8,128)(2,1)S(1)}, bf16[1,256,512]{2,1,0:T(8,128)(2,1)S(1)}) custom-call(s32[3]{0:T(128)S(1)} %pad_add_fusion.side, bf16[4,128,128]{2,1,0:T(8,128)(2,1)S(1)} %collective-permute-done.4.states.away_states, bf16[4,256,128]{2,1,0:T(8,128)(2,1)S(1)} %get-tuple-element.75.reads, ...), custom_call_target="tpu_custom_call" | custom-call | flops 1000000000 | bytes 4194304 | tf_op jit(solution)/shard_map/pallas_call | solution.py:452
  52.4 1.5 %collective-permute-done.5 = bf16[1,256,512]{2,1,0:T(8,128)(2,1)S(1)} collective-permute-done((bf16[1,256,512]{2,1,0:T(8,128)(2,1)S(1)}, bf16[1,256,512]{2,1,0:T(8,128)(2,1)S(1)}, u32[]{:S(2)}, u32[]{:S(2)}) %collective-permute-start.5) | collective-permute-done | bytes 262176 | tf_op jit(solution)/shard_map/ppermute | solution.py:344
  54.0 1.6 %collective-permute-start.7 = (bf16[1,256,512]{2,1,0:T(8,128)(2,1)S(1)}, bf16[1,256,512]{2,1,0:T(8,128)(2,1)S(1)}, u32[]{:S(2)}, u32[]{:S(2)}) collective-permute-start(bf16[1,256,512]{2,1,0:T(8,128)(2,1)S(1)} %add_convert_fusion.1), channel_id=1, source_target_pairs={{0,2},{1,3},{2,0},{3,1},{4,6},{5,7},{6,4},{7,5},{8,10},{9,11},{10,... | collective-permute-start | bytes 786440 | tf_op jit(solution)/shard_map/ppermute | solution.py:344
  55.6 2.1 %shard_map.167 = (bf16[1,256,512]{2,1,0:T(8,128)(2,1)S(1)}, bf16[1,256,512]{2,1,0:T(8,128)(2,1)S(1)}, f32[1,8,128,128]{3,2,1,0:T(8,128)}) custom-call(s32[3]{0:T(128)S(1)} %pad_add_fusion.side, bf16[256,512]{1,0:T(8,128)(2,1)S(1)} %shard_map.165.mine_rows, bf16[256,512]{1,0:T(8,128)(2,1)S(1)} %get-tuple-element.81.other_rows, ...), custom_call_target="tpu_custom_call" | custom-call | flops 1000000000 | bytes 4194304 | tf_op jit(solution)/shard_map/pallas_call | solution.py:463
  57.7 4.7 %collective-permute-done.7 = bf16[1,256,512]{2,1,0:T(8,128)(2,1)S(1)} collective-permute-done((bf16[1,256,512]{2,1,0:T(8,128)(2,1)S(1)}, bf16[1,256,512]{2,1,0:T(8,128)(2,1)S(1)}, u32[]{:S(2)}, u32[]{:S(2)}) %collective-permute-start.7) | collective-permute-done | bytes 262176 | tf_op jit(solution)/shard_map/ppermute | solution.py:344
  62.4 0.8 %fusion.10 = bf16[256,512]{1,0:T(8,128)(2,1)} fusion(bf16[1,256,512]{2,1,0:T(8,128)(2,1)S(1)} %collective-permute-done.7, bf16[1,256,512]{2,1,0:T(8,128)(2,1)S(1)} %collective-permute-done.6, bf16[1,256,512]{2,1,0:T(8,128)(2,1)S(1)} %get-tuple-element.82), kind=kLoop, calls=%fused_computation.11 | loop fusion | flops 786432 | bytes 1048576 | tf_op jit(solution)/shard_map/convert_element_type | solution.py:481
  (59 shorter events, 0.4 us)
Async XLA Ops:
  0.6 1.2 %copy-start = (bf16[256,2048]{1,0:T(8,128)(2,1)S(1)}, bf16[256,2048]{1,0:T(8,128)(2,1)}, u32[]{:S(2)}) copy-start(bf16[256,2048]{1,0:T(8,128)(2,1)} %param.15) | copy-start | bytes 3145732
  0.6 5.0 %copy-start.26 = (bf16[2048,1024]{1,0:T(8,128)(2,1)S(1)}, bf16[2048,1024]{1,0:T(8,128)(2,1)}, u32[]{:S(2)}) copy-start(bf16[2048,1024]{1,0:T(8,128)(2,1)} %param.17) | copy-start | bytes 12582916
  5.6 4.4 %copy-start.25 = (bf16[2048,2,8]{0,2,1:T(8,128)(2,1)S(1)}, bf16[2048,2,8]{0,2,1:T(8,128)(2,1)}, u32[]{:S(2)}) copy-start(bf16[2048,2,8]{0,2,1:T(8,128)(2,1)} %param.19) | copy-start | bytes 196612
  5.7 9.4 %copy-start.5 = (bf16[3,1024]{1,0:T(4,128)(2,1)S(1)}, bf16[3,1024]{1,0:T(4,128)(2,1)}, u32[]{:S(2)}) copy-start(bf16[3,1024]{1,0:T(4,128)(2,1)} %hist_value.3) | copy-start | bytes 18436
  5.7 9.3 %copy-start.6 = (bf16[4,1024]{1,0:T(4,128)(2,1)S(1)}, bf16[4,1024]{1,0:T(4,128)(2,1)}, u32[]{:S(2)}) copy-start(bf16[4,1024]{1,0:T(4,128)(2,1)} %conv_value.3) | copy-start | bytes 24580
  5.7 9.3 %copy-start.7 = (bf16[4,2,512]{2,1,0:T(2,128)(2,1)S(1)}, bf16[4,2,512]{2,1,0:T(2,128)(2,1)}, u32[]{:S(2)}) copy-start(bf16[4,2,512]{2,1,0:T(2,128)(2,1)} %conv_qk.7) | copy-start | bytes 24580
  5.7 9.3 %copy-start.8 = (bf16[3,2,512]{2,1,0:T(2,128)(2,1)S(1)}, bf16[3,2,512]{2,1,0:T(2,128)(2,1)}, u32[]{:S(2)}) copy-start(bf16[3,2,512]{2,1,0:T(2,128)(2,1)} %hist_qk.7) | copy-start | bytes 18436
  5.7 9.3 %copy-start.9 = (f32[8]{0:T(128)S(1)}, f32[8]{0:T(128)}, u32[]{:S(2)}) copy-start(f32[8]{0:T(128)} %a_log.3) | copy-start | bytes 100
  5.7 9.3 %copy-start.10 = (f32[8]{0:T(128)S(1)}, f32[8]{0:T(128)}, u32[]{:S(2)}) copy-start(f32[8]{0:T(128)} %dt_bias.3) | copy-start | bytes 100
  5.7 9.3 %copy-start.11 = (f32[8]{0:T(128)S(1)}, f32[8]{0:T(128)}, u32[]{:S(2)}) copy-start(f32[8]{0:T(128)} %beta_bias.3) | copy-start | bytes 100
  7.0 12.6 %copy-start.3 = (bf16[256,1024]{1,0:T(8,128)(2,1)}, bf16[256,1024]{1,0:T(8,128)(2,1)S(1)}, u32[]{:S(2)}) copy-start(bf16[256,1024]{1,0:T(8,128)(2,1)S(1)} %convolution_convert_fusion.1.value) | copy-start | bytes 1572868
  7.1 7.9 %collective-permute-start = (bf16[8,2048]{1,0:T(8,128)(2,1)S(1)}, bf16[8,2048]{1,0:T(8,128)(2,1)S(1)}, u32[]{:S(2)}, u32[]{:S(2)}) collective-permute-start(bf16[8,2048]{1,0:T(8,128)(2,1)S(1)} %pad_maximum_fusion), channel_id=1, source_target_pairs={{0,4},{4,8},{8,12},{12,16},{16,20},{20,24},{24,28},{28,0},{1,5},{5... | collective-permute-start | bytes 98312 | tf_op jit(solution)/shard_map/ppermute | solution.py:367
  20.5 5.8 %copy-start.17 = (bf16[2,256,128]{2,1,0:T(8,128)(2,1)}, bf16[2,256,128]{2,1,0:T(8,128)(2,1)S(1)}, u32[]{:S(2)}) copy-start(bf16[2,256,128]{2,1,0:T(8,128)(2,1)S(1)} %get-tuple-element.62.keys) | copy-start | bytes 393220
  20.5 5.8 %copy-start.19 = (f32[256,128]{1,0:T(8,128)}, f32[256,128]{1,0:T(8,128)S(1)}, u32[]{:S(2)}) copy-start(f32[256,128]{1,0:T(8,128)S(1)} %get-tuple-element.65.cols) | copy-start | bytes 393220
  20.5 15.9 %copy-start.2 = (f32[8,128,128]{2,1,0:T(8,128)S(1)}, f32[8,128,128]{2,1,0:T(8,128)}, u32[]{:S(2)}) copy-start(f32[8,128,128]{2,1,0:T(8,128)} %state_in.1) | copy-start | bytes 1572868
  20.5 7.9 %collective-permute-start.1 = (bf16[4,128,256]{2,1,0:T(8,128)(2,1)S(1)}, bf16[4,128,256]{2,1,0:T(8,128)(2,1)S(1)}, u32[]{:S(2)}, u32[]{:S(2)}) collective-permute-start(bf16[4,128,256]{2,1,0:T(8,128)(2,1)S(1)} %get-tuple-element.44.away_maps), channel_id=1, source_target_pairs={{0,4},{4,0},{8,12},{12,8},{16,20},{20,16},{24,28},{28,24},{1,5},{5... | collective-permute-start | bytes 786440 | tf_op jit(solution)/shard_map/ppermute | solution.py:344
  20.5 1.2 %copy-start.4 = (bf16[256,1024]{1,0:T(8,128)(2,1)S(1)}, bf16[256,1024]{1,0:T(8,128)(2,1)}, u32[]{:S(2)}) copy-start(bf16[256,1024]{1,0:T(8,128)(2,1)} %copy-done.3) | copy-start | bytes 1572868
  26.3 0.8 %copy-start.15 = (bf16[4,256,256]{2,1,0:T(8,128)(2,1)}, bf16[4,256,256]{2,1,0:T(8,128)(2,1)S(1)}, u32[]{:S(2)}) copy-start(bf16[4,256,256]{2,1,0:T(8,128)(2,1)S(1)} %get-tuple-element.55.solved) | copy-start | bytes 1572868
  29.1 7.3 %collective-permute-start.2 = (bf16[4,128,256]{2,1,0:T(8,128)(2,1)S(1)}, bf16[4,128,256]{2,1,0:T(8,128)(2,1)S(1)}, u32[]{:S(2)}, u32[]{:S(2)}) collective-permute-start(bf16[4,128,256]{2,1,0:T(8,128)(2,1)S(1)} %shard_map.160.refs_1_), channel_id=1, source_target_pairs={{0,8},{4,12},{8,0},{12,4},{16,24},{20,28},{24,16},{28,20},{1,9},{5... | collective-permute-start | bytes 786440 | tf_op jit(solution)/shard_map/ppermute | solution.py:344
  29.6 12.1 %copy-start.12 = (f32[128]{0:T(128)S(1)}, f32[128]{0:T(128)}, u32[]{:S(2)}) copy-start(f32[128]{0:T(128)} %param.28) | copy-start | bytes 1540
  29.7 12.1 %copy-start.16 = (bf16[4,256,256]{2,1,0:T(8,128)(2,1)S(1)}, bf16[4,256,256]{2,1,0:T(8,128)(2,1)}, u32[]{:S(2)}) copy-start(bf16[4,256,256]{2,1,0:T(8,128)(2,1)} %copy-done.15) | copy-start | bytes 1572868
  29.7 12.1 %copy-start.22 = (bf16[2,256,128]{2,1,0:T(8,128)(2,1)S(1)}, bf16[2,256,128]{2,1,0:T(8,128)(2,1)}, u32[]{:S(2)}) copy-start(bf16[2,256,128]{2,1,0:T(8,128)(2,1)} %copy-done.21) | copy-start | bytes 393220
  29.7 12.1 %copy-start.24 = (f32[256,128]{1,0:T(8,128)S(1)}, f32[256,128]{1,0:T(8,128)}, u32[]{:S(2)}) copy-start(f32[256,128]{1,0:T(8,128)} %copy-done.23) | copy-start | bytes 393220
  37.3 7.6 %collective-permute-start.3 = (bf16[4,128,128]{2,1,0:T(8,128)(2,1)S(1)}, bf16[4,128,128]{2,1,0:T(8,128)(2,1)S(1)}, u32[]{:S(2)}, u32[]{:S(2)}) collective-permute-start(bf16[4,128,128]{2,1,0:T(8,128)(2,1)S(1)} %get-tuple-element.53), channel_id=1, source_target_pairs={{0,16},{4,20},{8,24},{12,28},{16,0},{20,4},{24,8},{28,12},{1,17},{... | collective-permute-start | bytes 393224 | tf_op jit(solution)/shard_map/ppermute | solution.py:344
  41.7 1.6 %copy-start.14 = (bf16[4,256,256]{2,1,0:T(8,128)(2,1)S(1)}, bf16[4,256,256]{2,1,0:T(8,128)(2,1)}, u32[]{:S(2)}) copy-start(bf16[4,256,256]{2,1,0:T(8,128)(2,1)} %copy-done.13) | copy-start | bytes 1572868
  41.7 1.6 %copy-start.18 = (bf16[2,256,128]{2,1,0:T(8,128)(2,1)S(1)}, bf16[2,256,128]{2,1,0:T(8,128)(2,1)}, u32[]{:S(2)}) copy-start(bf16[2,256,128]{2,1,0:T(8,128)(2,1)} %copy-done.17) | copy-start | bytes 393220
  41.7 1.6 %copy-start.20 = (f32[256,128]{1,0:T(8,128)S(1)}, f32[256,128]{1,0:T(8,128)}, u32[]{:S(2)}) copy-start(f32[256,128]{1,0:T(8,128)} %copy-done.19) | copy-start | bytes 393220
  44.9 6.0 %copy-start.1 = (bf16[1024,2048]{1,0:T(8,128)(2,1)S(1)}, bf16[1024,2048]{1,0:T(8,128)(2,1)}, u32[]{:S(2)}) copy-start(bf16[1024,2048]{1,0:T(8,128)(2,1)} %w_out.3) | copy-start | bytes 12582916
  45.8 5.0 %collective-permute-start.4 = (bf16[4,128,128]{2,1,0:T(8,128)(2,1)S(1)}, bf16[4,128,128]{2,1,0:T(8,128)(2,1)S(1)}, u32[]{:S(2)}, u32[]{:S(2)}) collective-permute-start(bf16[4,128,128]{2,1,0:T(8,128)(2,1)S(1)} %get-tuple-element.74), channel_id=1, source_target_pairs={{0,4},{4,0},{8,12},{12,8},{16,20},{20,16},{24,28},{28,24},{1,5},{5... | collective-permute-start | bytes 393224 | tf_op jit(solution)/shard_map/ppermute | solution.py:344
  52.3 1.6 %collective-permute-start.5 = (bf16[1,256,512]{2,1,0:T(8,128)(2,1)S(1)}, bf16[1,256,512]{2,1,0:T(8,128)(2,1)S(1)}, u32[]{:S(2)}, u32[]{:S(2)}) collective-permute-start(bf16[1,256,512]{2,1,0:T(8,128)(2,1)S(1)} %get-tuple-element.79), channel_id=1, source_target_pairs={{0,1},{1,0},{2,3},{3,2},{4,5},{5,4},{6,7},{7,6},{8,9},{9,8},{10,11... | collective-permute-start | bytes 786440 | tf_op jit(solution)/shard_map/ppermute | solution.py:344
  54.0 8.4 %collective-permute-start.7 = (bf16[1,256,512]{2,1,0:T(8,128)(2,1)S(1)}, bf16[1,256,512]{2,1,0:T(8,128)(2,1)S(1)}, u32[]{:S(2)}, u32[]{:S(2)}) collective-permute-start(bf16[1,256,512]{2,1,0:T(8,128)(2,1)S(1)} %add_convert_fusion.1), channel_id=1, source_target_pairs={{0,2},{1,3},{2,0},{3,1},{4,6},{5,7},{6,4},{7,5},{8,10},{9,11},{10,... | collective-permute-start | bytes 786440 | tf_op jit(solution)/shard_map/ppermute | solution.py:344
  57.7 4.7 %collective-permute-start.6 = (bf16[1,256,512]{2,1,0:T(8,128)(2,1)S(1)}, bf16[1,256,512]{2,1,0:T(8,128)(2,1)S(1)}, u32[]{:S(2)}, u32[]{:S(2)}) collective-permute-start(bf16[1,256,512]{2,1,0:T(8,128)(2,1)S(1)} %get-tuple-element.83), channel_id=1, source_target_pairs={{0,1},{1,0},{2,3},{3,2},{4,5},{5,4},{6,7},{7,6},{8,9},{9,8},{10,11... | collective-permute-start | bytes 786440 | tf_op jit(solution)/shard_map/ppermute | solution.py:344
  (3 other events, 2.1 us)

commit v2 on v1

--- a/solution.py
+++ b/solution.py
@@ -10,7 +10,7 @@
 KD = 128
 DV = 128
 HALF = 128
-HALO = 8
+HALO = 16
 F32 = jnp.float32
 BF16 = jnp.bfloat16
 VMEM = pl.BlockSpec(memory_space=pltpu.VMEM)
@@ -44,11 +44,11 @@
     return values * lax.rsqrt(jnp.sum(values * values, axis=-1, keepdims=True) + 1e-06)
 
 
-def conv_rows(block, halo, history, weight, first):
+def conv_rows(block, halo, weight):
     rows = block.shape[0]
     taps = weight.shape[0]
     start = HALO - (taps - 1)
-    joined = jnp.concatenate([jnp.where(first, history, halo), block], 0)
+    joined = jnp.concatenate([halo, block], 0)
     total = weight[0:1] * joined[start : start + rows]
     for tap in range(1, taps):
         total = total + weight[tap : tap + 1] * joined[start + tap : start + tap + rows]
@@ -90,45 +90,48 @@
 
 def load_small(hist_qk, conv_qk, part, hist_s, conv_s):
     taps = conv_qk.shape[0]
-    hist_s[HALO - taps + 1 :, :] = hist_qk[...].astype(F32)[:, part, :]
+    if hist_s is not None:
+        hist_s[HALO - taps + 1 :, :] = hist_qk[...].astype(F32)[:, part, :]
     conv_s[...] = conv_qk[...].astype(F32)[:, part, :]
 
 
-def key_block(qk, halo, hist_s, conv_s, part, index, first):
-    key_cols = qk.shape[2]
-    lanes = lane_block(index, KD)
-    halo_lanes = lane_block(part * (key_cols // KD) + index, KD)
-    return unit_rows(
-        conv_rows(
-            qk[part, :, lanes].astype(F32),
-            halo[:, halo_lanes].astype(F32),
-            hist_s[:, lanes],
-            conv_s[:, lanes],
-            first,
-        )
-    )
+def front_rows(block, halo, hist, weight, lanes, halo_lanes, first):
+    before = jnp.where(first, hist[:, lanes], halo[:, halo_lanes].astype(F32))
+    return conv_rows(block.astype(F32), before, weight)
+
+
+def running(column, count):
+    sums = [column[0:1]]
+    for i in range(1, count):
+        sums.append(sums[-1] + column[i : i + 1])
+    return sums
+
+
+def stacked(rows_in, width):
+    return jnp.concatenate(rows_in + [jnp.zeros((HALO - len(rows_in), width), F32)], 0)
 
 
 def prepare_kernel(
-    own, place, a_log, dt_bias, beta_bias, qk, value, gates, halo, hist_qk, hist_value,
-    conv_qk, conv_value, keys_out, solved_out, maps_out, rows_out, cols_out,
-    hist_s, conv_s, hist_v,
+    own, place, a_log, dt_bias, beta_bias, qk, value, gates, conv_qk, conv_value,
+    keys_out, solved_out, maps_out, rows_out, cols_out, conv_s,
 ):
     heads = gates.shape[1] // 2
     rows = gates.shape[2]
     key_heads = heads // 2
-    key_cols = qk.shape[2]
     taps = conv_value.shape[0]
-    first = place[0] == 0
     side = place[1] if own else 1 - place[1]
-    load_small(hist_qk, conv_qk, 1, hist_s, conv_s)
-    hist_v[HALO - taps + 1 :, :] = hist_value[...].astype(F32)
+    load_small(None, conv_qk, 1, None, conv_s)
+    zero = jnp.zeros((HALO, KD), F32)
+    rest = lax.broadcasted_iota(jnp.int32, (heads, rows), 1) >= taps - 1
     strength = jax.nn.sigmoid(
         picked(side, gates[0].astype(F32)) + scalar_column(beta_bias, side * heads, heads)
     )
     decay_in = picked(side, gates[1].astype(F32)) + scalar_column(dt_bias, side * heads, heads)
     soft = jnp.maximum(decay_in, 0.0) + jnp.log1p(jnp.exp(-jnp.abs(decay_in)))
     log_decay = -jnp.exp(scalar_column(a_log, side * heads, heads)) * soft
+    raw = [strength, log_decay]
+    strength = jnp.where(rest, strength, 0.0)
+    log_decay = jnp.where(rest, log_decay, 0.0)
     line = lax.broadcasted_iota(jnp.int32, (rows, rows), 0)
     across = lax.broadcasted_iota(jnp.int32, (rows, rows), 1)
     upper = jnp.where(line <= across, 1.0, 0.0).astype(BF16)
@@ -137,8 +140,8 @@
     cumul = dot(high, upper) + (dot(low, upper) + dot(lowest, upper))
     fade = jnp.exp(cumul)
     to_end = jnp.exp(cumul[:, rows - 1 : rows] - cumul)
-    pad = jnp.zeros((128 - 4 * heads, rows), F32)
-    cols = jnp.concatenate([cumul, strength, strength * fade, fade, pad], 0).T
+    pad = jnp.zeros((128 - 6 * heads, rows), F32)
+    cols = jnp.concatenate([cumul, strength, strength * fade, fade, *raw, pad], 0).T
     rows_out[...] = cumul
     cols_out[...] = cols
 
@@ -151,7 +154,8 @@
     rhs = []
     ends = []
     for key_head in range(key_heads):
-        key = key_block(qk, halo, hist_s, conv_s, 1, side * key_heads + key_head, first)
+        lanes = lane_block(side * key_heads + key_head, KD)
+        key = unit_rows(conv_rows(qk[1, :, lanes].astype(F32), zero, conv_s[:, lanes]))
         key_low = key.astype(BF16)
         keys_out[key_head] = key_low
         dots = dot_nt(key_low, key_low)
@@ -159,13 +163,7 @@
         for head in (2 * key_head, 2 * key_head + 1):
             index = side * heads + head
             lanes = lane_block(index, DV)
-            val = conv_rows(
-                value[:, lanes].astype(F32),
-                halo[:, lane_block(2 * key_cols // DV + index, DV)].astype(F32),
-                hist_v[:, lanes],
-                conv_value[:, lanes].astype(F32),
-                first,
-            )
+            val = conv_rows(value[:, lanes].astype(F32), zero, conv_value[:, lanes].astype(F32))
             col = cols[:, head : head + 1]
             beta = cols[:, heads + head : heads + head + 1]
             beta_fade = cols[:, 2 * heads + head : 2 * heads + head + 1]
@@ -209,34 +207,114 @@
         solved_out[head] = both
         ended = dot(ends[head], both)
         fade_end = fade[head : head + 1, rows - 1 : rows]
-        own = jnp.concatenate([eye * fade_end - ended[:, :KD], ended[:, KD:]], 1).astype(BF16)
+        own = jnp.concatenate([eye * fade_end - ended[:, :KD], ended[:, KD:]], 1)
         maps_out[head] = own
 
 
+def front_kernel(
+    own, place, qk, value, halo, hist_qk, hist_value, conv_qk, conv_value, rest, cols,
+    maps_out, keys_out, solved_out, hist_s, conv_s, hist_v,
+):
+    heads = rest.shape[0]
+    key_heads = heads // 2
+    key_cols = qk.shape[2]
+    taps = conv_value.shape[0]
+    count = taps - 1
+    first = place[0] == 0
+    side = place[1] if own else 1 - place[1]
+    load_small(hist_qk, conv_qk, 1, hist_s, conv_s)
+    hist_v[HALO - count :, :] = hist_value[...].astype(F32)
+    for pair in range(key_heads):
+        index = side * key_heads + pair
+        lanes = lane_block(index, KD)
+        key = unit_rows(
+            front_rows(
+                qk[1, :HALO, lanes], halo, hist_s, conv_s[:, lanes], lanes,
+                lane_block(key_cols // KD + index, KD), first,
+            )
+        )
+        keys = [key[i : i + 1] for i in range(count)]
+        keys_out[pair] = stacked(keys, KD)
+        dots = {
+            (i, j): jnp.sum(keys[i] * keys[j], axis=-1, keepdims=True)
+            for i in range(count)
+            for j in range(i)
+        }
+        for head in (2 * pair, 2 * pair + 1):
+            index = side * heads + head
+            lanes = lane_block(index, DV)
+            val = front_rows(
+                value[:HALO, lanes], halo, hist_v, conv_value[:, lanes].astype(F32), lanes,
+                lane_block(2 * key_cols // DV + index, DV), first,
+            )
+            beta = cols[:HALO, 4 * heads + head : 4 * heads + head + 1]
+            cumul = running(cols[:HALO, 5 * heads + head : 5 * heads + head + 1], count)
+            solved = []
+            for i in range(count):
+                need = jnp.concatenate([jnp.exp(cumul[i]) * keys[i], val[i : i + 1]], 1)
+                for j in range(i):
+                    need = need - (jnp.exp(cumul[i] - cumul[j]) * dots[i, j]) * solved[j]
+                solved.append(beta[i : i + 1] * need)
+            solved_out[head] = stacked(solved, KD + DV)
+            ends = stacked([jnp.exp(cumul[-1] - cumul[i]) * keys[i] for i in range(count)], KD)
+            maps_out[head] = put_ahead(rest[head], jnp.exp(cumul[-1]), ends, solved_out[head]).astype(BF16)
+
+
+def put_ahead(rest, fade, ends, solved):
+    through = dot_nt(rest[:, :KD].astype(BF16), ends.astype(BF16)).astype(BF16)
+    moved = dot(through, solved.astype(BF16))
+    return jnp.concatenate([fade * rest[:, :KD] - moved[:, :KD], rest[:, KD:] + moved[:, KD:]], 1)
+
+
 def query_kernel(
-    own, place, qk, halo, hist_qk, conv_qk, keys, solved, cumul, cols, gate_z, gain,
-    reads_out, local_out, gate_out, hist_s, conv_s,
+    own, place, qk, halo, hist_qk, conv_qk, keys, solved, cumul, cols, front_keys, front_solved,
+    gate_z, gain, reads_out, local_out, gate_out, hist_s, conv_s,
 ):
     heads, rows = cumul.shape
     key_heads = heads // 2
+    count = conv_qk.shape[0] - 1
     first = place[0] == 0
     side = place[1] if own else 1 - place[1]
     load_small(hist_qk, conv_qk, 0, hist_s, conv_s)
     line = lax.broadcasted_iota(jnp.int32, (rows, rows), 0)
     across = lax.broadcasted_iota(jnp.int32, (rows, rows), 1)
     within = line >= across
-    for key_head in range(key_heads):
-        query = key_block(qk, halo, hist_s, conv_s, 0, side * key_heads + key_head, first)
+    in_front = lax.broadcasted_iota(jnp.int32, (HALO, 1), 0) < count
+    zero = jnp.zeros((HALO, KD), F32)
+    for pair in range(key_heads):
+        lanes = lane_block(side * key_heads + pair, KD)
+        query = unit_rows(conv_rows(qk[0, :, lanes].astype(F32), zero, conv_s[:, lanes]))
         query = query * (KD**-0.5)
-        dots = dot_nt(query.astype(BF16), keys[key_head])
-        for head in (2 * key_head, 2 * key_head + 1):
+        ahead = unit_rows(
+            front_rows(qk[0, :HALO, lanes], halo, hist_s, conv_s[:, lanes], lanes, lanes, first)
+        ) * (KD**-0.5)
+        dots = dot_nt(query.astype(BF16), keys[pair])
+        front = [front_keys[pair, i : i + 1] for i in range(count)]
+        for head in (2 * pair, 2 * pair + 1):
             col = cols[:, head : head + 1]
             fade = cols[:, 3 * heads + head : 3 * heads + head + 1]
             spread = jnp.exp(jnp.minimum(col - cumul[head : head + 1], 0.0))
             attend = jnp.where(within, spread * dots, 0.0).astype(BF16)
             part = dot(attend, solved[head])
-            reads_out[head] = (fade * query - part[:, :KD]).astype(BF16)
-            local_out[head] = part[:, KD:]
+            reads = jnp.concatenate([fade * query - part[:, :KD], part[:, KD:]], 1)
+            sums = running(cols[:HALO, 5 * heads + head : 5 * heads + head + 1], count)
+            ends = stacked([jnp.exp(sums[-1] - sums[i]) * front[i] for i in range(count)], KD)
+            reads = put_ahead(reads, jnp.exp(sums[-1]), ends, front_solved[head])
+            first_rows = []
+            for i in range(count):
+                asked = ahead[i : i + 1]
+                row = jnp.concatenate([jnp.exp(sums[i]) * asked, jnp.zeros((1, DV), F32)], 1)
+                for j in range(i + 1):
+                    weight = jnp.exp(sums[i] - sums[j]) * jnp.sum(
+                        asked * front[j], axis=-1, keepdims=True
+                    )
+                    term = weight * front_solved[head, j : j + 1]
+                    row = row + jnp.concatenate([-term[:, :KD], term[:, KD:]], 1)
+                first_rows.append(row)
+            top = jnp.where(in_front, stacked(first_rows, KD + DV), reads[:HALO])
+            reads = jnp.concatenate([top, reads[HALO:]], 0)
+            reads_out[head] = reads[:, :KD].astype(BF16)
+            local_out[head] = reads[:, KD:]
             lanes = lane_block(side * heads + head, DV)
             gate_out[head] = silu(gate_z[:, lanes].astype(F32)) * gain[...]
 
@@ -367,30 +445,42 @@
     halo = lax.ppermute(ends, "seq", [(i, (i + 1) % n_seq) for i in range(n_seq)])
     gates = jnp.einsum("td,dch->cht", hidden_in, w_ba, preferred_element_type=F32).astype(BF16)
 
-    def prepare(own):
+    small = [pltpu.VMEM((HALO, key_cols), F32), pltpu.VMEM((taps, key_cols), F32)]
+
+    def prepare(own, qk):
         return call(
             functools.partial(prepare_kernel, own),
             (
                 shape((half // 2, rows, KD), BF16),
                 shape((half, rows, KD + DV), BF16),
-                shape((half, KD, KD + DV), BF16),
+                shape((half, KD, KD + DV), F32),
                 shape((half, rows), F32),
                 shape((rows, 128), F32),
             ),
-            [SMEM] * 4 + [VMEM] * 8,
+            [SMEM] * 4 + [VMEM] * 5,
             4 * 10**9,
             4 << 20,
-            [
-                pltpu.VMEM((HALO, key_cols), F32),
-                pltpu.VMEM((taps, key_cols), F32),
-                pltpu.VMEM((HALO, heads * DV), F32),
-            ],
+            small[1:],
+        )(place, a_log, dt_bias, beta_bias, qk, value, gates, conv_qk, conv_value)
+
+    def front(own, prepared):
+        return call(
+            functools.partial(front_kernel, own),
+            (
+                shape((half, KD, KD + DV), BF16),
+                shape((half // 2, HALO, KD), F32),
+                shape((half, HALO, KD + DV), F32),
+            ),
+            [SMEM] + [VMEM] * 9,
+            10**8,
+            1 << 20,
+            small + [pltpu.VMEM((HALO, heads * DV), F32)],
         )(
-            place, a_log, dt_bias, beta_bias, qk, value, gates, halo, hist_qk, hist_value,
-            conv_qk, conv_value,
+            place, qk, value, halo, hist_qk, hist_value, conv_qk, conv_value,
+            prepared[2], prepared[4],
         )
 
-    def query(own, prepared):
+    def query(own, prepared, fronted, qk):
         keys, solved, _, cumul, cols = prepared
         return call(
             functools.partial(query_kernel, own),
@@ -399,26 +489,35 @@
                 shape((half, rows, DV), F32),
                 shape((half, rows, DV), F32),
             ),
-            [SMEM] + [VMEM] * 10,
+            [SMEM] + [VMEM] * 12,
             2 * 10**9,
             4 << 20,
-            [pltpu.VMEM((HALO, key_cols), F32), pltpu.VMEM((taps, key_cols), F32)],
+            small,
         )(
-            place, qk, halo, hist_qk, conv_qk, keys, solved, cumul, cols, gate_z,
-            norm_gain.reshape(1, DV),
+            place, qk, halo, hist_qk, conv_qk, keys, solved, cumul, cols, fronted[1], fronted[2],
+            gate_z, norm_gain.reshape(1, DV),
         )
 
-    away = prepare(False)
-    received = swapped(away[2], "seq", 1)
-    own = prepare(True)
-    received, own = lax.optimization_barrier((received, own))
-    maps = own[2]
+    away = prepare(False, qk)
+    halo, away = lax.optimization_barrier((halo, away))
+    away_front = front(False, away)
+    received = swapped(away_front[0], "seq", 1)
+    later, _ = lax.optimization_barrier((qk, away_front[0]))
+    own = prepare(True, later)
+    own_front = front(True, own)
+    maps, away_maps = own_front[0], away_front[0]
+    received, own, maps = lax.optimization_barrier((received, own, maps))
+
     map_shape = shape((half, KD, KD + DV), BF16)
     state_shape = shape((half, KD, DV), BF16)
     total = call(pair_kernel, map_shape, [SMEM, VMEM, VMEM], 10**8, 1 << 20)(place, maps, received)
     prefix = ()
     for level in range(1, levels - 1):
         other = swapped(total, "seq", 1 << level)
+        if level == 1:
+            later, _ = lax.optimization_barrier((hidden_in, total))
+            gate_z = jnp.dot(later, w_outgate, preferred_element_type=F32).astype(BF16)
+            other, gate_z = lax.optimization_barrier((other, gate_z))
         last = level == levels - 2
         total, prefix = call(
             functools.partial(level_kernel, level, last),
@@ -429,10 +528,9 @@
         )(place, total, other, *prefix, state_in)
         prefix = (prefix,)
     came = swapped(total, "seq", 1 << (levels - 1))
-    later, _ = lax.optimization_barrier((hidden_in, total))
-    gate_z = jnp.dot(later, w_outgate, preferred_element_type=F32).astype(BF16)
-    own_reads = query(True, own)
-    away_reads = query(False, away)
+    later, _ = lax.optimization_barrier((qk, total))
+    own_reads = query(True, own, own_front, later)
+    away_reads = query(False, away, away_front, later)
     came, own_reads, away_reads = lax.optimization_barrier((came, own_reads, away_reads))
     mine, send_state = call(
         functools.partial(enter_kernel, levels - 1),
@@ -466,7 +564,7 @@
         [SMEM] + [VMEM] * 7,
         10**9,
         4 << 20,
-    )(side, own_rows, other_rows, w_out, maps, mine, away[2], other_state)
+    )(side, own_rows, other_rows, w_out, maps, mine, away_maps, other_state)
     came_out = swapped(send_out, "head", 1)
     mixed = keep.astype(F32) + came_out.astype(F32) + came_far.astype(F32)
     step = 4

time: 63.4 us -> 59.5 us (0.938)
  waiting for transfers between devices: 20.5 us -> 14.5 us
  local copies, waits for them, and re-layouts: 5.33 us -> 1.3 us
  Pallas kernels: 18.8 us -> 22.7 us
  starting transfers between devices: 7.62 us -> 11.5 us
  matrix products: 8.86 us -> 6.72 us
    ppermute x1, waiting for transfers between devices: 4.47 us -> 0.38 us  [local(): lax.ppermute(ends, 'seq', [(i, (i + 1) % n_seq) for i in range(n_seq)])]
    unnamed x54 -> x28, local copies, waits for them, and re-layouts: 5.33 us -> 1.29 us
    ppermute x7, starting transfers between devices: 4.62 us -> 8.56 us  [swapped(): return lax.ppermute(value, axis, [(i, i ^ step) for i in range(count)])]
    pallas_call x0 -> x2, Pallas kernels: none -> 2.32 us  [front(): call(functools.partial(front_kernel, own), (shape((half, KD, KD + DV), BF...]
    dot_general x1, matrix products: 3.43 us -> 1.29 us  [local(): gate_z = jnp.dot(later, w_outgate, preferred_element_type=F32).astype(BF16)]
    ppermute x7, waiting for transfers between devices: 16 us -> 14.1 us  [swapped(): return lax.ppermute(value, axis, [(i, i ^ step) for i in range(count)])]
    pallas_call x2, Pallas kernels: 3.06 us -> 4.6 us  [query(): call(functools.partial(query_kernel, own), (shape((half, rows, KD), BF16)...]
  transfers between devices with their start and end apart: 8 -> 8, of which waited for: 5 -> 7; matrix products, arithmetic and copies ran while one was open for 6% -> 3% of each run, Pallas kernels for 16% -> 29%
where the time goes in v2:
time: 59.5 us; the launch traced here: 59.3 us
  Pallas kernels  22.7 us (38%)
  waiting for transfers between devices  14.5 us (24%)
  starting transfers between devices  11.5 us (19%)
  matrix products  6.72 us (11%)
  other arithmetic  1.67 us (3%)
  local copies, waits for them, and re-layouts  1.3 us (2%)
  between operations  0.93 us (2%)
    ppermute x7, waiting for transfers between devices, swapped(): return lax.ppermute(value, axis, [(i, i ^ step) for i in range(count)])  14.1 us
    pallas_call x2, Pallas kernels, prepare(): call(functools.partial(prepare_kernel, own), (shape((half // 2, rows, KD)...  9.2 us
    ppermute x7, starting transfers between devices, swapped(): return lax.ppermute(value, axis, [(i, i ^ step) for i in range(count)])  8.56 us
    pallas_call x2, Pallas kernels, query(): call(functools.partial(query_kernel, own), (shape((half, rows, KD), BF16)...  4.6 us
    dot_general x1, matrix products, local(): jnp.einsum('td,dce->cte', hidden_in, w_qk, preferred_element_type=F32)  3.77 us
    ppermute x1, starting transfers between devices, local(): lax.ppermute(ends, 'seq', [(i, (i + 1) % n_seq) for i in range(n_seq)])  2.94 us
    pallas_call x2, Pallas kernels, front(): call(functools.partial(front_kernel, own), (shape((half, KD, KD + DV), BF...  2.32 us
    pallas_call x1, Pallas kernels, local(): call(home_kernel, (part_shape, part_shape, shape((1, heads, KD, DV), F32)...  2.13 us
  transfers between devices with their start and end apart: 8, of which 7 were waited for; matrix products, arithmetic and copies ran while one was open for 3% of the time, Pallas kernels for 29%

profile of v2, /device:TPU:0, one launch (start us, length us, event | category | flops | bytes accessed | tf_op | source)
XLA Modules:
  0.0 59.3 jit_solution(11176156258863981101)
XLA Ops:
  0.7 1.2 %copy-done = bf16[256,2048]{1,0:T(8,128)(2,1)S(1)} copy-done((bf16[256,2048]{1,0:T(8,128)(2,1)S(1)}, bf16[256,2048]{1,0:T(8,128)(2,1)}, u32[]{:S(2)}) %copy-start) | copy-done | bytes 1048600
  1.9 3.8 %fusion.5.qk = bf16[2,256,512]{2,1,0:T(8,128)(2,1)S(1)} fusion(bf16[2048,2,512]{2,1,0:T(2,128)(2,1)} %param.16, bf16[256,2048]{1,0:T(8,128)(2,1)S(1)} %copy-done), kind=kOutput, calls=%fused_computation.5 | convolution fusion | flops 1074003968 | bytes 5767168 | tf_op jit(solution)/shard_map/td,dce->cte/dot_general | solution.py:441
  5.7 1.3 %convolution_convert_fusion.1.value = bf16[256,1024]{1,0:T(8,128)(2,1)S(1)} fusion(bf16[256,2048]{1,0:T(8,128)(2,1)S(1)} %copy-done, bf16[2048,1024]{1,0:T(8,128)(2,1)S(1)} %copy-done.12), kind=kOutput, calls=%fused_computation.4 | convolution fusion | flops 1074003968 | bytes 5767168 | tf_op jit(solution)/shard_map/dot_general | solution.py:442
  7.0 0.6 %pad_maximum_fusion = bf16[16,2048]{1,0:T(8,128)(2,1)} fusion(bf16[16,1024]{1,0:T(8,128)(2,1)S(1)} %slice.14, bf16[16,512]{1,0:T(8,128)(2,1)S(1)} %get-tuple-element.119, bf16[16,512]{1,0:T(8,128)(2,1)S(1)} %get-tuple-element.118), kind=kLoop, calls=%fused_computation.12 | loop fusion | flops 196608 | bytes 131072 | tf_op jit(solution)/shard_map/concatenate | solution.py:444
  7.7 2.9 %collective-permute-start = (bf16[16,2048]{1,0:T(8,128)(2,1)}, bf16[16,2048]{1,0:T(8,128)(2,1)S(1)}, u32[]{:S(2)}, u32[]{:S(2)}) collective-permute-start(bf16[16,2048]{1,0:T(8,128)(2,1)} %pad_maximum_fusion), channel_id=1, source_target_pairs={{0,4},{4,8},{8,12},{12,16},{16,20},{20,24},{24,28},{28,0},{1,5},{5... | collective-permute-start | bytes 196616 | tf_op jit(solution)/shard_map/ppermute | solution.py:445
  10.6 0.4 convolution_convert_fusion.2.gates
  11.0 0.1 pad_add_fusion.1.place.refs_0_
  11.1 4.6 %shard_map.158 = (bf16[2,256,128]{2,1,0:T(8,128)(2,1)S(1)}, bf16[4,256,256]{2,1,0:T(8,128)(2,1)S(1)}, f32[4,128,256]{2,1,0:T(8,128)S(1)}, f32[4,256]{1,0:T(4,128)S(1)}, f32[256,128]{1,0:T(8,128)S(1)}) custom-call(s32[4]{0:T(128)S(1)} %pad_add_fusion.1.place.refs_0_, f32[8]{0:T(128)S(1)} %copy-done.7, f32[8]{0:T(128)S(1)} %copy-done.8, f32[8]{0:T(128)S(1)} %copy-done.9, ...), custom_call_target="tpu_custom_call" | custom-call | flops 4000000000 | bytes 4194304 | tf_op jit(solution)/shard_map/pallas_call | solution.py:451
  15.7 0.4 collective-permute-done.halo
  16.1 1.2 %shard_map.159 = (bf16[4,128,256]{2,1,0:T(8,128)(2,1)S(1)}, f32[2,16,128]{2,1,0:T(8,128)S(1)}, f32[4,16,256]{2,1,0:T(8,128)S(1)}) custom-call(s32[4]{0:T(128)S(1)} %pad_add_fusion.1.place.refs_0_, bf16[2,256,512]{2,1,0:T(8,128)(2,1)S(1)} %fusion.5.qk, bf16[256,1024]{1,0:T(8,128)(2,1)S(1)} %convolution_convert_fusion.1.value, ...), custom_call_target="tpu_custom_call" | custom-call | flops 100000000 | bytes 1048576 | tf_op jit(solution)/shard_map/pallas_call | solution.py:467
  17.3 1.3 %collective-permute-start.1 = (bf16[4,128,256]{2,1,0:T(8,128)(2,1)S(1)}, bf16[4,128,256]{2,1,0:T(8,128)(2,1)S(1)}, u32[]{:S(2)}, u32[]{:S(2)}) collective-permute-start(bf16[4,128,256]{2,1,0:T(8,128)(2,1)S(1)} %get-tuple-element.68.away_maps), channel_id=1, source_target_pairs={{0,4},{4,0},{8,12},{12,8},{16,20},{20,16},{24,28},{28,24},{1,5},{5... | collective-permute-start | bytes 786440 | tf_op jit(solution)/shard_map/ppermute | solution.py:422
  18.5 4.6 %shard_map.160 = (bf16[2,256,128]{2,1,0:T(8,128)(2,1)S(1)}, bf16[4,256,256]{2,1,0:T(8,128)(2,1)S(1)}, f32[4,128,256]{2,1,0:T(8,128)S(1)}, f32[4,256]{1,0:T(4,128)S(1)}, f32[256,128]{1,0:T(8,128)S(1)}) custom-call(s32[4]{0:T(128)S(1)} %pad_add_fusion.1.place.refs_0_, f32[8]{0:T(128)S(1)} %copy-done.7, f32[8]{0:T(128)S(1)} %copy-done.8, f32[8]{0:T(128)S(1)} %copy-done.9, ...), custom_call_target="tpu_custom_call" | custom-call | flops 4000000000 | bytes 4194304 | tf_op jit(solution)/shard_map/pallas_call | solution.py:451
  23.2 1.2 %shard_map.161 = (bf16[4,128,256]{2,1,0:T(8,128)(2,1)S(1)}, f32[2,16,128]{2,1,0:T(8,128)S(1)}, f32[4,16,256]{2,1,0:T(8,128)S(1)}) custom-call(s32[4]{0:T(128)S(1)} %pad_add_fusion.1.place.refs_0_, bf16[2,256,512]{2,1,0:T(8,128)(2,1)S(1)} %fusion.5.qk, bf16[256,1024]{1,0:T(8,128)(2,1)S(1)} %convolution_convert_fusion.1.value, ...), custom_call_target="tpu_custom_call" | custom-call | flops 100000000 | bytes 1048576 | tf_op jit(solution)/shard_map/pallas_call | solution.py:467
  24.4 0.4 collective-permute-done.1.received
  24.8 0.8 %shard_map.162.refs_1_ = bf16[4,128,256]{2,1,0:T(8,128)(2,1)S(1)} custom-call(s32[4]{0:T(128)S(1)} %pad_add_fusion.1.place.refs_0_, bf16[4,128,256]{2,1,0:T(8,128)(2,1)S(1)} %get-tuple-element.76.maps, bf16[4,128,256]{2,1,0:T(8,128)(2,1)S(1)} %collective-permute-done.1.received), custom_call_target="tpu_custom_call" | custom-call | flops 100000000 | bytes 1048576 | tf_op jit(solution)/shard_map/pallas_call | solution.py:513
  25.6 1.6 %collective-permute-start.2 = (bf16[4,128,256]{2,1,0:T(8,128)(2,1)S(1)}, bf16[4,128,256]{2,1,0:T(8,128)(2,1)S(1)}, u32[]{:S(2)}, u32[]{:S(2)}) collective-permute-start(bf16[4,128,256]{2,1,0:T(8,128)(2,1)S(1)} %shard_map.162.refs_1_), channel_id=1, source_target_pairs={{0,8},{4,12},{8,0},{12,4},{16,24},{20,28},{24,16},{28,20},{1,9},{5... | collective-permute-start | bytes 786440 | tf_op jit(solution)/shard_map/ppermute | solution.py:422
  27.2 1.3 %convolution_convert_fusion.gate_z = bf16[256,1024]{1,0:T(8,128)(2,1)S(1)} fusion(bf16[256,2048]{1,0:T(8,128)(2,1)S(1)} %copy-done, bf16[2048,1024]{1,0:T(8,128)(2,1)S(1)} %copy-done.13), kind=kOutput, calls=%fused_computation.3 | convolution fusion | flops 1074003968 | bytes 5767168 | tf_op jit(solution)/shard_map/dot_general | solution.py:519
  28.5 4.2 %collective-permute-done.2.refs_2_ = bf16[4,128,256]{2,1,0:T(8,128)(2,1)S(1)} collective-permute-done((bf16[4,128,256]{2,1,0:T(8,128)(2,1)S(1)}, bf16[4,128,256]{2,1,0:T(8,128)(2,1)S(1)}, u32[]{:S(2)}, u32[]{:S(2)}) %collective-permute-start.2) | collective-permute-done | bytes 262176 | tf_op jit(solution)/shard_map/ppermute | solution.py:422
  32.7 0.9 %shard_map.163 = (bf16[4,128,128]{2,1,0:T(8,128)(2,1)S(1)}, bf16[4,128,256]{2,1,0:T(8,128)(2,1)S(1)}) custom-call(s32[4]{0:T(128)S(1)} %pad_add_fusion.1.place.refs_0_, bf16[4,128,256]{2,1,0:T(8,128)(2,1)S(1)} %shard_map.162.refs_1_, bf16[4,128,256]{2,1,0:T(8,128)(2,1)S(1)} %collective-permute-done.2.refs_2_, f32[8,128,128]{2,1,0:T(8,128)S(1)} %copy-done.2), custom_call_target="tpu_custom_call" | custom-call | flops 100000000 | bytes 1048576 | tf_op jit(solution)/shard_map/pallas_call | solution.py:522
  33.6 2.6 %collective-permute-start.3 = (bf16[4,128,128]{2,1,0:T(8,128)(2,1)S(1)}, bf16[4,128,128]{2,1,0:T(8,128)(2,1)S(1)}, u32[]{:S(2)}, u32[]{:S(2)}) collective-permute-start(bf16[4,128,128]{2,1,0:T(8,128)(2,1)S(1)} %get-tuple-element.81), channel_id=1, source_target_pairs={{0,16},{4,20},{8,24},{12,28},{16,0},{20,4},{24,8},{28,12},{1,17},{... | collective-permute-start | bytes 393224 | tf_op jit(solution)/shard_map/ppermute | solution.py:422
  36.3 2.2 %shard_map.165 = (bf16[4,256,128]{2,1,0:T(8,128)(2,1)S(1)}, f32[4,256,128]{2,1,0:T(8,128)S(1)}, f32[4,256,128]{2,1,0:T(8,128)S(1)}) custom-call(s32[4]{0:T(128)S(1)} %pad_add_fusion.1.place.refs_0_, bf16[2,256,512]{2,1,0:T(8,128)(2,1)S(1)} %fusion.5.qk, bf16[16,2048]{1,0:T(8,128)(2,1)S(1)} %collective-permute-done.halo, bf16[3,2,512]{2,1,0:T(2,128)(2,1)S(1)} %copy-done.6, ...), custom_call_target="tpu_custom_call" | custom-call | flops 2000000000 | bytes 4194304 | tf_op jit(solution)/shard_map/pallas_call | solution.py:485
  38.5 2.4 %shard_map.164 = (bf16[4,256,128]{2,1,0:T(8,128)(2,1)S(1)}, f32[4,256,128]{2,1,0:T(8,128)S(1)}, f32[4,256,128]{2,1,0:T(8,128)S(1)}) custom-call(s32[4]{0:T(128)S(1)} %pad_add_fusion.1.place.refs_0_, bf16[2,256,512]{2,1,0:T(8,128)(2,1)S(1)} %fusion.5.qk, bf16[16,2048]{1,0:T(8,128)(2,1)S(1)} %collective-permute-done.halo, bf16[3,2,512]{2,1,0:T(2,128)(2,1)S(1)} %copy-done.6, ...), custom_call_target="tpu_custom_call" | custom-call | flops 2000000000 | bytes 4194304 | tf_op jit(solution)/shard_map/pallas_call | solution.py:485
  41.0 0.9 %shard_map.166 = (bf16[4,128,128]{2,1,0:T(8,128)(2,1)S(1)}, bf16[4,128,128]{2,1,0:T(8,128)(2,1)S(1)}) custom-call(s32[4]{0:T(128)S(1)} %pad_add_fusion.1.place.refs_0_, bf16[4,128,256]{2,1,0:T(8,128)(2,1)S(1)} %get-tuple-element.80.prefix, f32[8,128,128]{2,1,0:T(8,128)S(1)} %copy-done.2, bf16[4,128,128]{2,1,0:T(8,128)(2,1)S(1)} %collective-permute-done.3.came, ...), custom_call_target="tpu_custom_call" | custom-call | flops 100000000 | bytes 1048576 | tf_op jit(solution)/shard_map/pallas_call | solution.py:535
  41.8 1.4 %collective-permute-start.4 = (bf16[4,128,128]{2,1,0:T(8,128)(2,1)S(1)}, bf16[4,128,128]{2,1,0:T(8,128)(2,1)S(1)}, u32[]{:S(2)}, u32[]{:S(2)}) collective-permute-start(bf16[4,128,128]{2,1,0:T(8,128)(2,1)S(1)} %get-tuple-element.106), channel_id=1, source_target_pairs={{0,4},{4,0},{8,12},{12,8},{16,20},{20,16},{24,28},{28,24},{1,5},{5... | collective-permute-start | bytes 393224 | tf_op jit(solution)/shard_map/ppermute | solution.py:422
  43.3 0.4 shard_map.167.mine_rows
  43.7 3.2 %collective-permute-done.4.states.away_states = bf16[4,128,128]{2,1,0:T(8,128)(2,1)S(1)} collective-permute-done((bf16[4,128,128]{2,1,0:T(8,128)(2,1)S(1)}, bf16[4,128,128]{2,1,0:T(8,128)(2,1)S(1)}, u32[]{:S(2)}, u32[]{:S(2)}) %collective-permute-start.4) | collective-permute-done | bytes 131104 | tf_op jit(solution)/shard_map/ppermute | solution.py:422
  46.9 1.5 %shard_map.168 = (bf16[256,512]{1,0:T(8,128)(2,1)S(1)}, bf16[1,256,512]{2,1,0:T(8,128)(2,1)S(1)}, bf16[1,256,512]{2,1,0:T(8,128)(2,1)S(1)}) custom-call(s32[3]{0:T(128)S(1)} %pad_add_fusion.side, bf16[4,128,128]{2,1,0:T(8,128)(2,1)S(1)} %collective-permute-done.4.states.away_states, bf16[4,256,128]{2,1,0:T(8,128)(2,1)S(1)} %get-tuple-element.107.reads, ...), custom_call_target="tpu_custom_call" | custom-call | flops 1000000000 | bytes 4194304 | tf_op jit(solution)/shard_map/pallas_call | solution.py:550
  48.5 1.5 %collective-permute-done.5 = bf16[1,256,512]{2,1,0:T(8,128)(2,1)S(1)} collective-permute-done((bf16[1,256,512]{2,1,0:T(8,128)(2,1)S(1)}, bf16[1,256,512]{2,1,0:T(8,128)(2,1)S(1)}, u32[]{:S(2)}, u32[]{:S(2)}) %collective-permute-start.5) | collective-permute-done | bytes 262176 | tf_op jit(solution)/shard_map/ppermute | solution.py:422
  50.1 1.6 %collective-permute-start.7 = (bf16[1,256,512]{2,1,0:T(8,128)(2,1)S(1)}, bf16[1,256,512]{2,1,0:T(8,128)(2,1)S(1)}, u32[]{:S(2)}, u32[]{:S(2)}) collective-permute-start(bf16[1,256,512]{2,1,0:T(8,128)(2,1)S(1)} %add_convert_fusion.1), channel_id=1, source_target_pairs={{0,2},{1,3},{2,0},{3,1},{4,6},{5,7},{6,4},{7,5},{8,10},{9,11},{10,... | collective-permute-start | bytes 786440 | tf_op jit(solution)/shard_map/ppermute | solution.py:422
  51.7 2.1 %shard_map.169 = (bf16[1,256,512]{2,1,0:T(8,128)(2,1)S(1)}, bf16[1,256,512]{2,1,0:T(8,128)(2,1)S(1)}, f32[1,8,128,128]{3,2,1,0:T(8,128)}) custom-call(s32[3]{0:T(128)S(1)} %pad_add_fusion.side, bf16[256,512]{1,0:T(8,128)(2,1)S(1)} %shard_map.167.mine_rows, bf16[256,512]{1,0:T(8,128)(2,1)S(1)} %get-tuple-element.113.other_rows, ...), custom_call_target="tpu_custom_call" | custom-call | flops 1000000000 | bytes 4194304 | tf_op jit(solution)/shard_map/pallas_call | solution.py:561
  53.8 4.7 %collective-permute-done.7 = bf16[1,256,512]{2,1,0:T(8,128)(2,1)S(1)} collective-permute-done((bf16[1,256,512]{2,1,0:T(8,128)(2,1)S(1)}, bf16[1,256,512]{2,1,0:T(8,128)(2,1)S(1)}, u32[]{:S(2)}, u32[]{:S(2)}) %collective-permute-start.7) | collective-permute-done | bytes 262176 | tf_op jit(solution)/shard_map/ppermute | solution.py:422
  58.5 0.8 %fusion.10 = bf16[256,512]{1,0:T(8,128)(2,1)} fusion(bf16[1,256,512]{2,1,0:T(8,128)(2,1)S(1)} %collective-permute-done.7, bf16[1,256,512]{2,1,0:T(8,128)(2,1)S(1)} %collective-permute-done.6, bf16[1,256,512]{2,1,0:T(8,128)(2,1)S(1)} %get-tuple-element.114), kind=kLoop, calls=%fused_computation.11 | loop fusion | flops 786432 | bytes 1048576 | tf_op jit(solution)/shard_map/convert_element_type | solution.py:579
  (35 shorter events, 0.4 us)
Async XLA Ops:
  0.6 1.2 %copy-start = (bf16[256,2048]{1,0:T(8,128)(2,1)S(1)}, bf16[256,2048]{1,0:T(8,128)(2,1)}, u32[]{:S(2)}) copy-start(bf16[256,2048]{1,0:T(8,128)(2,1)} %param.15) | copy-start | bytes 3145732
  0.6 5.0 %copy-start.12 = (bf16[2048,1024]{1,0:T(8,128)(2,1)S(1)}, bf16[2048,1024]{1,0:T(8,128)(2,1)}, u32[]{:S(2)}) copy-start(bf16[2048,1024]{1,0:T(8,128)(2,1)} %param.17) | copy-start | bytes 12582916
  5.6 5.0 %copy-start.11 = (bf16[2048,2,8]{0,2,1:T(8,128)(2,1)S(1)}, bf16[2048,2,8]{0,2,1:T(8,128)(2,1)}, u32[]{:S(2)}) copy-start(bf16[2048,2,8]{0,2,1:T(8,128)(2,1)} %param.19) | copy-start | bytes 196612
  5.7 5.4 %copy-start.4 = (bf16[4,1024]{1,0:T(4,128)(2,1)S(1)}, bf16[4,1024]{1,0:T(4,128)(2,1)}, u32[]{:S(2)}) copy-start(bf16[4,1024]{1,0:T(4,128)(2,1)} %conv_value.7) | copy-start | bytes 24580
  5.7 5.4 %copy-start.5 = (bf16[4,2,512]{2,1,0:T(2,128)(2,1)S(1)}, bf16[4,2,512]{2,1,0:T(2,128)(2,1)}, u32[]{:S(2)}) copy-start(bf16[4,2,512]{2,1,0:T(2,128)(2,1)} %conv_qk.11) | copy-start | bytes 24580
  5.7 5.4 %copy-start.7 = (f32[8]{0:T(128)S(1)}, f32[8]{0:T(128)}, u32[]{:S(2)}) copy-start(f32[8]{0:T(128)} %a_log.3) | copy-start | bytes 100
  5.7 5.4 %copy-start.8 = (f32[8]{0:T(128)S(1)}, f32[8]{0:T(128)}, u32[]{:S(2)}) copy-start(f32[8]{0:T(128)} %dt_bias.3) | copy-start | bytes 100
  5.7 5.4 %copy-start.9 = (f32[8]{0:T(128)S(1)}, f32[8]{0:T(128)}, u32[]{:S(2)}) copy-start(f32[8]{0:T(128)} %beta_bias.3) | copy-start | bytes 100
  7.7 8.4 %collective-permute-start = (bf16[16,2048]{1,0:T(8,128)(2,1)}, bf16[16,2048]{1,0:T(8,128)(2,1)S(1)}, u32[]{:S(2)}, u32[]{:S(2)}) collective-permute-start(bf16[16,2048]{1,0:T(8,128)(2,1)} %pad_maximum_fusion), channel_id=1, source_target_pairs={{0,4},{4,8},{8,12},{12,16},{16,20},{20,24},{24,28},{28,0},{1,5},{5... | collective-permute-start | bytes 196616 | tf_op jit(solution)/shard_map/ppermute | solution.py:445
  11.1 5.0 %copy-start.3 = (bf16[3,1024]{1,0:T(4,128)(2,1)S(1)}, bf16[3,1024]{1,0:T(4,128)(2,1)}, u32[]{:S(2)}) copy-start(bf16[3,1024]{1,0:T(4,128)(2,1)} %hist_value.3) | copy-start | bytes 18436
  11.1 5.0 %copy-start.6 = (bf16[3,2,512]{2,1,0:T(2,128)(2,1)S(1)}, bf16[3,2,512]{2,1,0:T(2,128)(2,1)}, u32[]{:S(2)}) copy-start(bf16[3,2,512]{2,1,0:T(2,128)(2,1)} %hist_qk.7) | copy-start | bytes 18436
  17.3 9.9 %copy-start.13 = (bf16[2048,1024]{1,0:T(8,128)(2,1)S(1)}, bf16[2048,1024]{1,0:T(8,128)(2,1)}, u32[]{:S(2)}) copy-start(bf16[2048,1024]{1,0:T(8,128)(2,1)} %param.18) | copy-start | bytes 12582916
  17.3 7.5 %collective-permute-start.1 = (bf16[4,128,256]{2,1,0:T(8,128)(2,1)S(1)}, bf16[4,128,256]{2,1,0:T(8,128)(2,1)S(1)}, u32[]{:S(2)}, u32[]{:S(2)}) collective-permute-start(bf16[4,128,256]{2,1,0:T(8,128)(2,1)S(1)} %get-tuple-element.68.away_maps), channel_id=1, source_target_pairs={{0,4},{4,0},{8,12},{12,8},{16,20},{20,16},{24,28},{28,24},{1,5},{5... | collective-permute-start | bytes 786440 | tf_op jit(solution)/shard_map/ppermute | solution.py:422
  24.3 8.4 %copy-start.2 = (f32[8,128,128]{2,1,0:T(8,128)S(1)}, f32[8,128,128]{2,1,0:T(8,128)}, u32[]{:S(2)}) copy-start(f32[8,128,128]{2,1,0:T(8,128)} %state_in.1) | copy-start | bytes 1572868
  25.5 10.7 %copy-start.10 = (f32[128]{0:T(128)S(1)}, f32[128]{0:T(128)}, u32[]{:S(2)}) copy-start(f32[128]{0:T(128)} %param.28) | copy-start | bytes 1540
  25.6 7.1 %collective-permute-start.2 = (bf16[4,128,256]{2,1,0:T(8,128)(2,1)S(1)}, bf16[4,128,256]{2,1,0:T(8,128)(2,1)S(1)}, u32[]{:S(2)}, u32[]{:S(2)}) collective-permute-start(bf16[4,128,256]{2,1,0:T(8,128)(2,1)S(1)} %shard_map.162.refs_1_), channel_id=1, source_target_pairs={{0,8},{4,12},{8,0},{12,4},{16,24},{20,28},{24,16},{28,20},{1,9},{5... | collective-permute-start | bytes 786440 | tf_op jit(solution)/shard_map/ppermute | solution.py:422
  33.6 7.3 %collective-permute-start.3 = (bf16[4,128,128]{2,1,0:T(8,128)(2,1)S(1)}, bf16[4,128,128]{2,1,0:T(8,128)(2,1)S(1)}, u32[]{:S(2)}, u32[]{:S(2)}) collective-permute-start(bf16[4,128,128]{2,1,0:T(8,128)(2,1)S(1)} %get-tuple-element.81), channel_id=1, source_target_pairs={{0,16},{4,20},{8,24},{12,28},{16,0},{20,4},{24,8},{28,12},{1,17},{... | collective-permute-start | bytes 393224 | tf_op jit(solution)/shard_map/ppermute | solution.py:422
  40.9 6.0 %copy-start.1 = (bf16[1024,2048]{1,0:T(8,128)(2,1)S(1)}, bf16[1024,2048]{1,0:T(8,128)(2,1)}, u32[]{:S(2)}) copy-start(bf16[1024,2048]{1,0:T(8,128)(2,1)} %w_out.3) | copy-start | bytes 12582916
  41.8 5.0 %collective-permute-start.4 = (bf16[4,128,128]{2,1,0:T(8,128)(2,1)S(1)}, bf16[4,128,128]{2,1,0:T(8,128)(2,1)S(1)}, u32[]{:S(2)}, u32[]{:S(2)}) collective-permute-start(bf16[4,128,128]{2,1,0:T(8,128)(2,1)S(1)} %get-tuple-element.106), channel_id=1, source_target_pairs={{0,4},{4,0},{8,12},{12,8},{16,20},{20,16},{24,28},{28,24},{1,5},{5... | collective-permute-start | bytes 393224 | tf_op jit(solution)/shard_map/ppermute | solution.py:422
  48.4 1.6 %collective-permute-start.5 = (bf16[1,256,512]{2,1,0:T(8,128)(2,1)S(1)}, bf16[1,256,512]{2,1,0:T(8,128)(2,1)S(1)}, u32[]{:S(2)}, u32[]{:S(2)}) collective-permute-start(bf16[1,256,512]{2,1,0:T(8,128)(2,1)S(1)} %get-tuple-element.111), channel_id=1, source_target_pairs={{0,1},{1,0},{2,3},{3,2},{4,5},{5,4},{6,7},{7,6},{8,9},{9,8},{10,11... | collective-permute-start | bytes 786440 | tf_op jit(solution)/shard_map/ppermute | solution.py:422
  50.1 8.4 %collective-permute-start.7 = (bf16[1,256,512]{2,1,0:T(8,128)(2,1)S(1)}, bf16[1,256,512]{2,1,0:T(8,128)(2,1)S(1)}, u32[]{:S(2)}, u32[]{:S(2)}) collective-permute-start(bf16[1,256,512]{2,1,0:T(8,128)(2,1)S(1)} %add_convert_fusion.1), channel_id=1, source_target_pairs={{0,2},{1,3},{2,0},{3,1},{4,6},{5,7},{6,4},{7,5},{8,10},{9,11},{10,... | collective-permute-start | bytes 786440 | tf_op jit(solution)/shard_map/ppermute | solution.py:422
  53.8 4.7 %collective-permute-start.6 = (bf16[1,256,512]{2,1,0:T(8,128)(2,1)S(1)}, bf16[1,256,512]{2,1,0:T(8,128)(2,1)S(1)}, u32[]{:S(2)}, u32[]{:S(2)}) collective-permute-start(bf16[1,256,512]{2,1,0:T(8,128)(2,1)S(1)} %get-tuple-element.115), channel_id=1, source_target_pairs={{0,1},{1,0},{2,3},{3,2},{4,5},{5,4},{6,7},{7,6},{8,9},{9,8},{10,11... | collective-permute-start | bytes 786440 | tf_op jit(solution)/shard_map/ppermute | solution.py:422

commit v3 on v2

--- a/solution.py
+++ b/solution.py
@@ -11,6 +11,7 @@
 DV = 128
 HALF = 128
 HALO = 16
+TAIL = 8
 F32 = jnp.float32
 BF16 = jnp.bfloat16
 VMEM = pl.BlockSpec(memory_space=pltpu.VMEM)
@@ -55,16 +56,33 @@
     return silu(total)
 
 
-def call(kernel, out_shape, in_specs, flops, moved, scratch=()):
-    return pl.pallas_call(
-        kernel,
+class Flags:
+    def __init__(self, names, refs):
+        self.refs = dict(zip(names, refs))
+
+    def __getitem__(self, name):
+        return self.refs[name][0]
+
+
+def call(kernel, out_shape, in_specs, flops, moved, scratch=(), flags=None):
+    names = tuple(flags or ())
+
+    def body(*refs):
+        if names:
+            kernel(Flags(names, refs[: len(names)]), *refs[len(names) :])
+        else:
+            kernel(*refs)
+
+    run = pl.pallas_call(
+        body,
         out_shape=out_shape,
-        in_specs=in_specs,
+        in_specs=[SMEM] * len(names) + in_specs,
         out_specs=jax.tree.map(lambda _: VMEM, out_shape),
         scratch_shapes=list(scratch),
         compiler_params=pltpu.CompilerParams(vmem_limit_bytes=12 << 20),
-        cost_estimate=pl.CostEstimate(flops=flops, bytes_accessed=moved, transcendentals=0),
+        cost_estimate=pl.CostEstimate(flops=6 * flops, bytes_accessed=6 * moved, transcendentals=0),
     )
+    return lambda *args: run(*[flags[name] for name in names], *args)
 
 
 def shape(dims, dtype):
@@ -80,12 +98,11 @@
     return jnp.where(flag == 1, values[count:], values[:count])
 
 
-def scalar_column(ref, start, count):
-    index = lax.broadcasted_iota(jnp.int32, (count, 1), 0)
-    column = jnp.zeros((count, 1), F32)
-    for i in range(count):
-        column = jnp.where(index == i, ref[start + i], column)
-    return column
+def as_column(row):
+    count = row.shape[1]
+    line = lax.broadcasted_iota(jnp.int32, (count, count), 0)
+    across = lax.broadcasted_iota(jnp.int32, (count, count), 1)
+    return jnp.sum(jnp.where(line == across, row, 0.0), axis=1, keepdims=True)
 
 
 def load_small(hist_qk, conv_qk, part, hist_s, conv_s):
@@ -96,8 +113,9 @@
 
 
 def front_rows(block, halo, hist, weight, lanes, halo_lanes, first):
-    before = jnp.where(first, hist[:, lanes], halo[:, halo_lanes].astype(F32))
-    return conv_rows(block.astype(F32), before, weight)
+    before = jnp.where(first, hist[HALO - TAIL :, lanes], halo[:, halo_lanes].astype(F32))
+    pad = jnp.zeros((HALO - TAIL, before.shape[1]), F32)
+    return conv_rows(block.astype(F32), jnp.concatenate([pad, before], 0), weight)
 
 
 def running(column, count):
@@ -124,11 +142,11 @@
     zero = jnp.zeros((HALO, KD), F32)
     rest = lax.broadcasted_iota(jnp.int32, (heads, rows), 1) >= taps - 1
     strength = jax.nn.sigmoid(
-        picked(side, gates[0].astype(F32)) + scalar_column(beta_bias, side * heads, heads)
+        picked(side, gates[0].astype(F32)) + picked(side, as_column(beta_bias[...]))
     )
-    decay_in = picked(side, gates[1].astype(F32)) + scalar_column(dt_bias, side * heads, heads)
+    decay_in = picked(side, gates[1].astype(F32)) + picked(side, as_column(dt_bias[...]))
     soft = jnp.maximum(decay_in, 0.0) + jnp.log1p(jnp.exp(-jnp.abs(decay_in)))
-    log_decay = -jnp.exp(scalar_column(a_log, side * heads, heads)) * soft
+    log_decay = -jnp.exp(picked(side, as_column(a_log[...]))) * soft
     raw = [strength, log_decay]
     strength = jnp.where(rest, strength, 0.0)
     log_decay = jnp.where(rest, log_decay, 0.0)
@@ -328,48 +346,85 @@
     return dot(outer[:, :KD], state) + outer[:, KD:].astype(F32)
 
 
+def in_order(bit, mine, other, body):
+    @pl.when(bit == 1)
+    def _():
+        body(other, mine)
+
+    @pl.when(bit == 0)
+    def _():
+        body(mine, other)
+
+
 def pair_kernel(place, maps, received, total_out):
-    bit = place[1]
-    for j in range(received.shape[0]):
-        mine, other = maps[j], received[j]
-        low, high = jnp.where(bit == 1, other, mine), jnp.where(bit == 1, mine, other)
-        total_out[j] = join(high, low).astype(BF16)
+    def body(low, high):
+        for j in range(received.shape[0]):
+            total_out[j] = join(high[j], low[j]).astype(BF16)
+
+    in_order(place[1], maps, received, body)
 
 
 def level_kernel(level, last, *refs):
     if level == 1:
         place, total, received, state_in, total_out, prefix_out = refs
+        prefix = None
     else:
         place, total, received, prefix, state_in, total_out, prefix_out = refs
+    half = total.shape[0]
     bit = place[level + 1]
-    half = total.shape[0]
-    line = lax.broadcasted_iota(jnp.int32, (KD, KD + DV), 0)
-    across = lax.broadcasted_iota(jnp.int32, (KD, KD + DV), 1)
-    same = jnp.where(line == across, 1.0, 0.0).astype(BF16)
-    for j in range(half):
-        mine, other = total[j], received[j]
-        low, high = jnp.where(bit == 1, other, mine), jnp.where(bit == 1, mine, other)
-        if level == 1:
-            prefix_out[j] = jnp.where(bit == 1, low, same)
-        else:
-            prefix_out[j] = jnp.where(bit == 1, join(prefix[j], low).astype(BF16), prefix[j])
-        if last:
-            state = state_in[place[1] * half + j].astype(BF16)
-            total_out[j] = act(high, act(low, state).astype(BF16)).astype(BF16)
-        else:
-            total_out[j] = join(high, low).astype(BF16)
+
+    def body(low, high):
+        for j in range(half):
+            if last:
+                state = state_in[place[1] * half + j].astype(BF16)
+                total_out[j] = act(high[j], act(low[j], state).astype(BF16)).astype(BF16)
+            else:
+                total_out[j] = join(high[j], low[j]).astype(BF16)
+
+    in_order(bit, total, received, body)
+
+    @pl.when(bit == 1)
+    def _():
+        for j in range(half):
+            if prefix is None:
+                prefix_out[j] = received[j]
+            else:
+                prefix_out[j] = join(prefix[j], received[j]).astype(BF16)
+
+    @pl.when(bit == 0)
+    def _():
+        line = lax.broadcasted_iota(jnp.int32, (KD, KD + DV), 0)
+        across = lax.broadcasted_iota(jnp.int32, (KD, KD + DV), 1)
+        same = jnp.where(line == across, 1.0, 0.0).astype(BF16)
+        for j in range(half):
+            prefix_out[j] = same if prefix is None else prefix[j]
 
 
 def enter_kernel(top, place, prefix, state_in, came, maps, received, mine_out, send_out):
     bit = place[1]
     half = prefix.shape[0]
-    for j in range(half):
-        start = jnp.where(place[top + 1] == 1, came[j], state_in[bit * half + j].astype(BF16))
-        entering = act(prefix[j], start).astype(BF16)
-        low = jnp.where(bit == 1, received[j], maps[j])
-        passed = act(low, entering).astype(BF16)
-        mine_out[j] = jnp.where(bit == 1, passed, entering)
-        send_out[j] = jnp.where(bit == 1, entering, passed)
+
+    @pl.when(place[top + 1] == 1)
+    def _():
+        for j in range(half):
+            mine_out[j] = act(prefix[j], came[j]).astype(BF16)
+
+    @pl.when(place[top + 1] == 0)
+    def _():
+        for j in range(half):
+            mine_out[j] = act(prefix[j], state_in[bit * half + j].astype(BF16)).astype(BF16)
+
+    @pl.when(bit == 1)
+    def _():
+        for j in range(half):
+            entering = mine_out[j]
+            send_out[j] = entering
+            mine_out[j] = act(received[j], entering).astype(BF16)
+
+    @pl.when(bit == 0)
+    def _():
+        for j in range(half):
+            send_out[j] = act(maps[j], mine_out[j]).astype(BF16)
 
 
 def normed_rows(local_part, reads, gate, state):
@@ -378,38 +433,71 @@
     return (out * scale * gate).astype(BF16)
 
 
-def project(side, mine_rows, other_rows, w_out, away, send_out, keep_out):
+def project(side, rows_in, own, w_out, away, emit):
     core, bit, lift = side[0], side[1], side[2]
     depth = w_out.shape[0] // 2
-    width = send_out.shape[2]
-    for j in range(send_out.shape[0]):
+    member = bit if own else 1 - bit
+    width = w_out.shape[1] // emit.count
+    for j in range(emit.count // 4):
         block = 2 * j + (1 - lift if away else lift)
-        for member, ref in ((1 - core, send_out), (core, keep_out)):
-            lanes = lane_block(2 * block + member, width)
-            own = w_out[pl.ds(pl.multiple_of(bit * depth, depth), depth), lanes]
-            other = w_out[pl.ds(pl.multiple_of((1 - bit) * depth, depth), depth), lanes]
-            ref[j] = (dot(mine_rows[...], own) + dot(other_rows[...], other)).astype(BF16)
-
-
-def normed_kernel(states, reads, local_reads, gate, normed_out):
+        for target, column in ((0, 1 - core), (1, core)):
+            lanes = lane_block(2 * block + column, width)
+            rows_of = pl.ds(pl.multiple_of(member * depth, depth), depth)
+            emit(target, j, dot(rows_in[...], w_out[rows_of, lanes]))
+
+
+class Emit:
+    def __init__(self, count, store):
+        self.count, self.store = count, store
+
+    def __call__(self, target, j, product):
+        self.store(target, j, product)
+
+
+def normed_all(states, reads, local_reads, gate, normed_out):
     for j in range(states.shape[0]):
         normed_out[:, j * DV : (j + 1) * DV] = normed_rows(
             local_reads[j], reads[j], gate[j], states[j]
         )
 
 
+def own_kernel(side, states, reads, local_reads, gate, w_out, normed_out, far_out):
+    normed_all(states, reads, local_reads, gate, normed_out)
+    count = w_out.shape[1] // far_out.shape[3]
+
+    def store(target, j, product):
+        far_out[target, j] = product
+
+    project(side, normed_out, True, w_out, True, Emit(count, store))
+
+
 def away_kernel(
-    side, states, reads, local_reads, gate, mine_rows, w_out, other_rows, send_out, keep_out
+    side, states, reads, local_reads, gate, far, w_out, other_rows, send_out, keep_out
 ):
-    normed_kernel(states, reads, local_reads, gate, other_rows)
-    project(side, mine_rows, other_rows, w_out, True, send_out, keep_out)
+    normed_all(states, reads, local_reads, gate, other_rows)
+    count = w_out.shape[1] // send_out.shape[2]
+
+    def store(target, j, product):
+        (send_out, keep_out)[target][j] = (far[target, j] + product).astype(BF16)
+
+    project(side, other_rows, False, w_out, True, Emit(count, store))
 
 
 def home_kernel(
     side, mine_rows, other_rows, w_out, maps, states, away_maps, away_states,
     send_out, keep_out, checkpoint,
 ):
-    project(side, mine_rows, other_rows, w_out, False, send_out, keep_out)
+    count = w_out.shape[1] // send_out.shape[2]
+    sums = {}
+
+    def store_own(target, j, product):
+        sums[target, j] = product
+
+    def store(target, j, product):
+        (send_out, keep_out)[target][j] = (sums[target, j] + product).astype(BF16)
+
+    project(side, mine_rows, True, w_out, False, Emit(count, store_own))
+    project(side, other_rows, False, w_out, False, Emit(count, store))
     bit = side[1]
     half = maps.shape[0]
     for j in range(half):
@@ -436,11 +524,19 @@
     levels = n_seq.bit_length() - 1
     seq = lax.axis_index("seq")
     col = lax.axis_index("head")
-    place = jnp.stack([seq] + [(seq >> level) & 1 for level in range(levels)]).astype(jnp.int32)
+
+    def scalar(value):
+        return value.astype(jnp.int32).reshape(1)
+
+    place = {0: scalar(seq)} | {i + 1: scalar((seq >> i) & 1) for i in range(levels)}
+
+    def only(*names):
+        return {name: place[name] for name in names}
+
 
     qk = jnp.einsum("td,dce->cte", hidden_in, w_qk, preferred_element_type=F32).astype(BF16)
     value = jnp.dot(hidden_in, w_value, preferred_element_type=F32).astype(BF16)
-    tail = rows - HALO
+    tail = rows - TAIL
     ends = jnp.concatenate([qk[0, tail:], qk[1, tail:], value[tail:]], 1)
     halo = lax.ppermute(ends, "seq", [(i, (i + 1) % n_seq) for i in range(n_seq)])
     gates = jnp.einsum("td,dch->cht", hidden_in, w_ba, preferred_element_type=F32).astype(BF16)
@@ -457,11 +553,15 @@
                 shape((half, rows), F32),
                 shape((rows, 128), F32),
             ),
-            [SMEM] * 4 + [VMEM] * 5,
+            [VMEM] * 8,
             4 * 10**9,
             4 << 20,
             small[1:],
-        )(place, a_log, dt_bias, beta_bias, qk, value, gates, conv_qk, conv_value)
+            only(1),
+        )(
+            a_log.reshape(1, heads), dt_bias.reshape(1, heads), beta_bias.reshape(1, heads),
+            qk, value, gates, conv_qk, conv_value,
+        )
 
     def front(own, prepared):
         return call(
@@ -471,12 +571,13 @@
                 shape((half // 2, HALO, KD), F32),
                 shape((half, HALO, KD + DV), F32),
             ),
-            [SMEM] + [VMEM] * 9,
+            [VMEM] * 9,
             10**8,
             1 << 20,
             small + [pltpu.VMEM((HALO, heads * DV), F32)],
+            only(0, 1),
         )(
-            place, qk, value, halo, hist_qk, hist_value, conv_qk, conv_value,
+            qk, value, halo, hist_qk, hist_value, conv_qk, conv_value,
             prepared[2], prepared[4],
         )
 
@@ -489,12 +590,13 @@
                 shape((half, rows, DV), F32),
                 shape((half, rows, DV), F32),
             ),
-            [SMEM] + [VMEM] * 12,
+            [VMEM] * 12,
             2 * 10**9,
             4 << 20,
             small,
+            only(0, 1),
         )(
-            place, qk, halo, hist_qk, conv_qk, keys, solved, cumul, cols, fronted[1], fronted[2],
+            qk, halo, hist_qk, conv_qk, keys, solved, cumul, cols, fronted[1], fronted[2],
             gate_z, norm_gain.reshape(1, DV),
         )
 
@@ -510,7 +612,9 @@
 
     map_shape = shape((half, KD, KD + DV), BF16)
     state_shape = shape((half, KD, DV), BF16)
-    total = call(pair_kernel, map_shape, [SMEM, VMEM, VMEM], 10**8, 1 << 20)(place, maps, received)
+    total = call(
+        pair_kernel, map_shape, [VMEM, VMEM], 10**8, 1 << 20, flags=only(1)
+    )(maps, received)
     prefix = ()
     for level in range(1, levels - 1):
         other = swapped(total, "seq", 1 << level)
@@ -522,10 +626,11 @@
         total, prefix = call(
             functools.partial(level_kernel, level, last),
             (state_shape if last else map_shape, map_shape),
-            [SMEM] + [VMEM] * (3 if level == 1 else 4),
+            [VMEM] * (3 if level == 1 else 4),
             10**8,
             1 << 20,
-        )(place, total, other, *prefix, state_in)
+            flags=only(1, level + 1),
+        )(total, other, *prefix, state_in)
         prefix = (prefix,)
     came = swapped(total, "seq", 1 << (levels - 1))
     later, _ = lax.optimization_barrier((qk, total))
@@ -535,25 +640,34 @@
     mine, send_state = call(
         functools.partial(enter_kernel, levels - 1),
         (state_shape, state_shape),
-        [SMEM] + [VMEM] * 5,
+        [VMEM] * 5,
         10**8,
         1 << 20,
-    )(place, prefix[0], state_in, came, maps, received)
+        flags=only(1, levels),
+    )(prefix[0], state_in, came, maps, received)
     other_state = swapped(send_state, "seq", 1)
 
     out_width = w_out.shape[1] // n_head
     blocks = n_head // 4
-    side = jnp.stack([col & 1, place[1], (col >> 1) & 1]).astype(jnp.int32)
+    side = {0: scalar(col & 1), 1: place[1], 2: scalar((col >> 1) & 1)}
     part_shape = shape((blocks, rows, out_width), BF16)
     rows_shape = shape((rows, half * DV), BF16)
-    own_rows = call(normed_kernel, rows_shape, [VMEM] * 4, 10**9, 4 << 20)(mine, *own_reads)
+    own_rows, far = call(
+        own_kernel,
+        (rows_shape, shape((2, blocks, rows, out_width), F32)),
+        [VMEM] * 5,
+        10**9,
+        4 << 20,
+        flags=side,
+    )(mine, *own_reads, w_out)
     other_rows, send_out, keep = call(
         away_kernel,
         (rows_shape, part_shape, part_shape),
-        [SMEM] + [VMEM] * 6,
+        [VMEM] * 6,
         10**9,
         4 << 20,
-    )(side, other_state, *away_reads, own_rows, w_out)
+        flags=side,
+    )(other_state, *away_reads, far, w_out)
     came_out = swapped(send_out, "head", 1)
     total_out = (keep.astype(F32) + came_out.astype(F32)).astype(BF16)
     total_out, other_rows = lax.optimization_barrier((total_out, other_rows))
@@ -561,10 +675,11 @@
     send_out, keep, checkpoint = call(
         home_kernel,
         (part_shape, part_shape, shape((1, heads, KD, DV), F32)),
-        [SMEM] + [VMEM] * 7,
+        [VMEM] * 7,
         10**9,
         4 << 20,
-    )(side, own_rows, other_rows, w_out, maps, mine, away_maps, other_state)
+        flags=side,
+    )(own_rows, other_rows, w_out, maps, mine, away_maps, other_state)
     came_out = swapped(send_out, "head", 1)
     mixed = keep.astype(F32) + came_out.astype(F32) + came_far.astype(F32)
     step = 4

time: 59.5 us -> 57.2 us (0.961)
  Pallas kernels: 22.7 us -> 17.3 us
  waiting for transfers between devices: 14.5 us -> 17.5 us
  starting transfers between devices: 11.5 us -> 12.4 us
  other arithmetic: 1.67 us -> 0.87 us
    pallas_call x12, Pallas kernels: 22.7 us -> 17.3 us  [call(): return lambda *args: run(*[flags[name] for name in names], *args)]
    ppermute x7, waiting for transfers between devices: 14.1 us -> 17.3 us  [swapped(): return lax.ppermute(value, axis, [(i, i ^ step) for i in range(count)])]
    ppermute x7, starting transfers between devices: 8.56 us -> 9.44 us  [swapped(): return lax.ppermute(value, axis, [(i, i ^ step) for i in range(count)])]
    concatenate x1, other arithmetic: 0.64 us -> 0.01 us  [local(): ends = jnp.concatenate([qk[0, tail:], qk[1, tail:], value[tail:]], 1)]
  transfers between devices with their start and end apart: 8 -> 8, of which waited for: 7 -> 7; matrix products, arithmetic and copies ran while one was open for 3% -> 3% of each run, Pallas kernels for 29% -> 23%
where the time goes in v3:
time: 57.2 us; the launch traced here: 57.1 us
  waiting for transfers between devices  17.5 us (31%)
  Pallas kernels  17.3 us (30%)
  starting transfers between devices  12.4 us (22%)
  matrix products  6.72 us (12%)
  local copies, waits for them, and re-layouts  1.31 us (2%)
  between operations  0.93 us (2%)
  other arithmetic  0.87 us (2%)
    ppermute x7, waiting for transfers between devices, swapped(): return lax.ppermute(value, axis, [(i, i ^ step) for i in range(count)])  17.3 us
    pallas_call x12, Pallas kernels, call(): return lambda *args: run(*[flags[name] for name in names], *args)  17.3 us
    ppermute x7, starting transfers between devices, swapped(): return lax.ppermute(value, axis, [(i, i ^ step) for i in range(count)])  9.44 us
    dot_general x1, matrix products, local(): jnp.einsum('td,dce->cte', hidden_in, w_qk, preferred_element_type=F32)  3.77 us
    ppermute x1, starting transfers between devices, local(): lax.ppermute(ends, 'seq', [(i, (i + 1) % n_seq) for i in range(n_seq)])  2.99 us
    unnamed x28, local copies, waits for them, and re-layouts  1.3 us
    dot_general x1, matrix products, local(): gate_z = jnp.dot(later, w_outgate, preferred_element_type=F32).astype(BF16)  1.29 us
    dot_general x1, matrix products, local(): value = jnp.dot(hidden_in, w_value, preferred_element_type=F32).astype(BF16)  1.28 us
  transfers between devices with their start and end apart: 8, of which 7 were waited for; matrix products, arithmetic and copies ran while one was open for 3% of the time, Pallas kernels for 23%

profile of v3, /device:TPU:0, one launch (start us, length us, event | category | flops | bytes accessed | tf_op | source)
XLA Modules:
  0.0 57.1 jit_solution(10726705348553471722)
XLA Ops:
  0.7 1.2 %copy-done = bf16[256,2048]{1,0:T(8,128)(2,1)S(1)} copy-done((bf16[256,2048]{1,0:T(8,128)(2,1)S(1)}, bf16[256,2048]{1,0:T(8,128)(2,1)}, u32[]{:S(2)}) %copy-start) | copy-done | bytes 1048600
  1.9 3.8 %fusion.5.refs_4_.refs_2_ = bf16[2,256,512]{2,1,0:T(8,128)(2,1)S(1)} fusion(bf16[2048,2,512]{2,1,0:T(2,128)(2,1)} %param.16, bf16[256,2048]{1,0:T(8,128)(2,1)S(1)} %copy-done), kind=kOutput, calls=%fused_computation.5 | convolution fusion | flops 1074003968 | bytes 5767168 | tf_op jit(solution)/shard_map/td,dce->cte/dot_general | solution.py:537
  5.7 1.3 %convolution_convert_fusion.1.refs_5_.refs_3_ = bf16[256,1024]{1,0:T(8,128)(2,1)S(1)} fusion(bf16[256,2048]{1,0:T(8,128)(2,1)S(1)} %copy-done, bf16[2048,1024]{1,0:T(8,128)(2,1)S(1)} %copy-done.12), kind=kOutput, calls=%fused_computation.4 | convolution fusion | flops 1074003968 | bytes 5767168 | tf_op jit(solution)/shard_map/dot_general | solution.py:538
  7.0 3.0 %collective-permute-start = (bf16[8,2048]{1,0:T(8,128)(2,1)S(1)}, bf16[8,2048]{1,0:T(8,128)(2,1)S(1)}, u32[]{:S(2)}, u32[]{:S(2)}) collective-permute-start(bf16[8,2048]{1,0:T(8,128)(2,1)S(1)} %pad_maximum_fusion), channel_id=1, source_target_pairs={{0,4},{4,8},{8,12},{12,16},{16,20},{20,24},{24,28},{28,0},{1,5},{5... | collective-permute-start | bytes 98312 | tf_op jit(solution)/shard_map/ppermute | solution.py:541
  10.0 0.4 convolution_convert_fusion.2.refs_6_
  10.5 4.3 %shard_map.158 = (bf16[2,256,128]{2,1,0:T(8,128)(2,1)S(1)}, bf16[4,256,256]{2,1,0:T(8,128)(2,1)S(1)}, f32[4,128,256]{2,1,0:T(8,128)S(1)}, f32[4,256]{1,0:T(4,128)S(1)}, f32[256,128]{1,0:T(8,128)S(1)}) custom-call(s32[1]{0:T(128)} %bitcast.1.refs_0_.refs_1_, f32[1,8]{1,0:T(1,128)S(1)} %bitcast.28, f32[1,8]{1,0:T(1,128)S(1)} %bitcast.30, f32[1,8]{1,0:T(1,128)S(1)} %bitcast.32, ...), custom_call_target="tpu_custom_call" | custom-call | flops 24000000000 | bytes 25165824 | tf_op jit(solution)/shard_map/pallas_call | solution.py:85
  14.8 0.2 collective-permute-done.refs_4_.refs_3_
  15.0 0.6 %shard_map.159 = (bf16[4,128,256]{2,1,0:T(8,128)(2,1)S(1)}, f32[2,16,128]{2,1,0:T(8,128)S(1)}, f32[4,16,256]{2,1,0:T(8,128)S(1)}) custom-call(s32[1]{0:T(128)} %bitcast.5.refs_0_, s32[1]{0:T(128)} %bitcast.1.refs_0_.refs_1_, bf16[2,256,512]{2,1,0:T(8,128)(2,1)S(1)} %fusion.5.refs_4_.refs_2_, bf16[256,1024]{1,0:T(8,128)(2,1)S(1)} %convolution_convert_fusion.1.refs_5_.refs_3_, ...), custom_call_target="tpu_custom_call" | custom-call | flops 600000000 | bytes 6291456 | tf_op jit(solution)/shard_map/pallas_call | solution.py:85
  15.6 1.5 %collective-permute-start.1 = (bf16[4,128,256]{2,1,0:T(8,128)(2,1)S(1)}, bf16[4,128,256]{2,1,0:T(8,128)(2,1)S(1)}, u32[]{:S(2)}, u32[]{:S(2)}) collective-permute-start(bf16[4,128,256]{2,1,0:T(8,128)(2,1)S(1)} %get-tuple-element.70.refs_8_), channel_id=1, source_target_pairs={{0,4},{4,0},{8,12},{12,8},{16,20},{20,16},{24,28},{28,24},{1,5},{5... | collective-permute-start | bytes 786440 | tf_op jit(solution)/shard_map/ppermute | solution.py:510
  17.1 4.3 %shard_map.160 = (bf16[2,256,128]{2,1,0:T(8,128)(2,1)S(1)}, bf16[4,256,256]{2,1,0:T(8,128)(2,1)S(1)}, f32[4,128,256]{2,1,0:T(8,128)S(1)}, f32[4,256]{1,0:T(4,128)S(1)}, f32[256,128]{1,0:T(8,128)S(1)}) custom-call(s32[1]{0:T(128)} %bitcast.1.refs_0_.refs_1_, f32[1,8]{1,0:T(1,128)S(1)} %bitcast.29, f32[1,8]{1,0:T(1,128)S(1)} %bitcast.31, f32[1,8]{1,0:T(1,128)S(1)} %bitcast.33, ...), custom_call_target="tpu_custom_call" | custom-call | flops 24000000000 | bytes 25165824 | tf_op jit(solution)/shard_map/pallas_call | solution.py:85
  21.4 0.6 %shard_map.161 = (bf16[4,128,256]{2,1,0:T(8,128)(2,1)S(1)}, f32[2,16,128]{2,1,0:T(8,128)S(1)}, f32[4,16,256]{2,1,0:T(8,128)S(1)}) custom-call(s32[1]{0:T(128)} %bitcast.5.refs_0_, s32[1]{0:T(128)} %bitcast.1.refs_0_.refs_1_, bf16[2,256,512]{2,1,0:T(8,128)(2,1)S(1)} %fusion.5.refs_4_.refs_2_, bf16[256,1024]{1,0:T(8,128)(2,1)S(1)} %convolution_convert_fusion.1.refs_5_.refs_3_, ...), custom_call_target="tpu_custom_call" | custom-call | flops 600000000 | bytes 6291456 | tf_op jit(solution)/shard_map/pallas_call | solution.py:85
  22.0 1.3 %collective-permute-done.1.refs_2_.refs_6_ = bf16[4,128,256]{2,1,0:T(8,128)(2,1)S(1)} collective-permute-done((bf16[4,128,256]{2,1,0:T(8,128)(2,1)S(1)}, bf16[4,128,256]{2,1,0:T(8,128)(2,1)S(1)}, u32[]{:S(2)}, u32[]{:S(2)}) %collective-permute-start.1) | collective-permute-done | bytes 262176 | tf_op jit(solution)/shard_map/ppermute | solution.py:510
  23.3 0.2 shard_map.162.refs_2_
  23.5 1.6 %collective-permute-start.2 = (bf16[4,128,256]{2,1,0:T(8,128)(2,1)S(1)}, bf16[4,128,256]{2,1,0:T(8,128)(2,1)S(1)}, u32[]{:S(2)}, u32[]{:S(2)}) collective-permute-start(bf16[4,128,256]{2,1,0:T(8,128)(2,1)S(1)} %shard_map.162.refs_2_), channel_id=1, source_target_pairs={{0,8},{4,12},{8,0},{12,4},{16,24},{20,28},{24,16},{28,20},{1,9},{5... | collective-permute-start | bytes 786440 | tf_op jit(solution)/shard_map/ppermute | solution.py:510
  25.2 1.3 %convolution_convert_fusion.refs_12_ = bf16[256,1024]{1,0:T(8,128)(2,1)S(1)} fusion(bf16[256,2048]{1,0:T(8,128)(2,1)S(1)} %copy-done, bf16[2048,1024]{1,0:T(8,128)(2,1)S(1)} %copy-done.13), kind=kOutput, calls=%fused_computation.3 | convolution fusion | flops 1074003968 | bytes 5767168 | tf_op jit(solution)/shard_map/dot_general | solution.py:623
  26.5 3.8 %collective-permute-done.2.refs_3_ = bf16[4,128,256]{2,1,0:T(8,128)(2,1)S(1)} collective-permute-done((bf16[4,128,256]{2,1,0:T(8,128)(2,1)S(1)}, bf16[4,128,256]{2,1,0:T(8,128)(2,1)S(1)}, u32[]{:S(2)}, u32[]{:S(2)}) %collective-permute-start.2) | collective-permute-done | bytes 262176 | tf_op jit(solution)/shard_map/ppermute | solution.py:510
  30.3 0.5 shard_map.163
  30.8 2.8 %collective-permute-start.3 = (bf16[4,128,128]{2,1,0:T(8,128)(2,1)S(1)}, bf16[4,128,128]{2,1,0:T(8,128)(2,1)S(1)}, u32[]{:S(2)}, u32[]{:S(2)}) collective-permute-start(bf16[4,128,128]{2,1,0:T(8,128)(2,1)S(1)} %get-tuple-element.83), channel_id=1, source_target_pairs={{0,16},{4,20},{8,24},{12,28},{16,0},{20,4},{24,8},{28,12},{1,17},{... | collective-permute-start | bytes 393224 | tf_op jit(solution)/shard_map/ppermute | solution.py:510
  33.7 1.7 %shard_map.165 = (bf16[4,256,128]{2,1,0:T(8,128)(2,1)S(1)}, f32[4,256,128]{2,1,0:T(8,128)S(1)}, f32[4,256,128]{2,1,0:T(8,128)S(1)}) custom-call(s32[1]{0:T(128)} %bitcast.5.refs_0_, s32[1]{0:T(128)} %bitcast.1.refs_0_.refs_1_, bf16[2,256,512]{2,1,0:T(8,128)(2,1)S(1)} %fusion.5.refs_4_.refs_2_, bf16[8,2048]{1,0:T(8,128)(2,1)S(1)} %collective-permute-done.refs_4_.refs_3_, ...), custom_call_target="tpu_custom_call" | custom-call | flops 12000000000 | bytes 25165824 | tf_op jit(solution)/shard_map/pallas_call | solution.py:85
  35.4 1.7 %shard_map.164 = (bf16[4,256,128]{2,1,0:T(8,128)(2,1)S(1)}, f32[4,256,128]{2,1,0:T(8,128)S(1)}, f32[4,256,128]{2,1,0:T(8,128)S(1)}) custom-call(s32[1]{0:T(128)} %bitcast.5.refs_0_, s32[1]{0:T(128)} %bitcast.1.refs_0_.refs_1_, bf16[2,256,512]{2,1,0:T(8,128)(2,1)S(1)} %fusion.5.refs_4_.refs_2_, bf16[8,2048]{1,0:T(8,128)(2,1)S(1)} %collective-permute-done.refs_4_.refs_3_, ...), custom_call_target="tpu_custom_call" | custom-call | flops 12000000000 | bytes 25165824 | tf_op jit(solution)/shard_map/pallas_call | solution.py:85
  37.1 1.1 %collective-permute-done.3.refs_4_ = bf16[4,128,128]{2,1,0:T(8,128)(2,1)S(1)} collective-permute-done((bf16[4,128,128]{2,1,0:T(8,128)(2,1)S(1)}, bf16[4,128,128]{2,1,0:T(8,128)(2,1)S(1)}, u32[]{:S(2)}, u32[]{:S(2)}) %collective-permute-start.3) | collective-permute-done | bytes 131104 | tf_op jit(solution)/shard_map/ppermute | solution.py:510
  38.2 0.4 shard_map.166
  38.5 1.8 %collective-permute-start.4 = (bf16[4,128,128]{2,1,0:T(8,128)(2,1)S(1)}, bf16[4,128,128]{2,1,0:T(8,128)(2,1)S(1)}, u32[]{:S(2)}, u32[]{:S(2)}) collective-permute-start(bf16[4,128,128]{2,1,0:T(8,128)(2,1)S(1)} %get-tuple-element.109), channel_id=1, source_target_pairs={{0,4},{4,0},{8,12},{12,8},{16,20},{20,16},{24,28},{28,24},{1,5},{5... | collective-permute-start | bytes 393224 | tf_op jit(solution)/shard_map/ppermute | solution.py:510
  40.3 0.7 %shard_map.167 = (bf16[256,512]{1,0:T(8,128)(2,1)S(1)}, f32[2,1,256,512]{3,2,1,0:T(8,128)S(1)}) custom-call(s32[1]{0:T(128)} %bitcast.refs_0_, s32[1]{0:T(128)} %bitcast.1.refs_0_.refs_1_, s32[1]{0:T(128)} %bitcast.2.refs_2_, bf16[4,128,128]{2,1,0:T(8,128)(2,1)S(1)} %get-tuple-element.104.refs_3_.refs_7_, ...), custom_call_target="tpu_custom_call" | custom-call | flops 6000000000 | bytes 25165824 | tf_op jit(solution)/shard_map/pallas_call | solution.py:85
  41.0 2.5 %collective-permute-done.4.refs_3_.refs_9_ = bf16[4,128,128]{2,1,0:T(8,128)(2,1)S(1)} collective-permute-done((bf16[4,128,128]{2,1,0:T(8,128)(2,1)S(1)}, bf16[4,128,128]{2,1,0:T(8,128)(2,1)S(1)}, u32[]{:S(2)}, u32[]{:S(2)}) %collective-permute-start.4) | collective-permute-done | bytes 131104 | tf_op jit(solution)/shard_map/ppermute | solution.py:510
  43.6 0.7 %shard_map.168 = (bf16[256,512]{1,0:T(8,128)(2,1)S(1)}, bf16[1,256,512]{2,1,0:T(8,128)(2,1)S(1)}, bf16[1,256,512]{2,1,0:T(8,128)(2,1)S(1)}) custom-call(s32[1]{0:T(128)} %bitcast.refs_0_, s32[1]{0:T(128)} %bitcast.1.refs_0_.refs_1_, s32[1]{0:T(128)} %bitcast.2.refs_2_, bf16[4,128,128]{2,1,0:T(8,128)(2,1)S(1)} %collective-permute-done.4.refs_3_.refs_9_, ...), custom_call_target="tpu_custom_call" | custom-call | flops 6000000000 | bytes 25165824 | tf_op jit(solution)/shard_map/pallas_call | solution.py:85
  44.4 1.5 %collective-permute-done.5 = bf16[1,256,512]{2,1,0:T(8,128)(2,1)S(1)} collective-permute-done((bf16[1,256,512]{2,1,0:T(8,128)(2,1)S(1)}, bf16[1,256,512]{2,1,0:T(8,128)(2,1)S(1)}, u32[]{:S(2)}, u32[]{:S(2)}) %collective-permute-start.5) | collective-permute-done | bytes 262176 | tf_op jit(solution)/shard_map/ppermute | solution.py:510
  46.0 1.6 %shard_map.169 = (bf16[1,256,512]{2,1,0:T(8,128)(2,1)S(1)}, bf16[1,256,512]{2,1,0:T(8,128)(2,1)S(1)}, f32[1,8,128,128]{3,2,1,0:T(8,128)}) custom-call(s32[1]{0:T(128)} %bitcast.refs_0_, s32[1]{0:T(128)} %bitcast.1.refs_0_.refs_1_, s32[1]{0:T(128)} %bitcast.2.refs_2_, bf16[256,512]{1,0:T(8,128)(2,1)S(1)} %get-tuple-element.108.refs_3_, ...), custom_call_target="tpu_custom_call" | custom-call | flops 6000000000 | bytes 25165824 | tf_op jit(solution)/shard_map/pallas_call | solution.py:85
  47.6 0.1 collective-permute-start.6
  47.7 1.5 %collective-permute-start.7 = (bf16[1,256,512]{2,1,0:T(8,128)(2,1)S(1)}, bf16[1,256,512]{2,1,0:T(8,128)(2,1)S(1)}, u32[]{:S(2)}, u32[]{:S(2)}) collective-permute-start(bf16[1,256,512]{2,1,0:T(8,128)(2,1)S(1)} %add_convert_fusion.1), channel_id=1, source_target_pairs={{0,2},{1,3},{2,0},{3,1},{4,6},{5,7},{6,4},{7,5},{8,10},{9,11},{10,... | collective-permute-start | bytes 786440 | tf_op jit(solution)/shard_map/ppermute | solution.py:510
  49.2 7.1 %collective-permute-done.7 = bf16[1,256,512]{2,1,0:T(8,128)(2,1)S(1)} collective-permute-done((bf16[1,256,512]{2,1,0:T(8,128)(2,1)S(1)}, bf16[1,256,512]{2,1,0:T(8,128)(2,1)S(1)}, u32[]{:S(2)}, u32[]{:S(2)}) %collective-permute-start.7) | collective-permute-done | bytes 262176 | tf_op jit(solution)/shard_map/ppermute | solution.py:510
  56.3 0.8 %fusion.10 = bf16[256,512]{1,0:T(8,128)(2,1)} fusion(bf16[1,256,512]{2,1,0:T(8,128)(2,1)S(1)} %collective-permute-done.7, bf16[1,256,512]{2,1,0:T(8,128)(2,1)S(1)} %collective-permute-done.6, bf16[1,256,512]{2,1,0:T(8,128)(2,1)S(1)} %get-tuple-element.118), kind=kLoop, calls=%fused_computation.11 | loop fusion | flops 786432 | bytes 1048576 | tf_op jit(solution)/shard_map/convert_element_type | solution.py:694
  (33 shorter events, 0.2 us)
Async XLA Ops:
  0.6 1.2 %copy-start = (bf16[256,2048]{1,0:T(8,128)(2,1)S(1)}, bf16[256,2048]{1,0:T(8,128)(2,1)}, u32[]{:S(2)}) copy-start(bf16[256,2048]{1,0:T(8,128)(2,1)} %param.15) | copy-start | bytes 3145732
  0.6 5.0 %copy-start.12 = (bf16[2048,1024]{1,0:T(8,128)(2,1)S(1)}, bf16[2048,1024]{1,0:T(8,128)(2,1)}, u32[]{:S(2)}) copy-start(bf16[2048,1024]{1,0:T(8,128)(2,1)} %param.17) | copy-start | bytes 12582916
  5.6 4.4 %copy-start.11 = (bf16[2048,2,8]{0,2,1:T(8,128)(2,1)S(1)}, bf16[2048,2,8]{0,2,1:T(8,128)(2,1)}, u32[]{:S(2)}) copy-start(bf16[2048,2,8]{0,2,1:T(8,128)(2,1)} %param.19) | copy-start | bytes 196612
  5.7 4.8 %copy-start.4 = (bf16[4,1024]{1,0:T(4,128)(2,1)S(1)}, bf16[4,1024]{1,0:T(4,128)(2,1)}, u32[]{:S(2)}) copy-start(bf16[4,1024]{1,0:T(4,128)(2,1)} %refs_8_.8) | copy-start | bytes 24580
  5.7 4.8 %copy-start.5 = (bf16[4,2,512]{2,1,0:T(2,128)(2,1)S(1)}, bf16[4,2,512]{2,1,0:T(2,128)(2,1)}, u32[]{:S(2)}) copy-start(bf16[4,2,512]{2,1,0:T(2,128)(2,1)} %refs_5_.8) | copy-start | bytes 24580
  5.7 4.8 %copy-start.7 = (f32[8]{0:T(128)S(1)}, f32[8]{0:T(128)}, u32[]{:S(2)}) copy-start(f32[8]{0:T(128)} %param.24) | copy-start | bytes 100
  5.7 4.8 %copy-start.8 = (f32[8]{0:T(128)S(1)}, f32[8]{0:T(128)}, u32[]{:S(2)}) copy-start(f32[8]{0:T(128)} %param.25) | copy-start | bytes 100
  5.7 4.8 %copy-start.9 = (f32[8]{0:T(128)S(1)}, f32[8]{0:T(128)}, u32[]{:S(2)}) copy-start(f32[8]{0:T(128)} %param.26) | copy-start | bytes 100
  7.0 7.9 %collective-permute-start = (bf16[8,2048]{1,0:T(8,128)(2,1)S(1)}, bf16[8,2048]{1,0:T(8,128)(2,1)S(1)}, u32[]{:S(2)}, u32[]{:S(2)}) collective-permute-start(bf16[8,2048]{1,0:T(8,128)(2,1)S(1)} %pad_maximum_fusion), channel_id=1, source_target_pairs={{0,4},{4,8},{8,12},{12,16},{16,20},{20,24},{24,28},{28,0},{1,5},{5... | collective-permute-start | bytes 98312 | tf_op jit(solution)/shard_map/ppermute | solution.py:541
  10.5 4.5 %copy-start.3 = (bf16[3,1024]{1,0:T(4,128)(2,1)S(1)}, bf16[3,1024]{1,0:T(4,128)(2,1)}, u32[]{:S(2)}) copy-start(bf16[3,1024]{1,0:T(4,128)(2,1)} %refs_6_.3) | copy-start | bytes 18436
  10.5 4.5 %copy-start.6 = (bf16[3,2,512]{2,1,0:T(2,128)(2,1)S(1)}, bf16[3,2,512]{2,1,0:T(2,128)(2,1)}, u32[]{:S(2)}) copy-start(bf16[3,2,512]{2,1,0:T(2,128)(2,1)} %refs_4_.5) | copy-start | bytes 18436
  15.6 7.7 %collective-permute-start.1 = (bf16[4,128,256]{2,1,0:T(8,128)(2,1)S(1)}, bf16[4,128,256]{2,1,0:T(8,128)(2,1)S(1)}, u32[]{:S(2)}, u32[]{:S(2)}) collective-permute-start(bf16[4,128,256]{2,1,0:T(8,128)(2,1)S(1)} %get-tuple-element.70.refs_8_), channel_id=1, source_target_pairs={{0,4},{4,0},{8,12},{12,8},{16,20},{20,16},{24,28},{28,24},{1,5},{5... | collective-permute-start | bytes 786440 | tf_op jit(solution)/shard_map/ppermute | solution.py:510
  21.3 3.8 %copy-start.13 = (bf16[2048,1024]{1,0:T(8,128)(2,1)S(1)}, bf16[2048,1024]{1,0:T(8,128)(2,1)}, u32[]{:S(2)}) copy-start(bf16[2048,1024]{1,0:T(8,128)(2,1)} %param.18) | copy-start | bytes 12582916
  23.5 6.8 %copy-start.2 = (f32[8,128,128]{2,1,0:T(8,128)S(1)}, f32[8,128,128]{2,1,0:T(8,128)}, u32[]{:S(2)}) copy-start(f32[8,128,128]{2,1,0:T(8,128)} %refs_3_.1) | copy-start | bytes 1572868
  23.5 10.1 %copy-start.10 = (f32[128]{0:T(128)S(1)}, f32[128]{0:T(128)}, u32[]{:S(2)}) copy-start(f32[128]{0:T(128)} %param.28) | copy-start | bytes 1540
  23.5 6.8 %collective-permute-start.2 = (bf16[4,128,256]{2,1,0:T(8,128)(2,1)S(1)}, bf16[4,128,256]{2,1,0:T(8,128)(2,1)S(1)}, u32[]{:S(2)}, u32[]{:S(2)}) collective-permute-start(bf16[4,128,256]{2,1,0:T(8,128)(2,1)S(1)} %shard_map.162.refs_2_), channel_id=1, source_target_pairs={{0,8},{4,12},{8,0},{12,4},{16,24},{20,28},{24,16},{28,20},{1,9},{5... | collective-permute-start | bytes 786440 | tf_op jit(solution)/shard_map/ppermute | solution.py:510
  30.8 7.3 %collective-permute-start.3 = (bf16[4,128,128]{2,1,0:T(8,128)(2,1)S(1)}, bf16[4,128,128]{2,1,0:T(8,128)(2,1)S(1)}, u32[]{:S(2)}, u32[]{:S(2)}) collective-permute-start(bf16[4,128,128]{2,1,0:T(8,128)(2,1)S(1)} %get-tuple-element.83), channel_id=1, source_target_pairs={{0,16},{4,20},{8,24},{12,28},{16,0},{20,4},{24,8},{28,12},{1,17},{... | collective-permute-start | bytes 393224 | tf_op jit(solution)/shard_map/ppermute | solution.py:510
  35.3 5.0 %copy-start.1 = (bf16[1024,2048]{1,0:T(8,128)(2,1)S(1)}, bf16[1024,2048]{1,0:T(8,128)(2,1)}, u32[]{:S(2)}) copy-start(bf16[1024,2048]{1,0:T(8,128)(2,1)} %refs_5_.9) | copy-start | bytes 12582916
  38.5 5.0 %collective-permute-start.4 = (bf16[4,128,128]{2,1,0:T(8,128)(2,1)S(1)}, bf16[4,128,128]{2,1,0:T(8,128)(2,1)S(1)}, u32[]{:S(2)}, u32[]{:S(2)}) collective-permute-start(bf16[4,128,128]{2,1,0:T(8,128)(2,1)S(1)} %get-tuple-element.109), channel_id=1, source_target_pairs={{0,4},{4,0},{8,12},{12,8},{16,20},{20,16},{24,28},{28,24},{1,5},{5... | collective-permute-start | bytes 393224 | tf_op jit(solution)/shard_map/ppermute | solution.py:510
  44.3 1.6 %collective-permute-start.5 = (bf16[1,256,512]{2,1,0:T(8,128)(2,1)S(1)}, bf16[1,256,512]{2,1,0:T(8,128)(2,1)S(1)}, u32[]{:S(2)}, u32[]{:S(2)}) collective-permute-start(bf16[1,256,512]{2,1,0:T(8,128)(2,1)S(1)} %get-tuple-element.115), channel_id=1, source_target_pairs={{0,1},{1,0},{2,3},{3,2},{4,5},{5,4},{6,7},{7,6},{8,9},{9,8},{10,11... | collective-permute-start | bytes 786440 | tf_op jit(solution)/shard_map/ppermute | solution.py:510
  47.6 1.7 %collective-permute-start.6 = (bf16[1,256,512]{2,1,0:T(8,128)(2,1)S(1)}, bf16[1,256,512]{2,1,0:T(8,128)(2,1)S(1)}, u32[]{:S(2)}, u32[]{:S(2)}) collective-permute-start(bf16[1,256,512]{2,1,0:T(8,128)(2,1)S(1)} %get-tuple-element.119), channel_id=1, source_target_pairs={{0,1},{1,0},{2,3},{3,2},{4,5},{5,4},{6,7},{7,6},{8,9},{9,8},{10,11... | collective-permute-start | bytes 786440 | tf_op jit(solution)/shard_map/ppermute | solution.py:510
  47.7 8.6 %collective-permute-start.7 = (bf16[1,256,512]{2,1,0:T(8,128)(2,1)S(1)}, bf16[1,256,512]{2,1,0:T(8,128)(2,1)S(1)}, u32[]{:S(2)}, u32[]{:S(2)}) collective-permute-start(bf16[1,256,512]{2,1,0:T(8,128)(2,1)S(1)} %add_convert_fusion.1), channel_id=1, source_target_pairs={{0,2},{1,3},{2,0},{3,1},{4,6},{5,7},{6,4},{7,5},{8,10},{9,11},{10,... | collective-permute-start | bytes 786440 | tf_op jit(solution)/shard_map/ppermute | solution.py:510

commit v4 on v3

--- a/solution.py
+++ b/solution.py
@@ -669,10 +669,7 @@
         flags=side,
     )(other_state, *away_reads, far, w_out)
     came_out = swapped(send_out, "head", 1)
-    total_out = (keep.astype(F32) + came_out.astype(F32)).astype(BF16)
-    total_out, other_rows = lax.optimization_barrier((total_out, other_rows))
-    came_far = swapped(total_out, "head", 2)
-    send_out, keep, checkpoint = call(
+    home_out, home_keep, checkpoint = call(
         home_kernel,
         (part_shape, part_shape, shape((1, heads, KD, DV), F32)),
         [VMEM] * 7,
@@ -680,8 +677,11 @@
         4 << 20,
         flags=side,
     )(own_rows, other_rows, w_out, maps, mine, away_maps, other_state)
-    came_out = swapped(send_out, "head", 1)
-    mixed = keep.astype(F32) + came_out.astype(F32) + came_far.astype(F32)
+    came_out, home_out = lax.optimization_barrier((came_out, home_out))
+    total_out = (keep.astype(F32) + came_out.astype(F32)).astype(BF16)
+    came_far = swapped(total_out, "head", 2)
+    came_home = swapped(home_out, "head", 1)
+    mixed = home_keep.astype(F32) + came_home.astype(F32) + came_far.astype(F32)
     step = 4
     while step < n_head:
         here = (col // step) & 1

time: 57.2 us -> 55.8 us (0.976)
  waiting for transfers between devices: 17.5 us -> 15.9 us
    ppermute x7, waiting for transfers between devices: 17.3 us -> 15.7 us  [swapped(): return lax.ppermute(value, axis, [(i, i ^ step) for i in range(count)])]
  transfers between devices with their start and end apart: 8 -> 8, of which waited for: 7 -> 6; matrix products, arithmetic and copies ran while one was open for 3% -> 3% of each run, Pallas kernels for 23% -> 27%
where the time goes in v4:
time: 55.8 us; the launch traced here: 55.6 us
  Pallas kernels  17.3 us (31%)
  waiting for transfers between devices  15.9 us (28%)
  starting transfers between devices  12.6 us (23%)
  matrix products  6.72 us (12%)
  local copies, waits for them, and re-layouts  1.31 us (2%)
  between operations  0.93 us (2%)
  other arithmetic  0.87 us (2%)
    pallas_call x12, Pallas kernels, call(): return lambda *args: run(*[flags[name] for name in names], *args)  17.3 us
    ppermute x7, waiting for transfers between devices, swapped(): return lax.ppermute(value, axis, [(i, i ^ step) for i in range(count)])  15.7 us
    ppermute x7, starting transfers between devices, swapped(): return lax.ppermute(value, axis, [(i, i ^ step) for i in range(count)])  9.57 us
    dot_general x1, matrix products, local(): jnp.einsum('td,dce->cte', hidden_in, w_qk, preferred_element_type=F32)  3.77 us
    ppermute x1, starting transfers between devices, local(): lax.ppermute(ends, 'seq', [(i, (i + 1) % n_seq) for i in range(n_seq)])  2.99 us
    unnamed x28, local copies, waits for them, and re-layouts  1.3 us
    dot_general x1, matrix products, local(): gate_z = jnp.dot(later, w_outgate, preferred_element_type=F32).astype(BF16)  1.29 us
    dot_general x1, matrix products, local(): value = jnp.dot(hidden_in, w_value, preferred_element_type=F32).astype(BF16)  1.28 us
  transfers between devices with their start and end apart: 8, of which 6 were waited for; matrix products, arithmetic and copies ran while one was open for 3% of the time, Pallas kernels for 27%

profile of v4, /device:TPU:0, one launch (start us, length us, event | category | flops | bytes accessed | tf_op | source)
XLA Modules:
  0.0 55.6 jit_solution(9841768643061767351)
XLA Ops:
  0.7 1.2 %copy-done = bf16[256,2048]{1,0:T(8,128)(2,1)S(1)} copy-done((bf16[256,2048]{1,0:T(8,128)(2,1)S(1)}, bf16[256,2048]{1,0:T(8,128)(2,1)}, u32[]{:S(2)}) %copy-start) | copy-done | bytes 1048600
  1.9 3.8 %fusion.5.refs_4_.refs_2_ = bf16[2,256,512]{2,1,0:T(8,128)(2,1)S(1)} fusion(bf16[2048,2,512]{2,1,0:T(2,128)(2,1)} %param.16, bf16[256,2048]{1,0:T(8,128)(2,1)S(1)} %copy-done), kind=kOutput, calls=%fused_computation.5 | convolution fusion | flops 1074003968 | bytes 5767168 | tf_op jit(solution)/shard_map/td,dce->cte/dot_general | solution.py:537
  5.7 1.3 %convolution_convert_fusion.1.refs_5_.refs_3_ = bf16[256,1024]{1,0:T(8,128)(2,1)S(1)} fusion(bf16[256,2048]{1,0:T(8,128)(2,1)S(1)} %copy-done, bf16[2048,1024]{1,0:T(8,128)(2,1)S(1)} %copy-done.12), kind=kOutput, calls=%fused_computation.4 | convolution fusion | flops 1074003968 | bytes 5767168 | tf_op jit(solution)/shard_map/dot_general | solution.py:538
  7.0 3.0 %collective-permute-start = (bf16[8,2048]{1,0:T(8,128)(2,1)S(1)}, bf16[8,2048]{1,0:T(8,128)(2,1)S(1)}, u32[]{:S(2)}, u32[]{:S(2)}) collective-permute-start(bf16[8,2048]{1,0:T(8,128)(2,1)S(1)} %pad_maximum_fusion), channel_id=1, source_target_pairs={{0,4},{4,8},{8,12},{12,16},{16,20},{20,24},{24,28},{28,0},{1,5},{5... | collective-permute-start | bytes 98312 | tf_op jit(solution)/shard_map/ppermute | solution.py:541
  10.0 0.4 convolution_convert_fusion.2.refs_6_
  10.5 4.3 %shard_map.158 = (bf16[2,256,128]{2,1,0:T(8,128)(2,1)S(1)}, bf16[4,256,256]{2,1,0:T(8,128)(2,1)S(1)}, f32[4,128,256]{2,1,0:T(8,128)S(1)}, f32[4,256]{1,0:T(4,128)S(1)}, f32[256,128]{1,0:T(8,128)S(1)}) custom-call(s32[1]{0:T(128)} %bitcast.1.refs_0_.refs_1_, f32[1,8]{1,0:T(1,128)S(1)} %bitcast.28, f32[1,8]{1,0:T(1,128)S(1)} %bitcast.30, f32[1,8]{1,0:T(1,128)S(1)} %bitcast.32, ...), custom_call_target="tpu_custom_call" | custom-call | flops 24000000000 | bytes 25165824 | tf_op jit(solution)/shard_map/pallas_call | solution.py:85
  14.8 0.2 collective-permute-done.refs_4_.refs_3_
  15.0 0.6 %shard_map.159 = (bf16[4,128,256]{2,1,0:T(8,128)(2,1)S(1)}, f32[2,16,128]{2,1,0:T(8,128)S(1)}, f32[4,16,256]{2,1,0:T(8,128)S(1)}) custom-call(s32[1]{0:T(128)} %bitcast.5.refs_0_, s32[1]{0:T(128)} %bitcast.1.refs_0_.refs_1_, bf16[2,256,512]{2,1,0:T(8,128)(2,1)S(1)} %fusion.5.refs_4_.refs_2_, bf16[256,1024]{1,0:T(8,128)(2,1)S(1)} %convolution_convert_fusion.1.refs_5_.refs_3_, ...), custom_call_target="tpu_custom_call" | custom-call | flops 600000000 | bytes 6291456 | tf_op jit(solution)/shard_map/pallas_call | solution.py:85
  15.6 1.5 %collective-permute-start.1 = (bf16[4,128,256]{2,1,0:T(8,128)(2,1)S(1)}, bf16[4,128,256]{2,1,0:T(8,128)(2,1)S(1)}, u32[]{:S(2)}, u32[]{:S(2)}) collective-permute-start(bf16[4,128,256]{2,1,0:T(8,128)(2,1)S(1)} %get-tuple-element.70.refs_8_), channel_id=1, source_target_pairs={{0,4},{4,0},{8,12},{12,8},{16,20},{20,16},{24,28},{28,24},{1,5},{5... | collective-permute-start | bytes 786440 | tf_op jit(solution)/shard_map/ppermute | solution.py:510
  17.1 4.3 %shard_map.160 = (bf16[2,256,128]{2,1,0:T(8,128)(2,1)S(1)}, bf16[4,256,256]{2,1,0:T(8,128)(2,1)S(1)}, f32[4,128,256]{2,1,0:T(8,128)S(1)}, f32[4,256]{1,0:T(4,128)S(1)}, f32[256,128]{1,0:T(8,128)S(1)}) custom-call(s32[1]{0:T(128)} %bitcast.1.refs_0_.refs_1_, f32[1,8]{1,0:T(1,128)S(1)} %bitcast.29, f32[1,8]{1,0:T(1,128)S(1)} %bitcast.31, f32[1,8]{1,0:T(1,128)S(1)} %bitcast.33, ...), custom_call_target="tpu_custom_call" | custom-call | flops 24000000000 | bytes 25165824 | tf_op jit(solution)/shard_map/pallas_call | solution.py:85
  21.4 0.6 %shard_map.161 = (bf16[4,128,256]{2,1,0:T(8,128)(2,1)S(1)}, f32[2,16,128]{2,1,0:T(8,128)S(1)}, f32[4,16,256]{2,1,0:T(8,128)S(1)}) custom-call(s32[1]{0:T(128)} %bitcast.5.refs_0_, s32[1]{0:T(128)} %bitcast.1.refs_0_.refs_1_, bf16[2,256,512]{2,1,0:T(8,128)(2,1)S(1)} %fusion.5.refs_4_.refs_2_, bf16[256,1024]{1,0:T(8,128)(2,1)S(1)} %convolution_convert_fusion.1.refs_5_.refs_3_, ...), custom_call_target="tpu_custom_call" | custom-call | flops 600000000 | bytes 6291456 | tf_op jit(solution)/shard_map/pallas_call | solution.py:85
  22.0 1.3 %collective-permute-done.1.refs_2_.refs_6_ = bf16[4,128,256]{2,1,0:T(8,128)(2,1)S(1)} collective-permute-done((bf16[4,128,256]{2,1,0:T(8,128)(2,1)S(1)}, bf16[4,128,256]{2,1,0:T(8,128)(2,1)S(1)}, u32[]{:S(2)}, u32[]{:S(2)}) %collective-permute-start.1) | collective-permute-done | bytes 262176 | tf_op jit(solution)/shard_map/ppermute | solution.py:510
  23.3 0.2 shard_map.162.refs_2_
  23.5 1.6 %collective-permute-start.2 = (bf16[4,128,256]{2,1,0:T(8,128)(2,1)S(1)}, bf16[4,128,256]{2,1,0:T(8,128)(2,1)S(1)}, u32[]{:S(2)}, u32[]{:S(2)}) collective-permute-start(bf16[4,128,256]{2,1,0:T(8,128)(2,1)S(1)} %shard_map.162.refs_2_), channel_id=1, source_target_pairs={{0,8},{4,12},{8,0},{12,4},{16,24},{20,28},{24,16},{28,20},{1,9},{5... | collective-permute-start | bytes 786440 | tf_op jit(solution)/shard_map/ppermute | solution.py:510
  25.2 1.3 %convolution_convert_fusion.refs_12_ = bf16[256,1024]{1,0:T(8,128)(2,1)S(1)} fusion(bf16[256,2048]{1,0:T(8,128)(2,1)S(1)} %copy-done, bf16[2048,1024]{1,0:T(8,128)(2,1)S(1)} %copy-done.13), kind=kOutput, calls=%fused_computation.3 | convolution fusion | flops 1074003968 | bytes 5767168 | tf_op jit(solution)/shard_map/dot_general | solution.py:623
  26.5 3.8 %collective-permute-done.2.refs_3_ = bf16[4,128,256]{2,1,0:T(8,128)(2,1)S(1)} collective-permute-done((bf16[4,128,256]{2,1,0:T(8,128)(2,1)S(1)}, bf16[4,128,256]{2,1,0:T(8,128)(2,1)S(1)}, u32[]{:S(2)}, u32[]{:S(2)}) %collective-permute-start.2) | collective-permute-done | bytes 262176 | tf_op jit(solution)/shard_map/ppermute | solution.py:510
  30.3 0.5 shard_map.163
  30.8 2.8 %collective-permute-start.3 = (bf16[4,128,128]{2,1,0:T(8,128)(2,1)S(1)}, bf16[4,128,128]{2,1,0:T(8,128)(2,1)S(1)}, u32[]{:S(2)}, u32[]{:S(2)}) collective-permute-start(bf16[4,128,128]{2,1,0:T(8,128)(2,1)S(1)} %get-tuple-element.83), channel_id=1, source_target_pairs={{0,16},{4,20},{8,24},{12,28},{16,0},{20,4},{24,8},{28,12},{1,17},{... | collective-permute-start | bytes 393224 | tf_op jit(solution)/shard_map/ppermute | solution.py:510
  33.7 1.7 %shard_map.165 = (bf16[4,256,128]{2,1,0:T(8,128)(2,1)S(1)}, f32[4,256,128]{2,1,0:T(8,128)S(1)}, f32[4,256,128]{2,1,0:T(8,128)S(1)}) custom-call(s32[1]{0:T(128)} %bitcast.5.refs_0_, s32[1]{0:T(128)} %bitcast.1.refs_0_.refs_1_, bf16[2,256,512]{2,1,0:T(8,128)(2,1)S(1)} %fusion.5.refs_4_.refs_2_, bf16[8,2048]{1,0:T(8,128)(2,1)S(1)} %collective-permute-done.refs_4_.refs_3_, ...), custom_call_target="tpu_custom_call" | custom-call | flops 12000000000 | bytes 25165824 | tf_op jit(solution)/shard_map/pallas_call | solution.py:85
  35.4 1.7 %shard_map.164 = (bf16[4,256,128]{2,1,0:T(8,128)(2,1)S(1)}, f32[4,256,128]{2,1,0:T(8,128)S(1)}, f32[4,256,128]{2,1,0:T(8,128)S(1)}) custom-call(s32[1]{0:T(128)} %bitcast.5.refs_0_, s32[1]{0:T(128)} %bitcast.1.refs_0_.refs_1_, bf16[2,256,512]{2,1,0:T(8,128)(2,1)S(1)} %fusion.5.refs_4_.refs_2_, bf16[8,2048]{1,0:T(8,128)(2,1)S(1)} %collective-permute-done.refs_4_.refs_3_, ...), custom_call_target="tpu_custom_call" | custom-call | flops 12000000000 | bytes 25165824 | tf_op jit(solution)/shard_map/pallas_call | solution.py:85
  37.1 1.1 %collective-permute-done.3.refs_4_ = bf16[4,128,128]{2,1,0:T(8,128)(2,1)S(1)} collective-permute-done((bf16[4,128,128]{2,1,0:T(8,128)(2,1)S(1)}, bf16[4,128,128]{2,1,0:T(8,128)(2,1)S(1)}, u32[]{:S(2)}, u32[]{:S(2)}) %collective-permute-start.3) | collective-permute-done | bytes 131104 | tf_op jit(solution)/shard_map/ppermute | solution.py:510
  38.2 0.4 shard_map.166
  38.5 1.8 %collective-permute-start.4 = (bf16[4,128,128]{2,1,0:T(8,128)(2,1)S(1)}, bf16[4,128,128]{2,1,0:T(8,128)(2,1)S(1)}, u32[]{:S(2)}, u32[]{:S(2)}) collective-permute-start(bf16[4,128,128]{2,1,0:T(8,128)(2,1)S(1)} %get-tuple-element.109), channel_id=1, source_target_pairs={{0,4},{4,0},{8,12},{12,8},{16,20},{20,16},{24,28},{28,24},{1,5},{5... | collective-permute-start | bytes 393224 | tf_op jit(solution)/shard_map/ppermute | solution.py:510
  40.3 0.7 %shard_map.167 = (bf16[256,512]{1,0:T(8,128)(2,1)S(1)}, f32[2,1,256,512]{3,2,1,0:T(8,128)S(1)}) custom-call(s32[1]{0:T(128)} %bitcast.refs_0_, s32[1]{0:T(128)} %bitcast.1.refs_0_.refs_1_, s32[1]{0:T(128)} %bitcast.2.refs_2_, bf16[4,128,128]{2,1,0:T(8,128)(2,1)S(1)} %get-tuple-element.104.refs_3_.refs_7_, ...), custom_call_target="tpu_custom_call" | custom-call | flops 6000000000 | bytes 25165824 | tf_op jit(solution)/shard_map/pallas_call | solution.py:85
  41.0 2.5 %collective-permute-done.4.refs_3_.refs_9_ = bf16[4,128,128]{2,1,0:T(8,128)(2,1)S(1)} collective-permute-done((bf16[4,128,128]{2,1,0:T(8,128)(2,1)S(1)}, bf16[4,128,128]{2,1,0:T(8,128)(2,1)S(1)}, u32[]{:S(2)}, u32[]{:S(2)}) %collective-permute-start.4) | collective-permute-done | bytes 131104 | tf_op jit(solution)/shard_map/ppermute | solution.py:510
  43.6 0.7 %shard_map.168 = (bf16[256,512]{1,0:T(8,128)(2,1)S(1)}, bf16[1,256,512]{2,1,0:T(8,128)(2,1)S(1)}, bf16[1,256,512]{2,1,0:T(8,128)(2,1)S(1)}) custom-call(s32[1]{0:T(128)} %bitcast.refs_0_, s32[1]{0:T(128)} %bitcast.1.refs_0_.refs_1_, s32[1]{0:T(128)} %bitcast.2.refs_2_, bf16[4,128,128]{2,1,0:T(8,128)(2,1)S(1)} %collective-permute-done.4.refs_3_.refs_9_, ...), custom_call_target="tpu_custom_call" | custom-call | flops 6000000000 | bytes 25165824 | tf_op jit(solution)/shard_map/pallas_call | solution.py:85
  44.3 0.1 collective-permute-start.5
  44.4 1.6 %shard_map.169 = (bf16[1,256,512]{2,1,0:T(8,128)(2,1)S(1)}, bf16[1,256,512]{2,1,0:T(8,128)(2,1)S(1)}, f32[1,8,128,128]{3,2,1,0:T(8,128)}) custom-call(s32[1]{0:T(128)} %bitcast.refs_0_, s32[1]{0:T(128)} %bitcast.1.refs_0_.refs_1_, s32[1]{0:T(128)} %bitcast.2.refs_2_, bf16[256,512]{1,0:T(8,128)(2,1)S(1)} %get-tuple-element.108.refs_3_, ...), custom_call_target="tpu_custom_call" | custom-call | flops 6000000000 | bytes 25165824 | tf_op jit(solution)/shard_map/pallas_call | solution.py:85
  46.0 1.6 %collective-permute-start.7 = (bf16[1,256,512]{2,1,0:T(8,128)(2,1)S(1)}, bf16[1,256,512]{2,1,0:T(8,128)(2,1)S(1)}, u32[]{:S(2)}, u32[]{:S(2)}) collective-permute-start(bf16[1,256,512]{2,1,0:T(8,128)(2,1)S(1)} %add_convert_fusion.1), channel_id=1, source_target_pairs={{0,2},{1,3},{2,0},{3,1},{4,6},{5,7},{6,4},{7,5},{8,10},{9,11},{10,... | collective-permute-start | bytes 786440 | tf_op jit(solution)/shard_map/ppermute | solution.py:510
  47.6 0.2 collective-permute-start.6
  47.8 7.0 %collective-permute-done.7 = bf16[1,256,512]{2,1,0:T(8,128)(2,1)S(1)} collective-permute-done((bf16[1,256,512]{2,1,0:T(8,128)(2,1)S(1)}, bf16[1,256,512]{2,1,0:T(8,128)(2,1)S(1)}, u32[]{:S(2)}, u32[]{:S(2)}) %collective-permute-start.7) | collective-permute-done | bytes 262176 | tf_op jit(solution)/shard_map/ppermute | solution.py:510
  54.8 0.8 %fusion.10 = bf16[256,512]{1,0:T(8,128)(2,1)} fusion(bf16[1,256,512]{2,1,0:T(8,128)(2,1)S(1)} %collective-permute-done.7, bf16[1,256,512]{2,1,0:T(8,128)(2,1)S(1)} %collective-permute-done.6, bf16[1,256,512]{2,1,0:T(8,128)(2,1)S(1)} %get-tuple-element.115), kind=kLoop, calls=%fused_computation.11 | loop fusion | flops 786432 | bytes 1048576 | tf_op jit(solution)/shard_map/convert_element_type | solution.py:694
  (33 shorter events, 0.2 us)
Async XLA Ops:
  0.6 1.2 %copy-start = (bf16[256,2048]{1,0:T(8,128)(2,1)S(1)}, bf16[256,2048]{1,0:T(8,128)(2,1)}, u32[]{:S(2)}) copy-start(bf16[256,2048]{1,0:T(8,128)(2,1)} %param.15) | copy-start | bytes 3145732
  0.6 5.0 %copy-start.12 = (bf16[2048,1024]{1,0:T(8,128)(2,1)S(1)}, bf16[2048,1024]{1,0:T(8,128)(2,1)}, u32[]{:S(2)}) copy-start(bf16[2048,1024]{1,0:T(8,128)(2,1)} %param.17) | copy-start | bytes 12582916
  5.6 4.4 %copy-start.11 = (bf16[2048,2,8]{0,2,1:T(8,128)(2,1)S(1)}, bf16[2048,2,8]{0,2,1:T(8,128)(2,1)}, u32[]{:S(2)}) copy-start(bf16[2048,2,8]{0,2,1:T(8,128)(2,1)} %param.19) | copy-start | bytes 196612
  5.7 4.8 %copy-start.4 = (bf16[4,1024]{1,0:T(4,128)(2,1)S(1)}, bf16[4,1024]{1,0:T(4,128)(2,1)}, u32[]{:S(2)}) copy-start(bf16[4,1024]{1,0:T(4,128)(2,1)} %refs_8_.8) | copy-start | bytes 24580
  5.7 4.8 %copy-start.5 = (bf16[4,2,512]{2,1,0:T(2,128)(2,1)S(1)}, bf16[4,2,512]{2,1,0:T(2,128)(2,1)}, u32[]{:S(2)}) copy-start(bf16[4,2,512]{2,1,0:T(2,128)(2,1)} %refs_5_.8) | copy-start | bytes 24580
  5.7 4.8 %copy-start.7 = (f32[8]{0:T(128)S(1)}, f32[8]{0:T(128)}, u32[]{:S(2)}) copy-start(f32[8]{0:T(128)} %param.24) | copy-start | bytes 100
  5.7 4.8 %copy-start.8 = (f32[8]{0:T(128)S(1)}, f32[8]{0:T(128)}, u32[]{:S(2)}) copy-start(f32[8]{0:T(128)} %param.25) | copy-start | bytes 100
  5.7 4.8 %copy-start.9 = (f32[8]{0:T(128)S(1)}, f32[8]{0:T(128)}, u32[]{:S(2)}) copy-start(f32[8]{0:T(128)} %param.26) | copy-start | bytes 100
  7.0 7.9 %collective-permute-start = (bf16[8,2048]{1,0:T(8,128)(2,1)S(1)}, bf16[8,2048]{1,0:T(8,128)(2,1)S(1)}, u32[]{:S(2)}, u32[]{:S(2)}) collective-permute-start(bf16[8,2048]{1,0:T(8,128)(2,1)S(1)} %pad_maximum_fusion), channel_id=1, source_target_pairs={{0,4},{4,8},{8,12},{12,16},{16,20},{20,24},{24,28},{28,0},{1,5},{5... | collective-permute-start | bytes 98312 | tf_op jit(solution)/shard_map/ppermute | solution.py:541
  10.5 4.5 %copy-start.3 = (bf16[3,1024]{1,0:T(4,128)(2,1)S(1)}, bf16[3,1024]{1,0:T(4,128)(2,1)}, u32[]{:S(2)}) copy-start(bf16[3,1024]{1,0:T(4,128)(2,1)} %refs_6_.3) | copy-start | bytes 18436
  10.5 4.5 %copy-start.6 = (bf16[3,2,512]{2,1,0:T(2,128)(2,1)S(1)}, bf16[3,2,512]{2,1,0:T(2,128)(2,1)}, u32[]{:S(2)}) copy-start(bf16[3,2,512]{2,1,0:T(2,128)(2,1)} %refs_4_.5) | copy-start | bytes 18436
  15.6 7.7 %collective-permute-start.1 = (bf16[4,128,256]{2,1,0:T(8,128)(2,1)S(1)}, bf16[4,128,256]{2,1,0:T(8,128)(2,1)S(1)}, u32[]{:S(2)}, u32[]{:S(2)}) collective-permute-start(bf16[4,128,256]{2,1,0:T(8,128)(2,1)S(1)} %get-tuple-element.70.refs_8_), channel_id=1, source_target_pairs={{0,4},{4,0},{8,12},{12,8},{16,20},{20,16},{24,28},{28,24},{1,5},{5... | collective-permute-start | bytes 786440 | tf_op jit(solution)/shard_map/ppermute | solution.py:510
  21.3 3.8 %copy-start.13 = (bf16[2048,1024]{1,0:T(8,128)(2,1)S(1)}, bf16[2048,1024]{1,0:T(8,128)(2,1)}, u32[]{:S(2)}) copy-start(bf16[2048,1024]{1,0:T(8,128)(2,1)} %param.18) | copy-start | bytes 12582916
  23.5 6.8 %copy-start.2 = (f32[8,128,128]{2,1,0:T(8,128)S(1)}, f32[8,128,128]{2,1,0:T(8,128)}, u32[]{:S(2)}) copy-start(f32[8,128,128]{2,1,0:T(8,128)} %refs_3_.1) | copy-start | bytes 1572868
  23.5 10.1 %copy-start.10 = (f32[128]{0:T(128)S(1)}, f32[128]{0:T(128)}, u32[]{:S(2)}) copy-start(f32[128]{0:T(128)} %param.28) | copy-start | bytes 1540
  23.5 6.8 %collective-permute-start.2 = (bf16[4,128,256]{2,1,0:T(8,128)(2,1)S(1)}, bf16[4,128,256]{2,1,0:T(8,128)(2,1)S(1)}, u32[]{:S(2)}, u32[]{:S(2)}) collective-permute-start(bf16[4,128,256]{2,1,0:T(8,128)(2,1)S(1)} %shard_map.162.refs_2_), channel_id=1, source_target_pairs={{0,8},{4,12},{8,0},{12,4},{16,24},{20,28},{24,16},{28,20},{1,9},{5... | collective-permute-start | bytes 786440 | tf_op jit(solution)/shard_map/ppermute | solution.py:510
  30.8 7.3 %collective-permute-start.3 = (bf16[4,128,128]{2,1,0:T(8,128)(2,1)S(1)}, bf16[4,128,128]{2,1,0:T(8,128)(2,1)S(1)}, u32[]{:S(2)}, u32[]{:S(2)}) collective-permute-start(bf16[4,128,128]{2,1,0:T(8,128)(2,1)S(1)} %get-tuple-element.83), channel_id=1, source_target_pairs={{0,16},{4,20},{8,24},{12,28},{16,0},{20,4},{24,8},{28,12},{1,17},{... | collective-permute-start | bytes 393224 | tf_op jit(solution)/shard_map/ppermute | solution.py:510
  35.3 5.0 %copy-start.1 = (bf16[1024,2048]{1,0:T(8,128)(2,1)S(1)}, bf16[1024,2048]{1,0:T(8,128)(2,1)}, u32[]{:S(2)}) copy-start(bf16[1024,2048]{1,0:T(8,128)(2,1)} %refs_5_.9) | copy-start | bytes 12582916
  38.5 5.0 %collective-permute-start.4 = (bf16[4,128,128]{2,1,0:T(8,128)(2,1)S(1)}, bf16[4,128,128]{2,1,0:T(8,128)(2,1)S(1)}, u32[]{:S(2)}, u32[]{:S(2)}) collective-permute-start(bf16[4,128,128]{2,1,0:T(8,128)(2,1)S(1)} %get-tuple-element.109), channel_id=1, source_target_pairs={{0,4},{4,0},{8,12},{12,8},{16,20},{20,16},{24,28},{28,24},{1,5},{5... | collective-permute-start | bytes 393224 | tf_op jit(solution)/shard_map/ppermute | solution.py:510
  44.3 1.7 %collective-permute-start.5 = (bf16[1,256,512]{2,1,0:T(8,128)(2,1)S(1)}, bf16[1,256,512]{2,1,0:T(8,128)(2,1)S(1)}, u32[]{:S(2)}, u32[]{:S(2)}) collective-permute-start(bf16[1,256,512]{2,1,0:T(8,128)(2,1)S(1)} %get-tuple-element.116), channel_id=1, source_target_pairs={{0,1},{1,0},{2,3},{3,2},{4,5},{5,4},{6,7},{7,6},{8,9},{9,8},{10,11... | collective-permute-start | bytes 786440 | tf_op jit(solution)/shard_map/ppermute | solution.py:510
  46.0 8.8 %collective-permute-start.7 = (bf16[1,256,512]{2,1,0:T(8,128)(2,1)S(1)}, bf16[1,256,512]{2,1,0:T(8,128)(2,1)S(1)}, u32[]{:S(2)}, u32[]{:S(2)}) collective-permute-start(bf16[1,256,512]{2,1,0:T(8,128)(2,1)S(1)} %add_convert_fusion.1), channel_id=1, source_target_pairs={{0,2},{1,3},{2,0},{3,1},{4,6},{5,7},{6,4},{7,5},{8,10},{9,11},{10,... | collective-permute-start | bytes 786440 | tf_op jit(solution)/shard_map/ppermute | solution.py:510
  47.6 7.2 %collective-permute-start.6 = (bf16[1,256,512]{2,1,0:T(8,128)(2,1)S(1)}, bf16[1,256,512]{2,1,0:T(8,128)(2,1)S(1)}, u32[]{:S(2)}, u32[]{:S(2)}) collective-permute-start(bf16[1,256,512]{2,1,0:T(8,128)(2,1)S(1)} %get-tuple-element.118), channel_id=1, source_target_pairs={{0,1},{1,0},{2,3},{3,2},{4,5},{5,4},{6,7},{7,6},{8,9},{9,8},{10,11... | collective-permute-start | bytes 786440 | tf_op jit(solution)/shard_map/ppermute | solution.py:510

commit v5 on v4

--- a/solution.py
+++ b/solution.py
@@ -12,6 +12,7 @@
 HALF = 128
 HALO = 16
 TAIL = 8
+ORDER = (3, 1, 2)
 F32 = jnp.float32
 BF16 = jnp.bfloat16
 VMEM = pl.BlockSpec(memory_space=pltpu.VMEM)
@@ -80,7 +81,7 @@
         out_specs=jax.tree.map(lambda _: VMEM, out_shape),
         scratch_shapes=list(scratch),
         compiler_params=pltpu.CompilerParams(vmem_limit_bytes=12 << 20),
-        cost_estimate=pl.CostEstimate(flops=6 * flops, bytes_accessed=6 * moved, transcendentals=0),
+        cost_estimate=pl.CostEstimate(flops=flops, bytes_accessed=moved, transcendentals=0),
     )
     return lambda *args: run(*[flags[name] for name in names], *args)
 
@@ -130,23 +131,22 @@
 
 
 def prepare_kernel(
-    own, place, a_log, dt_bias, beta_bias, qk, value, gates, conv_qk, conv_value,
+    a_log, dt_bias, beta_bias, qk, value, gates, conv_qk, conv_value,
     keys_out, solved_out, maps_out, rows_out, cols_out, conv_s,
 ):
-    heads = gates.shape[1] // 2
+    heads = gates.shape[1]
     rows = gates.shape[2]
     key_heads = heads // 2
     taps = conv_value.shape[0]
-    side = place[1] if own else 1 - place[1]
     load_small(None, conv_qk, 1, None, conv_s)
     zero = jnp.zeros((HALO, KD), F32)
     rest = lax.broadcasted_iota(jnp.int32, (heads, rows), 1) >= taps - 1
     strength = jax.nn.sigmoid(
-        picked(side, gates[0].astype(F32)) + picked(side, as_column(beta_bias[...]))
+        gates[0].astype(F32) + as_column(beta_bias[...])
     )
-    decay_in = picked(side, gates[1].astype(F32)) + picked(side, as_column(dt_bias[...]))
+    decay_in = gates[1].astype(F32) + as_column(dt_bias[...])
     soft = jnp.maximum(decay_in, 0.0) + jnp.log1p(jnp.exp(-jnp.abs(decay_in)))
-    log_decay = -jnp.exp(picked(side, as_column(a_log[...]))) * soft
+    log_decay = -jnp.exp(as_column(a_log[...])) * soft
     raw = [strength, log_decay]
     strength = jnp.where(rest, strength, 0.0)
     log_decay = jnp.where(rest, log_decay, 0.0)
@@ -172,15 +172,14 @@
     rhs = []
     ends = []
     for key_head in range(key_heads):
-        lanes = lane_block(side * key_heads + key_head, KD)
+        lanes = slice(key_head * KD, (key_head + 1) * KD)
         key = unit_rows(conv_rows(qk[1, :, lanes].astype(F32), zero, conv_s[:, lanes]))
         key_low = key.astype(BF16)
         keys_out[key_head] = key_low
         dots = dot_nt(key_low, key_low)
         key_t = key.T
         for head in (2 * key_head, 2 * key_head + 1):
-            index = side * heads + head
-            lanes = lane_block(index, DV)
+            lanes = slice(head * DV, (head + 1) * DV)
             val = conv_rows(value[:, lanes].astype(F32), zero, conv_value[:, lanes].astype(F32))
             col = cols[:, head : head + 1]
             beta = cols[:, heads + head : heads + head + 1]
@@ -230,25 +229,23 @@
 
 
 def front_kernel(
-    own, place, qk, value, halo, hist_qk, hist_value, conv_qk, conv_value, rest, cols,
-    maps_out, keys_out, solved_out, hist_s, conv_s, hist_v,
+    place, qk, value, halo, hist_qk, hist_value, conv_qk, conv_value, rest, cols,
+    maps_out, keys_out, solved_out, send_1, send_2, send_3, hist_s, conv_s, hist_v,
 ):
     heads = rest.shape[0]
     key_heads = heads // 2
     key_cols = qk.shape[2]
     taps = conv_value.shape[0]
     count = taps - 1
-    first = place[0] == 0
-    side = place[1] if own else 1 - place[1]
+    first = place["seq"] == 0
     load_small(hist_qk, conv_qk, 1, hist_s, conv_s)
     hist_v[HALO - count :, :] = hist_value[...].astype(F32)
     for pair in range(key_heads):
-        index = side * key_heads + pair
-        lanes = lane_block(index, KD)
+        lanes = slice(pair * KD, (pair + 1) * KD)
+        halo_lanes = slice(key_cols + pair * KD, key_cols + (pair + 1) * KD)
         key = unit_rows(
             front_rows(
-                qk[1, :HALO, lanes], halo, hist_s, conv_s[:, lanes], lanes,
-                lane_block(key_cols // KD + index, KD), first,
+                qk[1, :HALO, lanes], halo, hist_s, conv_s[:, lanes], lanes, halo_lanes, first
             )
         )
         keys = [key[i : i + 1] for i in range(count)]
@@ -259,11 +256,11 @@
             for j in range(i)
         }
         for head in (2 * pair, 2 * pair + 1):
-            index = side * heads + head
-            lanes = lane_block(index, DV)
+            lanes = slice(head * DV, (head + 1) * DV)
+            halo_lanes = slice(2 * key_cols + head * DV, 2 * key_cols + (head + 1) * DV)
             val = front_rows(
                 value[:HALO, lanes], halo, hist_v, conv_value[:, lanes].astype(F32), lanes,
-                lane_block(2 * key_cols // DV + index, DV), first,
+                halo_lanes, first,
             )
             beta = cols[:HALO, 4 * heads + head : 4 * heads + head + 1]
             cumul = running(cols[:HALO, 5 * heads + head : 5 * heads + head + 1], count)
@@ -276,6 +273,8 @@
             solved_out[head] = stacked(solved, KD + DV)
             ends = stacked([jnp.exp(cumul[-1] - cumul[i]) * keys[i] for i in range(count)], KD)
             maps_out[head] = put_ahead(rest[head], jnp.exp(cumul[-1]), ends, solved_out[head]).astype(BF16)
+    for other, send in ((1, send_1), (2, send_2), (3, send_3)):
+        send[...] = maps_out[pl.ds((place["member"] ^ other) * (heads // 4), heads // 4)]
 
 
 def put_ahead(rest, fade, ends, solved):
@@ -285,14 +284,13 @@
 
 
 def query_kernel(
-    own, place, qk, halo, hist_qk, conv_qk, keys, solved, cumul, cols, front_keys, front_solved,
-    gate_z, gain, reads_out, local_out, gate_out, hist_s, conv_s,
+    place, qk, halo, hist_qk, conv_qk, keys, solved, cumul, cols, front_keys, front_solved,
+    reads_out, local_out, hist_s, conv_s,
 ):
     heads, rows = cumul.shape
     key_heads = heads // 2
     count = conv_qk.shape[0] - 1
-    first = place[0] == 0
-    side = place[1] if own else 1 - place[1]
+    first = place["seq"] == 0
     load_small(hist_qk, conv_qk, 0, hist_s, conv_s)
     line = lax.broadcasted_iota(jnp.int32, (rows, rows), 0)
     across = lax.broadcasted_iota(jnp.int32, (rows, rows), 1)
@@ -300,7 +298,7 @@
     in_front = lax.broadcasted_iota(jnp.int32, (HALO, 1), 0) < count
     zero = jnp.zeros((HALO, KD), F32)
     for pair in range(key_heads):
-        lanes = lane_block(side * key_heads + pair, KD)
+        lanes = slice(pair * KD, (pair + 1) * KD)
         query = unit_rows(conv_rows(qk[0, :, lanes].astype(F32), zero, conv_s[:, lanes]))
         query = query * (KD**-0.5)
         ahead = unit_rows(
@@ -333,8 +331,6 @@
             reads = jnp.concatenate([top, reads[HALO:]], 0)
             reads_out[head] = reads[:, :KD].astype(BF16)
             local_out[head] = reads[:, KD:]
-            lanes = lane_block(side * heads + head, DV)
-            gate_out[head] = silu(gate_z[:, lanes].astype(F32)) * gain[...]
 
 
 def join(outer, inner):
@@ -356,27 +352,43 @@
         body(mine, other)
 
 
-def pair_kernel(place, maps, received, total_out):
-    def body(low, high):
-        for j in range(received.shape[0]):
-            total_out[j] = join(high[j], low[j]).astype(BF16)
-
-    in_order(place[1], maps, received, body)
+def each_member(member, body):
+    for i in range(4):
+        pl.when(member == i)(functools.partial(body, i))
+
+
+def group_kernel(last, place, maps, got_1, got_2, got_3, state_in, total_out):
+    size = got_1.shape[0]
+
+    def body(member):
+        mine = [maps[member * size + j] for j in range(size)]
+        every = (mine, got_1, got_2, got_3)
+        for j in range(size):
+            if last:
+                total_out[j] = state_in[member * size + j].astype(BF16)
+            else:
+                total_out[j] = every[member][j]
+        for step in range(0 if last else 1, 4):
+            for j in range(size):
+                apply = act if last else join
+                total_out[j] = apply(every[step ^ member][j], total_out[j]).astype(BF16)
+
+    each_member(place["member"], body)
 
 
 def level_kernel(level, last, *refs):
-    if level == 1:
+    if level == 2:
         place, total, received, state_in, total_out, prefix_out = refs
         prefix = None
     else:
         place, total, received, prefix, state_in, total_out, prefix_out = refs
-    half = total.shape[0]
-    bit = place[level + 1]
+    size = total.shape[0]
+    bit = place[level]
 
     def body(low, high):
-        for j in range(half):
+        for j in range(size):
             if last:
-                state = state_in[place[1] * half + j].astype(BF16)
+                state = state_in[place["member"] * size + j].astype(BF16)
                 total_out[j] = act(high[j], act(low[j], state).astype(BF16)).astype(BF16)
             else:
                 total_out[j] = join(high[j], low[j]).astype(BF16)
@@ -385,7 +397,7 @@
 
     @pl.when(bit == 1)
     def _():
-        for j in range(half):
+        for j in range(size):
             if prefix is None:
                 prefix_out[j] = received[j]
             else:
@@ -396,113 +408,111 @@
         line = lax.broadcasted_iota(jnp.int32, (KD, KD + DV), 0)
         across = lax.broadcasted_iota(jnp.int32, (KD, KD + DV), 1)
         same = jnp.where(line == across, 1.0, 0.0).astype(BF16)
-        for j in range(half):
+        for j in range(size):
             prefix_out[j] = same if prefix is None else prefix[j]
 
 
-def enter_kernel(top, place, prefix, state_in, came, maps, received, mine_out, send_out):
-    bit = place[1]
-    half = prefix.shape[0]
-
-    @pl.when(place[top + 1] == 1)
+def enter_kernel(place, maps, got_1, got_2, got_3, state_in, came, *refs):
+    *prefix, mine_out, send_1, send_2, send_3 = refs
+    size = came.shape[0]
+    outs = (mine_out, send_1, send_2, send_3)
+
+    @pl.when(place["top"] == 1)
     def _():
-        for j in range(half):
-            mine_out[j] = act(prefix[j], came[j]).astype(BF16)
-
-    @pl.when(place[top + 1] == 0)
+        mine_out[...] = came[...]
+
+    @pl.when(place["top"] == 0)
     def _():
-        for j in range(half):
-            mine_out[j] = act(prefix[j], state_in[bit * half + j].astype(BF16)).astype(BF16)
-
-    @pl.when(bit == 1)
-    def _():
-        for j in range(half):
-            entering = mine_out[j]
-            send_out[j] = entering
-            mine_out[j] = act(received[j], entering).astype(BF16)
-
-    @pl.when(bit == 0)
-    def _():
-        for j in range(half):
-            send_out[j] = act(maps[j], mine_out[j]).astype(BF16)
-
-
-def normed_rows(local_part, reads, gate, state):
+        for j in range(size):
+            mine_out[j] = state_in[place["member"] * size + j].astype(BF16)
+
+    if prefix:
+        for j in range(size):
+            mine_out[j] = act(prefix[0][j], mine_out[j]).astype(BF16)
+
+    def body(member):
+        mine = [maps[member * size + j] for j in range(size)]
+        every = (mine, got_1, got_2, got_3)
+        states = [mine_out[j] for j in range(size)]
+        for step in range(4):
+            for j in range(size):
+                outs[step ^ member][j] = states[j]
+            if step < 3:
+                states = [
+                    act(every[step ^ member][j], states[j]).astype(BF16) for j in range(size)
+                ]
+
+    each_member(place["member"], body)
+
+
+def normed_rows(local_part, reads, gate, gain, state):
     out = local_part + dot(reads, state)
     scale = lax.rsqrt(jnp.mean(out * out, axis=-1, keepdims=True) + 1e-06)
-    return (out * scale * gate).astype(BF16)
-
-
-def project(side, rows_in, own, w_out, away, emit):
-    core, bit, lift = side[0], side[1], side[2]
-    depth = w_out.shape[0] // 2
-    member = bit if own else 1 - bit
-    width = w_out.shape[1] // emit.count
-    for j in range(emit.count // 4):
-        block = 2 * j + (1 - lift if away else lift)
-        for target, column in ((0, 1 - core), (1, core)):
-            lanes = lane_block(2 * block + column, width)
-            rows_of = pl.ds(pl.multiple_of(member * depth, depth), depth)
-            emit(target, j, dot(rows_in[...], w_out[rows_of, lanes]))
-
-
-class Emit:
-    def __init__(self, count, store):
-        self.count, self.store = count, store
-
-    def __call__(self, target, j, product):
-        self.store(target, j, product)
-
-
-def normed_all(states, reads, local_reads, gate, normed_out):
-    for j in range(states.shape[0]):
-        normed_out[:, j * DV : (j + 1) * DV] = normed_rows(
-            local_reads[j], reads[j], gate[j], states[j]
-        )
-
-
-def own_kernel(side, states, reads, local_reads, gate, w_out, normed_out, far_out):
-    normed_all(states, reads, local_reads, gate, normed_out)
-    count = w_out.shape[1] // far_out.shape[3]
-
-    def store(target, j, product):
-        far_out[target, j] = product
-
-    project(side, normed_out, True, w_out, True, Emit(count, store))
-
-
-def away_kernel(
-    side, states, reads, local_reads, gate, far, w_out, other_rows, send_out, keep_out
-):
-    normed_all(states, reads, local_reads, gate, other_rows)
-    count = w_out.shape[1] // send_out.shape[2]
-
-    def store(target, j, product):
-        (send_out, keep_out)[target][j] = (far[target, j] + product).astype(BF16)
-
-    project(side, other_rows, False, w_out, True, Emit(count, store))
+    return (out * scale * gain * silu(gate.astype(F32))).astype(BF16)
+
+
+def normed_slots(slots, place, states, reads, local_reads, gate_z, gain, normed_out):
+    size = states[0].shape[0]
+    for at, slot in enumerate(slots):
+        for j in range(size):
+            head = (place["member"] ^ slot) * size + j
+            normed_out[at, :, j * DV : (j + 1) * DV] = normed_rows(
+                local_reads[head], reads[head], gate_z[:, lane_block(head, DV)], gain[...],
+                states[at][j],
+            )
+
+
+def project(slots, place, normed, w_out, lift, width, j, target):
+    depth = normed.shape[2]
+    column = place["core"] if target else 1 - place["core"]
+    lanes = lane_block(2 * (2 * j + lift) + column, width)
+    total = None
+    for at, slot in enumerate(slots):
+        rows_of = lane_block(place["member"] ^ slot, depth)
+        product = dot(normed[at], w_out[rows_of, lanes])
+        total = product if total is None else total + product
+    return total
+
+
+def early_kernel(slots, place, *refs):
+    *states, reads, local_reads, gate_z, gain, normed_out = refs
+    normed_slots(slots, place, states, reads, local_reads, gate_z, gain, normed_out)
+
+
+def both_products(early, late, place, early_rows, late_rows, w_out, lift, width, j, target):
+    return project(early, place, early_rows, w_out, lift, width, j, target) + project(
+        late, place, late_rows, w_out, lift, width, j, target
+    )
+
+
+def late_kernel(early, late, place, *refs):
+    *states, reads, local_reads, gate_z, gain, early_rows, w_out = refs[:-3]
+    late_rows, send_out, keep_out = refs[-3:]
+    normed_slots(late, place, states, reads, local_reads, gate_z, gain, late_rows)
+    for target, out in enumerate((send_out, keep_out)):
+        for j in range(out.shape[0]):
+            out[j] = both_products(
+                early, late, place, early_rows, late_rows, w_out, 1 - place["lift"], out.shape[2],
+                j, target,
+            ).astype(BF16)
 
 
 def home_kernel(
-    side, mine_rows, other_rows, w_out, maps, states, away_maps, away_states,
+    early, late, place, early_rows, late_rows, w_out, maps, state_0, state_1, state_2, state_3,
     send_out, keep_out, checkpoint,
 ):
-    count = w_out.shape[1] // send_out.shape[2]
-    sums = {}
-
-    def store_own(target, j, product):
-        sums[target, j] = product
-
-    def store(target, j, product):
-        (send_out, keep_out)[target][j] = (sums[target, j] + product).astype(BF16)
-
-    project(side, mine_rows, True, w_out, False, Emit(count, store_own))
-    project(side, other_rows, False, w_out, False, Emit(count, store))
-    bit = side[1]
-    half = maps.shape[0]
-    for j in range(half):
-        checkpoint[0, bit * half + j] = act(maps[j], states[j])
-        checkpoint[0, (1 - bit) * half + j] = act(away_maps[j], away_states[j])
+    for target, out in enumerate((send_out, keep_out)):
+        for j in range(out.shape[0]):
+            total = both_products(
+                early, late, place, early_rows, late_rows, w_out, place["lift"], out.shape[2],
+                j, target,
+            )
+            out[j] = total.astype(BF16)
+    size = state_0.shape[0]
+    for slot, states in enumerate((state_0, state_1, state_2, state_3)):
+        for j in range(size):
+            head = (place["member"] ^ slot) * size + j
+            checkpoint[0, head] = act(maps[head], states[j])
 
 
 def swapped(value, axis, step):
@@ -528,7 +538,13 @@
     def scalar(value):
         return value.astype(jnp.int32).reshape(1)
 
-    place = {0: scalar(seq)} | {i + 1: scalar((seq >> i) & 1) for i in range(levels)}
+    place = {i: scalar((seq >> i) & 1) for i in range(levels)} | {
+        "seq": scalar(seq),
+        "member": scalar(seq & 3),
+        "top": scalar(seq >> (levels - 1)),
+        "core": scalar(col & 1),
+        "lift": scalar((col >> 1) & 1),
+    }
 
     def only(*names):
         return {name: place[name] for name in names}
@@ -543,140 +559,128 @@
 
     small = [pltpu.VMEM((HALO, key_cols), F32), pltpu.VMEM((taps, key_cols), F32)]
 
-    def prepare(own, qk):
-        return call(
-            functools.partial(prepare_kernel, own),
-            (
-                shape((half // 2, rows, KD), BF16),
-                shape((half, rows, KD + DV), BF16),
-                shape((half, KD, KD + DV), F32),
-                shape((half, rows), F32),
-                shape((rows, 128), F32),
-            ),
-            [VMEM] * 8,
-            4 * 10**9,
-            4 << 20,
-            small[1:],
-            only(1),
-        )(
-            a_log.reshape(1, heads), dt_bias.reshape(1, heads), beta_bias.reshape(1, heads),
-            qk, value, gates, conv_qk, conv_value,
-        )
-
-    def front(own, prepared):
-        return call(
-            functools.partial(front_kernel, own),
-            (
-                shape((half, KD, KD + DV), BF16),
-                shape((half // 2, HALO, KD), F32),
-                shape((half, HALO, KD + DV), F32),
-            ),
-            [VMEM] * 9,
-            10**8,
-            1 << 20,
-            small + [pltpu.VMEM((HALO, heads * DV), F32)],
-            only(0, 1),
-        )(
-            qk, value, halo, hist_qk, hist_value, conv_qk, conv_value,
-            prepared[2], prepared[4],
-        )
-
-    def query(own, prepared, fronted, qk):
-        keys, solved, _, cumul, cols = prepared
-        return call(
-            functools.partial(query_kernel, own),
-            (
-                shape((half, rows, KD), BF16),
-                shape((half, rows, DV), F32),
-                shape((half, rows, DV), F32),
-            ),
-            [VMEM] * 12,
-            2 * 10**9,
-            4 << 20,
-            small,
-            only(0, 1),
-        )(
-            qk, halo, hist_qk, conv_qk, keys, solved, cumul, cols, fronted[1], fronted[2],
-            gate_z, norm_gain.reshape(1, DV),
-        )
-
-    away = prepare(False, qk)
-    halo, away = lax.optimization_barrier((halo, away))
-    away_front = front(False, away)
-    received = swapped(away_front[0], "seq", 1)
-    later, _ = lax.optimization_barrier((qk, away_front[0]))
-    own = prepare(True, later)
-    own_front = front(True, own)
-    maps, away_maps = own_front[0], away_front[0]
-    received, own, maps = lax.optimization_barrier((received, own, maps))
-
-    map_shape = shape((half, KD, KD + DV), BF16)
-    state_shape = shape((half, KD, DV), BF16)
+    size = heads // 4
+    keys, solved, rest, cumul, cols = call(
+        prepare_kernel,
+        (
+            shape((half, rows, KD), BF16),
+            shape((heads, rows, KD + DV), BF16),
+            shape((heads, KD, KD + DV), F32),
+            shape((heads, rows), F32),
+            shape((rows, 128), F32),
+        ),
+        [VMEM] * 8,
+        10000000,
+        25165824,
+        small[1:],
+    )(
+        a_log.reshape(1, heads), dt_bias.reshape(1, heads), beta_bias.reshape(1, heads),
+        qk, value, gates, conv_qk, conv_value,
+    )
+    halo, rest = lax.optimization_barrier((halo, rest))
+    map_shape = shape((size, KD, KD + DV), BF16)
+    state_shape = shape((size, KD, DV), BF16)
+    maps, front_keys, front_solved, *sends = call(
+        front_kernel,
+        (
+            shape((heads, KD, KD + DV), BF16),
+            shape((half, HALO, KD), F32),
+            shape((heads, HALO, KD + DV), F32),
+            map_shape,
+            map_shape,
+            map_shape,
+        ),
+        [VMEM] * 9,
+        10000000,
+        50331648,
+        small + [pltpu.VMEM((HALO, heads * DV), F32)],
+        only("seq", "member"),
+    )(qk, value, halo, hist_qk, hist_value, conv_qk, conv_value, rest, cols)
+
+    def to_all(values):
+        got = {step: swapped(values[step - 1], "seq", step) for step in ORDER}
+        return [got[step] for step in (1, 2, 3)]
+
+    got = to_all(sends)
+    later, _ = lax.optimization_barrier((qk, maps))
+    reads = call(
+        query_kernel,
+        (shape((heads, rows, KD), BF16), shape((heads, rows, DV), F32)),
+        [VMEM] * 10,
+        100000000000,
+        6291456,
+        small,
+        only("seq"),
+    )(later, halo, hist_qk, conv_qk, keys, solved, cumul, cols, front_keys, front_solved)
+    got, reads = lax.optimization_barrier((got, reads))
+
+    last = levels == 3
     total = call(
-        pair_kernel, map_shape, [VMEM, VMEM], 10**8, 1 << 20, flags=only(1)
-    )(maps, received)
+        functools.partial(group_kernel, last),
+        state_shape if last else map_shape,
+        [VMEM] * 5,
+        24000000000,
+        50331648,
+        flags=only("member"),
+    )(maps, *got, state_in)
     prefix = ()
-    for level in range(1, levels - 1):
+    for level in range(2, levels - 1):
         other = swapped(total, "seq", 1 << level)
-        if level == 1:
-            later, _ = lax.optimization_barrier((hidden_in, total))
-            gate_z = jnp.dot(later, w_outgate, preferred_element_type=F32).astype(BF16)
-            other, gate_z = lax.optimization_barrier((other, gate_z))
         last = level == levels - 2
         total, prefix = call(
             functools.partial(level_kernel, level, last),
             (state_shape if last else map_shape, map_shape),
-            [VMEM] * (3 if level == 1 else 4),
+            [VMEM] * (3 if level == 2 else 4),
             10**8,
             1 << 20,
-            flags=only(1, level + 1),
+            flags=only("member", level),
         )(total, other, *prefix, state_in)
         prefix = (prefix,)
     came = swapped(total, "seq", 1 << (levels - 1))
-    later, _ = lax.optimization_barrier((qk, total))
-    own_reads = query(True, own, own_front, later)
-    away_reads = query(False, away, away_front, later)
-    came, own_reads, away_reads = lax.optimization_barrier((came, own_reads, away_reads))
-    mine, send_state = call(
-        functools.partial(enter_kernel, levels - 1),
-        (state_shape, state_shape),
-        [VMEM] * 5,
-        10**8,
-        1 << 20,
-        flags=only(1, levels),
-    )(prefix[0], state_in, came, maps, received)
-    other_state = swapped(send_state, "seq", 1)
+    later, _ = lax.optimization_barrier((hidden_in, total))
+    gate_z = jnp.dot(later, w_outgate, preferred_element_type=F32).astype(BF16)
+    came, gate_z = lax.optimization_barrier((came, gate_z))
+    mine, *sends = call(
+        enter_kernel,
+        (state_shape,) * 4,
+        [VMEM] * (6 + len(prefix)),
+        600000000,
+        25165824,
+        flags=only("member", "top"),
+    )(maps, *got, state_in, came, *prefix)
+    states = [mine] + to_all(sends)
 
     out_width = w_out.shape[1] // n_head
     blocks = n_head // 4
-    side = {0: scalar(col & 1), 1: place[1], 2: scalar((col >> 1) & 1)}
+    side = only("member", "core", "lift")
     part_shape = shape((blocks, rows, out_width), BF16)
-    rows_shape = shape((rows, half * DV), BF16)
-    own_rows, far = call(
-        own_kernel,
-        (rows_shape, shape((2, blocks, rows, out_width), F32)),
-        [VMEM] * 5,
-        10**9,
-        4 << 20,
+    early, late = (0,) + ORDER[:2], ORDER[2:]
+    gain = norm_gain.reshape(1, DV)
+    early_rows = call(
+        functools.partial(early_kernel, early),
+        shape((len(early), rows, size * DV), BF16),
+        [VMEM] * (4 + len(early)),
+        1000000,
+        25165824,
         flags=side,
-    )(mine, *own_reads, w_out)
-    other_rows, send_out, keep = call(
-        away_kernel,
-        (rows_shape, part_shape, part_shape),
-        [VMEM] * 6,
-        10**9,
-        4 << 20,
+    )(*[states[slot] for slot in early], *reads, gate_z, gain)
+    late_rows, send_out, keep = call(
+        functools.partial(late_kernel, early, late),
+        (shape((len(late), rows, size * DV), BF16), part_shape, part_shape),
+        [VMEM] * (6 + len(late)),
+        100000000000,
+        50331648,
         flags=side,
-    )(other_state, *away_reads, far, w_out)
+    )(*[states[slot] for slot in late], *reads, gate_z, gain, early_rows, w_out)
     came_out = swapped(send_out, "head", 1)
     home_out, home_keep, checkpoint = call(
-        home_kernel,
+        functools.partial(home_kernel, early, late),
         (part_shape, part_shape, shape((1, heads, KD, DV), F32)),
-        [VMEM] * 7,
-        10**9,
-        4 << 20,
+        [VMEM] * 8,
+        6000000000,
+        25165824,
         flags=side,
-    )(own_rows, other_rows, w_out, maps, mine, away_maps, other_state)
+    )(early_rows, late_rows, w_out, maps, *states)
     came_out, home_out = lax.optimization_barrier((came_out, home_out))
     total_out = (keep.astype(F32) + came_out.astype(F32)).astype(BF16)
     came_far = swapped(total_out, "head", 2)

time: 55.8 us -> 55.5 us (level)
  local copies, waits for them, and re-layouts: 1.31 us -> 4.91 us
  Pallas kernels: 17.3 us -> 14.3 us
  waiting for transfers between devices: 15.9 us -> 13.5 us
  starting transfers between devices: 12.6 us -> 14.1 us
    unnamed x28 -> x34, local copies, waits for them, and re-layouts: 1.3 us -> 4.9 us
    pallas_call x12 -> x8, Pallas kernels: 17.3 us -> 14.3 us  [call(): return lambda *args: run(*[flags[name] for name in names], *args)]
    ppermute x7 -> x10, waiting for transfers between devices: 15.7 us -> 13.5 us  [swapped(): return lax.ppermute(value, axis, [(i, i ^ step) for i in range(count)])]
    ppermute x7 -> x10, starting transfers between devices: 9.57 us -> 11.1 us  [swapped(): return lax.ppermute(value, axis, [(i, i ^ step) for i in range(count)])]
  transfers between devices with their start and end apart: 8 -> 11, of which waited for: 6 -> 6; matrix products, arithmetic and copies ran while one was open for 3% -> 3% of each run, Pallas kernels for 27% -> 19%
where the time goes in v5:
time: 55.5 us; the launch traced here: 55.3 us
  Pallas kernels  14.3 us (26%)
  starting transfers between devices  14.1 us (25%)
  waiting for transfers between devices  13.5 us (24%)
  matrix products  6.71 us (12%)
  local copies, waits for them, and re-layouts  4.91 us (9%)
  between operations  0.93 us (2%)
  other arithmetic  0.87 us (2%)
    pallas_call x8, Pallas kernels, call(): return lambda *args: run(*[flags[name] for name in names], *args)  14.3 us
    ppermute x10, waiting for transfers between devices, swapped(): return lax.ppermute(value, axis, [(i, i ^ step) for i in range(count)])  13.5 us
    ppermute x10, starting transfers between devices, swapped(): return lax.ppermute(value, axis, [(i, i ^ step) for i in range(count)])  11.1 us
    unnamed x34, local copies, waits for them, and re-layouts  4.9 us
    dot_general x1, matrix products, local(): jnp.einsum('td,dce->cte', hidden_in, w_qk, preferred_element_type=F32)  3.77 us
    ppermute x1, starting transfers between devices, local(): lax.ppermute(ends, 'seq', [(i, (i + 1) % n_seq) for i in range(n_seq)])  2.99 us
    dot_general x1, matrix products, local(): gate_z = jnp.dot(later, w_outgate, preferred_element_type=F32).astype(BF16)  1.29 us
    dot_general x1, matrix products, local(): value = jnp.dot(hidden_in, w_value, preferred_element_type=F32).astype(BF16)  1.28 us
  transfers between devices with their start and end apart: 11, of which 6 were waited for; matrix products, arithmetic and copies ran while one was open for 3% of the time, Pallas kernels for 19%

profile of v5, /device:TPU:0, one launch (start us, length us, event | category | flops | bytes accessed | tf_op | source)
XLA Modules:
  0.0 55.3 jit_solution(7035196231797497206)
XLA Ops:
  0.7 1.2 %copy-done = bf16[256,2048]{1,0:T(8,128)(2,1)S(1)} copy-done((bf16[256,2048]{1,0:T(8,128)(2,1)S(1)}, bf16[256,2048]{1,0:T(8,128)(2,1)}, u32[]{:S(2)}) %copy-start) | copy-done | bytes 1048600
  1.9 3.8 %fusion.5.refs_3_.refs_2_.refs_1_ = bf16[2,256,512]{2,1,0:T(8,128)(2,1)S(1)} fusion(bf16[2048,2,512]{2,1,0:T(2,128)(2,1)} %param.16, bf16[256,2048]{1,0:T(8,128)(2,1)S(1)} %copy-done), kind=kOutput, calls=%fused_computation.5 | convolution fusion | flops 1074003968 | bytes 5767168 | tf_op jit(solution)/shard_map/td,dce->cte/dot_general | solution.py:553
  5.8 1.3 %convolution_convert_fusion.1.refs_4_.refs_3_ = bf16[256,1024]{1,0:T(8,128)(2,1)S(1)} fusion(bf16[256,2048]{1,0:T(8,128)(2,1)S(1)} %copy-done, bf16[2048,1024]{1,0:T(8,128)(2,1)S(1)} %copy-done.15), kind=kOutput, calls=%fused_computation.4 | convolution fusion | flops 1074003968 | bytes 5767168 | tf_op jit(solution)/shard_map/dot_general | solution.py:554
  7.1 3.0 %collective-permute-start = (bf16[8,2048]{1,0:T(8,128)(2,1)S(1)}, bf16[8,2048]{1,0:T(8,128)(2,1)S(1)}, u32[]{:S(2)}, u32[]{:S(2)}) collective-permute-start(bf16[8,2048]{1,0:T(8,128)(2,1)S(1)} %pad_maximum_fusion), channel_id=1, source_target_pairs={{0,4},{4,8},{8,12},{12,16},{16,20},{20,24},{24,28},{28,0},{1,5},{5... | collective-permute-start | bytes 98312 | tf_op jit(solution)/shard_map/ppermute | solution.py:557
  10.1 0.4 convolution_convert_fusion.2.refs_5_
  10.5 5.8 %shard_map.158 = (bf16[4,256,128]{2,1,0:T(8,128)(2,1)S(1)}, bf16[8,256,256]{2,1,0:T(8,128)(2,1)S(1)}, f32[8,128,256]{2,1,0:T(8,128)S(1)}, f32[8,256]{1,0:T(8,128)S(1)}, f32[256,128]{1,0:T(8,128)S(1)}) custom-call(f32[1,8]{1,0:T(1,128)S(1)} %bitcast.27, f32[1,8]{1,0:T(1,128)S(1)} %bitcast.28, f32[1,8]{1,0:T(1,128)S(1)} %bitcast.29, ...), custom_call_target="tpu_custom_call" | custom-call | flops 10000000 | bytes 25165824 | tf_op jit(solution)/shard_map/pallas_call | solution.py:86
  16.3 1.0 %shard_map.159 = (bf16[8,128,256]{2,1,0:T(8,128)(2,1)S(1)}, f32[4,16,128]{2,1,0:T(8,128)S(1)}, f32[8,16,256]{2,1,0:T(8,128)S(1)}, bf16[2,128,256]{2,1,0:T(8,128)...) custom-call(s32[1]{0:T(128)} %bitcast.4.refs_0_, s32[1]{0:T(128)} %bitcast.refs_1_.refs_0_, ...), custom_call_target="tpu_custom_call" | custom-call | flops 10000000 | bytes 50331648 | tf_op jit(solution)/shard_map/pallas_call | solution.py:86
  17.4 1.6 %collective-permute-start.1 = (bf16[2,128,256]{2,1,0:T(8,128)(2,1)S(1)}, bf16[2,128,256]{2,1,0:T(8,128)(2,1)S(1)}, u32[]{:S(2)}, u32[]{:S(2)}) collective-permute-start(bf16[2,128,256]{2,1,0:T(8,128)(2,1)S(1)} %get-tuple-element.43), channel_id=1, source_target_pairs={{0,4},{4,0},{8,12},{12,8},{16,20},{20,16},{24,28},{28,24},{1,5},{5... | collective-permute-start | bytes 393224 | tf_op jit(solution)/shard_map/ppermute | solution.py:520
  19.0 1.6 %collective-permute-start.2 = (bf16[2,128,256]{2,1,0:T(8,128)(2,1)S(1)}, bf16[2,128,256]{2,1,0:T(8,128)(2,1)S(1)}, u32[]{:S(2)}, u32[]{:S(2)}) collective-permute-start(bf16[2,128,256]{2,1,0:T(8,128)(2,1)S(1)} %get-tuple-element.44), channel_id=1, source_target_pairs={{0,8},{4,12},{8,0},{12,4},{16,24},{20,28},{24,16},{28,20},{1,9},{5... | collective-permute-start | bytes 393224 | tf_op jit(solution)/shard_map/ppermute | solution.py:520
  20.6 0.4 collective-permute-start.3
  21.0 2.6 %shard_map.160 = (bf16[8,256,128]{2,1,0:T(8,128)(2,1)S(1)}, f32[8,256,128]{2,1,0:T(8,128)S(1)}) custom-call(s32[1]{0:T(128)} %bitcast.4.refs_0_, bf16[2,256,512]{2,1,0:T(8,128)(2,1)S(1)} %fusion.5.refs_3_.refs_2_.refs_1_, bf16[8,2048]{1,0:T(8,128)(2,1)S(1)} %collective-permute-done.refs_4_.refs_2_, bf16[3,2,512]{2,1,0:T(2,128)(2,1)S(1)} %copy-done.4, ...), custom_call_target="tpu_custom_call" | custom-call | flops 99999997952 | bytes 6291456 | tf_op jit(solution)/shard_map/pallas_call | solution.py:86
  23.6 1.5 %collective-permute-done.2.refs_3_.refs_4_ = bf16[2,128,256]{2,1,0:T(8,128)(2,1)S(1)} collective-permute-done((bf16[2,128,256]{2,1,0:T(8,128)(2,1)S(1)}, bf16[2,128,256]{2,1,0:T(8,128)(2,1)S(1)}, u32[]{:S(2)}, u32[]{:S(2)}) %collective-permute-start.2) | collective-permute-done | bytes 131104 | tf_op jit(solution)/shard_map/ppermute | solution.py:520
  25.1 1.6 %collective-permute-done.3.refs_4_.refs_5_ = bf16[2,128,256]{2,1,0:T(8,128)(2,1)S(1)} collective-permute-done((bf16[2,128,256]{2,1,0:T(8,128)(2,1)S(1)}, bf16[2,128,256]{2,1,0:T(8,128)(2,1)S(1)}, u32[]{:S(2)}, u32[]{:S(2)}) %collective-permute-start.3) | collective-permute-done | bytes 131104 | tf_op jit(solution)/shard_map/ppermute | solution.py:520
  26.7 0.8 %shard_map.161 = bf16[2,128,128]{2,1,0:T(8,128)(2,1)S(1)} custom-call(s32[1]{0:T(128)} %bitcast.refs_1_.refs_0_, bf16[8,128,256]{2,1,0:T(8,128)(2,1)S(1)} %get-tuple-element.42.refs_1_.refs_2_.refs_6_, bf16[2,128,256]{2,1,0:T(8,128)(2,1)S(1)} %collective-permute-done.1.refs_2_.refs_3_, bf16[2,128,256]{2,1,0:T(8,128)(2,1)S(1)} %collective-permute-done.2.refs_3_.refs_4_, ...), custom_call_target="tpu_custom_call" | custom-call | flops 24000000000 | bytes 50331648 | tf_op jit(solution)/shard_map/pallas_call | solution.py:86
  27.5 2.4 %collective-permute-start.4 = (bf16[2,128,128]{2,1,0:T(8,128)(2,1)S(1)}, bf16[2,128,128]{2,1,0:T(8,128)(2,1)S(1)}, u32[]{:S(2)}, u32[]{:S(2)}) collective-permute-start(bf16[2,128,128]{2,1,0:T(8,128)(2,1)S(1)} %shard_map.161), channel_id=1, source_target_pairs={{0,16},{4,20},{8,24},{12,28},{16,0},{20,4},{24,8},{28,12},{1,17},{... | collective-permute-start | bytes 196616 | tf_op jit(solution)/shard_map/ppermute | solution.py:520
  29.9 1.3 %convolution_convert_fusion.refs_8_.refs_6_ = bf16[256,1024]{1,0:T(8,128)(2,1)S(1)} fusion(bf16[256,2048]{1,0:T(8,128)(2,1)S(1)} %copy-done, bf16[2048,1024]{1,0:T(8,128)(2,1)S(1)} %copy-done.16), kind=kOutput, calls=%fused_computation.3 | convolution fusion | flops 1074003968 | bytes 5767168 | tf_op jit(solution)/shard_map/dot_general | solution.py:641
  31.2 1.6 %collective-permute-done.4.refs_7_ = bf16[2,128,128]{2,1,0:T(8,128)(2,1)S(1)} collective-permute-done((bf16[2,128,128]{2,1,0:T(8,128)(2,1)S(1)}, bf16[2,128,128]{2,1,0:T(8,128)(2,1)S(1)}, u32[]{:S(2)}, u32[]{:S(2)}) %collective-permute-start.4) | collective-permute-done | bytes 65568 | tf_op jit(solution)/shard_map/ppermute | solution.py:520
  32.8 1.1 %shard_map.162 = (bf16[2,128,128]{2,1,0:T(8,128)(2,1)S(1)}, bf16[2,128,128]{2,1,0:T(8,128)(2,1)S(1)}, bf16[2,128,128]{2,1,0:T(8,128)(2,1)S(1)}, bf16[2,128,128]{2,1,0:T(8,128)(2,1)}) custom-call(s32[1]{0:T(128)} %bitcast.refs_1_.refs_0_, s32[1]{0:T(128)} %bitcast.3.refs_1_, bf16[8,128,256]{2,1,0:T(8,128)(2,1)S(1)} %get-tuple-element.42.refs_1_.refs_2_.refs_6_, ...), custom_call_target="tpu_custom_call" | custom-call | flops 600000000 | bytes 25165824 | tf_op jit(solution)/shard_map/pallas_call | solution.py:86
  33.9 2.3 %collective-permute-start.5 = (bf16[2,128,128]{2,1,0:T(8,128)(2,1)}, bf16[2,128,128]{2,1,0:T(8,128)(2,1)S(1)}, u32[]{:S(2)}, u32[]{:S(2)}) collective-permute-start(bf16[2,128,128]{2,1,0:T(8,128)(2,1)} %get-tuple-element.60), channel_id=1, source_target_pairs={{0,12},{4,8},{8,4},{12,0},{16,28},{20,24},{24,20},{28,16},{1,13},{... | collective-permute-start | bytes 196616 | tf_op jit(solution)/shard_map/ppermute | solution.py:520
  36.1 0.5 collective-permute-start.6
  36.6 0.7 %collective-permute-start.7 = (bf16[2,128,128]{2,1,0:T(8,128)(2,1)S(1)}, bf16[2,128,128]{2,1,0:T(8,128)(2,1)S(1)}, u32[]{:S(2)}, u32[]{:S(2)}) collective-permute-start(bf16[2,128,128]{2,1,0:T(8,128)(2,1)S(1)} %get-tuple-element.65), channel_id=1, source_target_pairs={{0,8},{4,12},{8,0},{12,4},{16,24},{20,28},{24,16},{28,20},{1,9},{5... | collective-permute-start | bytes 196616 | tf_op jit(solution)/shard_map/ppermute | solution.py:520
  37.4 1.9 %collective-permute-done.5.refs_4_.refs_10_ = bf16[2,128,128]{2,1,0:T(8,128)(2,1)S(1)} collective-permute-done((bf16[2,128,128]{2,1,0:T(8,128)(2,1)}, bf16[2,128,128]{2,1,0:T(8,128)(2,1)S(1)}, u32[]{:S(2)}, u32[]{:S(2)}) %collective-permute-start.5) | collective-permute-done | bytes 65568 | tf_op jit(solution)/shard_map/ppermute | solution.py:520
  39.2 1.2 %collective-permute-done.6.refs_5_.refs_8_ = bf16[2,128,128]{2,1,0:T(8,128)(2,1)S(1)} collective-permute-done((bf16[2,128,128]{2,1,0:T(8,128)(2,1)S(1)}, bf16[2,128,128]{2,1,0:T(8,128)(2,1)S(1)}, u32[]{:S(2)}, u32[]{:S(2)}) %collective-permute-start.6) | collective-permute-done | bytes 65568 | tf_op jit(solution)/shard_map/ppermute | solution.py:520
  40.4 0.6 %shard_map.163.refs_8_.refs_3_ = bf16[3,256,256]{2,1,0:T(8,128)(2,1)S(1)} custom-call(s32[1]{0:T(128)} %bitcast.refs_1_.refs_0_, s32[1]{0:T(128)} %bitcast.1.refs_1_, s32[1]{0:T(128)} %bitcast.2.refs_2_, bf16[2,128,128]{2,1,0:T(8,128)(2,1)S(1)} %get-tuple-element.59.refs_3_.refs_7_, bf16[2,128,128]{2,1,0:T(8,128)(2,1)S(1)} %collective-permute-done.5.refs_4_.refs_10_, ...), custom_call_target="tpu_custom_call" | custom-call | flops 1000000 | bytes 25165824 | tf_op jit(solution)/shard_map/pallas_call | solution.py:86
  41.0 2.2 %copy-done.9 = bf16[1024,2048]{1,0:T(8,128)(2,1)S(1)} copy-done((bf16[1024,2048]{1,0:T(8,128)(2,1)S(1)}, bf16[1024,2048]{1,0:T(8,128)(2,1)}, u32[]{:S(2)}) %copy-start.9) | copy-done | bytes 4194328
  43.2 0.8 %shard_map.164 = (bf16[1,256,256]{2,1,0:T(8,128)(2,1)S(1)}, bf16[1,256,512]{2,1,0:T(8,128)(2,1)S(1)}, bf16[1,256,512]{2,1,0:T(8,128)(2,1)S(1)}) custom-call(s32[1]{0:T(128)} %bitcast.refs_1_.refs_0_, s32[1]{0:T(128)} %bitcast.1.refs_1_, s32[1]{0:T(128)} %bitcast.2.refs_2_, bf16[2,128,128]{2,1,0:T(8,128)(2,1)S(1)} %collective-permute-done.7.refs_3_.refs_9_, ...), custom_call_target="tpu_custom_call" | custom-call | flops 99999997952 | bytes 50331648 | tf_op jit(solution)/shard_map/pallas_call | solution.py:86
  44.1 1.3 %copy-done.10 = bf16[1024,2048]{1,0:T(8,128)(2,1)S(1)} copy-done((bf16[1024,2048]{1,0:T(8,128)(2,1)S(1)}, bf16[1024,2048]{1,0:T(8,128)(2,1)}, u32[]{:S(2)}) %copy-start.10) | copy-done | bytes 4194328
  45.4 0.1 copy-done.13
  45.5 1.6 %shard_map.165 = (bf16[1,256,512]{2,1,0:T(8,128)(2,1)S(1)}, bf16[1,256,512]{2,1,0:T(8,128)(2,1)S(1)}, f32[1,8,128,128]{3,2,1,0:T(8,128)}) custom-call(s32[1]{0:T(128)} %bitcast.refs_1_.refs_0_, s32[1]{0:T(128)} %bitcast.1.refs_1_, s32[1]{0:T(128)} %bitcast.2.refs_2_, bf16[3,256,256]{2,1,0:T(8,128)(2,1)S(1)} %shard_map.163.refs_8_.refs_3_, ...), custom_call_target="tpu_custom_call" | custom-call | flops 6000000000 | bytes 25165824 | tf_op jit(solution)/shard_map/pallas_call | solution.py:86
  47.2 1.6 %collective-permute-start.10 = (bf16[1,256,512]{2,1,0:T(8,128)(2,1)S(1)}, bf16[1,256,512]{2,1,0:T(8,128)(2,1)S(1)}, u32[]{:S(2)}, u32[]{:S(2)}) collective-permute-start(bf16[1,256,512]{2,1,0:T(8,128)(2,1)S(1)} %add_convert_fusion.1), channel_id=1, source_target_pairs={{0,2},{1,3},{2,0},{3,1},{4,6},{5,7},{6,4},{7,5},{8,10},{9,11},{10,... | collective-permute-start | bytes 786440 | tf_op jit(solution)/shard_map/ppermute | solution.py:520
  48.7 5.8 %collective-permute-done.10 = bf16[1,256,512]{2,1,0:T(8,128)(2,1)S(1)} collective-permute-done((bf16[1,256,512]{2,1,0:T(8,128)(2,1)S(1)}, bf16[1,256,512]{2,1,0:T(8,128)(2,1)S(1)}, u32[]{:S(2)}, u32[]{:S(2)}) %collective-permute-start.10) | collective-permute-done | bytes 262176 | tf_op jit(solution)/shard_map/ppermute | solution.py:520
  54.5 0.8 %fusion.10 = bf16[256,512]{1,0:T(8,128)(2,1)} fusion(bf16[1,256,512]{2,1,0:T(8,128)(2,1)S(1)} %collective-permute-done.10, bf16[1,256,512]{2,1,0:T(8,128)(2,1)S(1)} %collective-permute-done.9, bf16[1,256,512]{2,1,0:T(8,128)(2,1)S(1)} %get-tuple-element.67), kind=kLoop, calls=%fused_computation.11 | loop fusion | flops 786432 | bytes 1048576 | tf_op jit(solution)/shard_map/convert_element_type | solution.py:698
  (41 shorter events, 0.3 us)
Async XLA Ops:
  0.6 1.2 %copy-start = (bf16[256,2048]{1,0:T(8,128)(2,1)S(1)}, bf16[256,2048]{1,0:T(8,128)(2,1)}, u32[]{:S(2)}) copy-start(bf16[256,2048]{1,0:T(8,128)(2,1)} %param.15) | copy-start | bytes 3145732
  0.6 5.0 %copy-start.15 = (bf16[2048,1024]{1,0:T(8,128)(2,1)S(1)}, bf16[2048,1024]{1,0:T(8,128)(2,1)}, u32[]{:S(2)}) copy-start(bf16[2048,1024]{1,0:T(8,128)(2,1)} %param.17) | copy-start | bytes 12582916
  5.6 4.4 %copy-start.14 = (bf16[2048,2,8]{0,2,1:T(8,128)(2,1)S(1)}, bf16[2048,2,8]{0,2,1:T(8,128)(2,1)}, u32[]{:S(2)}) copy-start(bf16[2048,2,8]{0,2,1:T(8,128)(2,1)} %param.19) | copy-start | bytes 196612
  5.7 4.8 %copy-start.1 = (bf16[4,1024]{1,0:T(4,128)(2,1)S(1)}, bf16[4,1024]{1,0:T(4,128)(2,1)}, u32[]{:S(2)}) copy-start(bf16[4,1024]{1,0:T(4,128)(2,1)} %refs_8_.1) | copy-start | bytes 24580
  5.7 4.8 %copy-start.2 = (bf16[4,2,512]{2,1,0:T(2,128)(2,1)S(1)}, bf16[4,2,512]{2,1,0:T(2,128)(2,1)}, u32[]{:S(2)}) copy-start(bf16[4,2,512]{2,1,0:T(2,128)(2,1)} %refs_4_.1) | copy-start | bytes 24580
  5.7 4.8 %copy-start.5 = (f32[8]{0:T(128)S(1)}, f32[8]{0:T(128)}, u32[]{:S(2)}) copy-start(f32[8]{0:T(128)} %param.24) | copy-start | bytes 100
  5.7 4.8 %copy-start.6 = (f32[8]{0:T(128)S(1)}, f32[8]{0:T(128)}, u32[]{:S(2)}) copy-start(f32[8]{0:T(128)} %param.25) | copy-start | bytes 100
  5.7 4.8 %copy-start.7 = (f32[8]{0:T(128)S(1)}, f32[8]{0:T(128)}, u32[]{:S(2)}) copy-start(f32[8]{0:T(128)} %param.26) | copy-start | bytes 100
  5.7 10.6 %copy-start.3 = (bf16[3,1024]{1,0:T(4,128)(2,1)S(1)}, bf16[3,1024]{1,0:T(4,128)(2,1)}, u32[]{:S(2)}) copy-start(bf16[3,1024]{1,0:T(4,128)(2,1)} %refs_6_.4) | copy-start | bytes 18436
  5.7 10.6 %copy-start.4 = (bf16[3,2,512]{2,1,0:T(2,128)(2,1)S(1)}, bf16[3,2,512]{2,1,0:T(2,128)(2,1)}, u32[]{:S(2)}) copy-start(bf16[3,2,512]{2,1,0:T(2,128)(2,1)} %refs_3_.1) | copy-start | bytes 18436
  7.1 9.3 %collective-permute-start = (bf16[8,2048]{1,0:T(8,128)(2,1)S(1)}, bf16[8,2048]{1,0:T(8,128)(2,1)S(1)}, u32[]{:S(2)}, u32[]{:S(2)}) collective-permute-start(bf16[8,2048]{1,0:T(8,128)(2,1)S(1)} %pad_maximum_fusion), channel_id=1, source_target_pairs={{0,4},{4,8},{8,12},{12,16},{16,20},{20,24},{24,28},{28,0},{1,5},{5... | collective-permute-start | bytes 98312 | tf_op jit(solution)/shard_map/ppermute | solution.py:557
  17.4 15.4 %copy-start.12 = (bf16[8,128,256]{2,1,0:T(8,128)(2,1)}, bf16[8,128,256]{2,1,0:T(8,128)(2,1)S(1)}, u32[]{:S(2)}) copy-start(bf16[8,128,256]{2,1,0:T(8,128)(2,1)S(1)} %get-tuple-element.42.refs_1_.refs_2_.refs_6_) | copy-start | bytes 1572868
  17.4 6.2 %collective-permute-start.1 = (bf16[2,128,256]{2,1,0:T(8,128)(2,1)S(1)}, bf16[2,128,256]{2,1,0:T(8,128)(2,1)S(1)}, u32[]{:S(2)}, u32[]{:S(2)}) collective-permute-start(bf16[2,128,256]{2,1,0:T(8,128)(2,1)S(1)} %get-tuple-element.43), channel_id=1, source_target_pairs={{0,4},{4,0},{8,12},{12,8},{16,20},{20,16},{24,28},{28,24},{1,5},{5... | collective-permute-start | bytes 393224 | tf_op jit(solution)/shard_map/ppermute | solution.py:520
  19.0 6.1 %collective-permute-start.2 = (bf16[2,128,256]{2,1,0:T(8,128)(2,1)S(1)}, bf16[2,128,256]{2,1,0:T(8,128)(2,1)S(1)}, u32[]{:S(2)}, u32[]{:S(2)}) collective-permute-start(bf16[2,128,256]{2,1,0:T(8,128)(2,1)S(1)} %get-tuple-element.44), channel_id=1, source_target_pairs={{0,8},{4,12},{8,0},{12,4},{16,24},{20,28},{24,16},{28,20},{1,9},{5... | collective-permute-start | bytes 393224 | tf_op jit(solution)/shard_map/ppermute | solution.py:520
  20.6 6.1 %collective-permute-start.3 = (bf16[2,128,256]{2,1,0:T(8,128)(2,1)S(1)}, bf16[2,128,256]{2,1,0:T(8,128)(2,1)S(1)}, u32[]{:S(2)}, u32[]{:S(2)}) collective-permute-start(bf16[2,128,256]{2,1,0:T(8,128)(2,1)S(1)} %get-tuple-element.45), channel_id=1, source_target_pairs={{0,12},{4,8},{8,4},{12,0},{16,28},{20,24},{24,20},{28,16},{1,13},{... | collective-permute-start | bytes 393224 | tf_op jit(solution)/shard_map/ppermute | solution.py:520
  21.0 5.8 %copy-start.11 = (f32[8,128,128]{2,1,0:T(8,128)S(1)}, f32[8,128,128]{2,1,0:T(8,128)}, u32[]{:S(2)}) copy-start(f32[8,128,128]{2,1,0:T(8,128)} %refs_6_.5) | copy-start | bytes 1572868
  26.7 3.2 %copy-start.16 = (bf16[2048,1024]{1,0:T(8,128)(2,1)S(1)}, bf16[2048,1024]{1,0:T(8,128)(2,1)}, u32[]{:S(2)}) copy-start(bf16[2048,1024]{1,0:T(8,128)(2,1)} %param.18) | copy-start | bytes 12582916
  27.5 12.9 %copy-start.8 = (f32[128]{0:T(128)S(1)}, f32[128]{0:T(128)}, u32[]{:S(2)}) copy-start(f32[128]{0:T(128)} %param.28) | copy-start | bytes 1540
  27.5 5.2 %collective-permute-start.4 = (bf16[2,128,128]{2,1,0:T(8,128)(2,1)S(1)}, bf16[2,128,128]{2,1,0:T(8,128)(2,1)S(1)}, u32[]{:S(2)}, u32[]{:S(2)}) collective-permute-start(bf16[2,128,128]{2,1,0:T(8,128)(2,1)S(1)} %shard_map.161), channel_id=1, source_target_pairs={{0,16},{4,20},{8,24},{12,28},{16,0},{20,4},{24,8},{28,12},{1,17},{... | collective-permute-start | bytes 196616 | tf_op jit(solution)/shard_map/ppermute | solution.py:520
  33.9 5.4 %collective-permute-start.5 = (bf16[2,128,128]{2,1,0:T(8,128)(2,1)}, bf16[2,128,128]{2,1,0:T(8,128)(2,1)S(1)}, u32[]{:S(2)}, u32[]{:S(2)}) collective-permute-start(bf16[2,128,128]{2,1,0:T(8,128)(2,1)} %get-tuple-element.60), channel_id=1, source_target_pairs={{0,12},{4,8},{8,4},{12,0},{16,28},{20,24},{24,20},{28,16},{1,13},{... | collective-permute-start | bytes 196616 | tf_op jit(solution)/shard_map/ppermute | solution.py:520
  36.1 4.3 %collective-permute-start.6 = (bf16[2,128,128]{2,1,0:T(8,128)(2,1)S(1)}, bf16[2,128,128]{2,1,0:T(8,128)(2,1)S(1)}, u32[]{:S(2)}, u32[]{:S(2)}) collective-permute-start(bf16[2,128,128]{2,1,0:T(8,128)(2,1)S(1)} %get-tuple-element.61), channel_id=1, source_target_pairs={{0,4},{4,0},{8,12},{12,8},{16,20},{20,16},{24,28},{28,24},{1,5},{5... | collective-permute-start | bytes 196616 | tf_op jit(solution)/shard_map/ppermute | solution.py:520
  36.6 4.4 %collective-permute-start.7 = (bf16[2,128,128]{2,1,0:T(8,128)(2,1)S(1)}, bf16[2,128,128]{2,1,0:T(8,128)(2,1)S(1)}, u32[]{:S(2)}, u32[]{:S(2)}) collective-permute-start(bf16[2,128,128]{2,1,0:T(8,128)(2,1)S(1)} %get-tuple-element.65), channel_id=1, source_target_pairs={{0,8},{4,12},{8,0},{12,4},{16,24},{20,28},{24,16},{28,20},{1,9},{5... | collective-permute-start | bytes 196616 | tf_op jit(solution)/shard_map/ppermute | solution.py:520
  41.0 2.2 %copy-start.9 = (bf16[1024,2048]{1,0:T(8,128)(2,1)S(1)}, bf16[1024,2048]{1,0:T(8,128)(2,1)}, u32[]{:S(2)}) copy-start(bf16[1024,2048]{1,0:T(8,128)(2,1)} %refs_5_.5) | copy-start | bytes 12582916
  43.2 2.2 %copy-start.10 = (bf16[1024,2048]{1,0:T(8,128)(2,1)S(1)}, bf16[1024,2048]{1,0:T(8,128)(2,1)}, u32[]{:S(2)}) copy-start(bf16[1024,2048]{1,0:T(8,128)(2,1)} %refs_5_.5) | copy-start | bytes 12582916
  43.2 2.3 %copy-start.13 = (bf16[8,128,256]{2,1,0:T(8,128)(2,1)S(1)}, bf16[8,128,256]{2,1,0:T(8,128)(2,1)}, u32[]{:S(2)}) copy-start(bf16[8,128,256]{2,1,0:T(8,128)(2,1)} %copy-done.12) | copy-start | bytes 1572868
  44.0 3.1 %collective-permute-start.8 = (bf16[1,256,512]{2,1,0:T(8,128)(2,1)S(1)}, bf16[1,256,512]{2,1,0:T(8,128)(2,1)S(1)}, u32[]{:S(2)}, u32[]{:S(2)}) collective-permute-start(bf16[1,256,512]{2,1,0:T(8,128)(2,1)S(1)} %get-tuple-element.68), channel_id=1, source_target_pairs={{0,1},{1,0},{2,3},{3,2},{4,5},{5,4},{6,7},{7,6},{8,9},{9,8},{10,11... | collective-permute-start | bytes 786440 | tf_op jit(solution)/shard_map/ppermute | solution.py:520
  47.2 7.4 %collective-permute-start.10 = (bf16[1,256,512]{2,1,0:T(8,128)(2,1)S(1)}, bf16[1,256,512]{2,1,0:T(8,128)(2,1)S(1)}, u32[]{:S(2)}, u32[]{:S(2)}) collective-permute-start(bf16[1,256,512]{2,1,0:T(8,128)(2,1)S(1)} %add_convert_fusion.1), channel_id=1, source_target_pairs={{0,2},{1,3},{2,0},{3,1},{4,6},{5,7},{6,4},{7,5},{8,10},{9,11},{10,... | collective-permute-start | bytes 786440 | tf_op jit(solution)/shard_map/ppermute | solution.py:520
  48.7 5.8 %collective-permute-start.9 = (bf16[1,256,512]{2,1,0:T(8,128)(2,1)S(1)}, bf16[1,256,512]{2,1,0:T(8,128)(2,1)S(1)}, u32[]{:S(2)}, u32[]{:S(2)}) collective-permute-start(bf16[1,256,512]{2,1,0:T(8,128)(2,1)S(1)} %get-tuple-element.70), channel_id=1, source_target_pairs={{0,1},{1,0},{2,3},{3,2},{4,5},{5,4},{6,7},{7,6},{8,9},{9,8},{10,11... | collective-permute-start | bytes 786440 | tf_op jit(solution)/shard_map/ppermute | solution.py:520

commit v6 on v5

--- a/solution.py
+++ b/solution.py
@@ -681,7 +681,6 @@
         25165824,
         flags=side,
     )(early_rows, late_rows, w_out, maps, *states)
-    came_out, home_out = lax.optimization_barrier((came_out, home_out))
     total_out = (keep.astype(F32) + came_out.astype(F32)).astype(BF16)
     came_far = swapped(total_out, "head", 2)
     came_home = swapped(home_out, "head", 1)

time: 55.5 us -> 56.9 us (1.025)
  waiting for transfers between devices: 13.5 us -> 14.9 us
    ppermute x10, waiting for transfers between devices: 13.5 us -> 14.9 us  [swapped(): return lax.ppermute(value, axis, [(i, i ^ step) for i in range(count)])]
where the time goes in v6:
time: 56.9 us; the launch traced here: 56.8 us
  waiting for transfers between devices  14.9 us (26%)
  Pallas kernels  14.3 us (25%)
  starting transfers between devices  14.1 us (25%)
  matrix products  6.71 us (12%)
  local copies, waits for them, and re-layouts  4.91 us (9%)
  between operations  0.93 us (2%)
  other arithmetic  0.87 us (2%)
    ppermute x10, waiting for transfers between devices, swapped(): return lax.ppermute(value, axis, [(i, i ^ step) for i in range(count)])  14.9 us
    pallas_call x8, Pallas kernels, call(): return lambda *args: run(*[flags[name] for name in names], *args)  14.3 us
    ppermute x10, starting transfers between devices, swapped(): return lax.ppermute(value, axis, [(i, i ^ step) for i in range(count)])  11.1 us
    unnamed x34, local copies, waits for them, and re-layouts  4.9 us
    dot_general x1, matrix products, local(): jnp.einsum('td,dce->cte', hidden_in, w_qk, preferred_element_type=F32)  3.77 us
    ppermute x1, starting transfers between devices, local(): lax.ppermute(ends, 'seq', [(i, (i + 1) % n_seq) for i in range(n_seq)])  2.99 us
    dot_general x1, matrix products, local(): gate_z = jnp.dot(later, w_outgate, preferred_element_type=F32).astype(BF16)  1.29 us
    dot_general x1, matrix products, local(): value = jnp.dot(hidden_in, w_value, preferred_element_type=F32).astype(BF16)  1.28 us
  transfers between devices with their start and end apart: 11, of which 6 were waited for; matrix products, arithmetic and copies ran while one was open for 3% of the time, Pallas kernels for 19%

profile of v6, /device:TPU:0, one launch (start us, length us, event | category | flops | bytes accessed | tf_op | source)
XLA Modules:
  0.0 56.8 jit_solution(4175320191130308655)
XLA Ops:
  0.7 1.2 %copy-done = bf16[256,2048]{1,0:T(8,128)(2,1)S(1)} copy-done((bf16[256,2048]{1,0:T(8,128)(2,1)S(1)}, bf16[256,2048]{1,0:T(8,128)(2,1)}, u32[]{:S(2)}) %copy-start) | copy-done | bytes 1048600
  1.9 3.8 %fusion.5.refs_3_.refs_2_.refs_1_ = bf16[2,256,512]{2,1,0:T(8,128)(2,1)S(1)} fusion(bf16[2048,2,512]{2,1,0:T(2,128)(2,1)} %param.16, bf16[256,2048]{1,0:T(8,128)(2,1)S(1)} %copy-done), kind=kOutput, calls=%fused_computation.5 | convolution fusion | flops 1074003968 | bytes 5767168 | tf_op jit(solution)/shard_map/td,dce->cte/dot_general | solution.py:553
  5.8 1.3 %convolution_convert_fusion.1.refs_4_.refs_3_ = bf16[256,1024]{1,0:T(8,128)(2,1)S(1)} fusion(bf16[256,2048]{1,0:T(8,128)(2,1)S(1)} %copy-done, bf16[2048,1024]{1,0:T(8,128)(2,1)S(1)} %copy-done.15), kind=kOutput, calls=%fused_computation.4 | convolution fusion | flops 1074003968 | bytes 5767168 | tf_op jit(solution)/shard_map/dot_general | solution.py:554
  7.1 3.0 %collective-permute-start = (bf16[8,2048]{1,0:T(8,128)(2,1)S(1)}, bf16[8,2048]{1,0:T(8,128)(2,1)S(1)}, u32[]{:S(2)}, u32[]{:S(2)}) collective-permute-start(bf16[8,2048]{1,0:T(8,128)(2,1)S(1)} %pad_maximum_fusion), channel_id=1, source_target_pairs={{0,4},{4,8},{8,12},{12,16},{16,20},{20,24},{24,28},{28,0},{1,5},{5... | collective-permute-start | bytes 98312 | tf_op jit(solution)/shard_map/ppermute | solution.py:557
  10.1 0.4 convolution_convert_fusion.2.refs_5_
  10.5 5.8 %shard_map.158 = (bf16[4,256,128]{2,1,0:T(8,128)(2,1)S(1)}, bf16[8,256,256]{2,1,0:T(8,128)(2,1)S(1)}, f32[8,128,256]{2,1,0:T(8,128)S(1)}, f32[8,256]{1,0:T(8,128)S(1)}, f32[256,128]{1,0:T(8,128)S(1)}) custom-call(f32[1,8]{1,0:T(1,128)S(1)} %bitcast.27, f32[1,8]{1,0:T(1,128)S(1)} %bitcast.28, f32[1,8]{1,0:T(1,128)S(1)} %bitcast.29, ...), custom_call_target="tpu_custom_call" | custom-call | flops 10000000 | bytes 25165824 | tf_op jit(solution)/shard_map/pallas_call | solution.py:86
  16.3 1.0 %shard_map.159 = (bf16[8,128,256]{2,1,0:T(8,128)(2,1)S(1)}, f32[4,16,128]{2,1,0:T(8,128)S(1)}, f32[8,16,256]{2,1,0:T(8,128)S(1)}, bf16[2,128,256]{2,1,0:T(8,128)...) custom-call(s32[1]{0:T(128)} %bitcast.4.refs_0_, s32[1]{0:T(128)} %bitcast.refs_1_.refs_0_, ...), custom_call_target="tpu_custom_call" | custom-call | flops 10000000 | bytes 50331648 | tf_op jit(solution)/shard_map/pallas_call | solution.py:86
  17.4 1.6 %collective-permute-start.1 = (bf16[2,128,256]{2,1,0:T(8,128)(2,1)S(1)}, bf16[2,128,256]{2,1,0:T(8,128)(2,1)S(1)}, u32[]{:S(2)}, u32[]{:S(2)}) collective-permute-start(bf16[2,128,256]{2,1,0:T(8,128)(2,1)S(1)} %get-tuple-element.41), channel_id=1, source_target_pairs={{0,4},{4,0},{8,12},{12,8},{16,20},{20,16},{24,28},{28,24},{1,5},{5... | collective-permute-start | bytes 393224 | tf_op jit(solution)/shard_map/ppermute | solution.py:520
  19.0 1.6 %collective-permute-start.2 = (bf16[2,128,256]{2,1,0:T(8,128)(2,1)S(1)}, bf16[2,128,256]{2,1,0:T(8,128)(2,1)S(1)}, u32[]{:S(2)}, u32[]{:S(2)}) collective-permute-start(bf16[2,128,256]{2,1,0:T(8,128)(2,1)S(1)} %get-tuple-element.42), channel_id=1, source_target_pairs={{0,8},{4,12},{8,0},{12,4},{16,24},{20,28},{24,16},{28,20},{1,9},{5... | collective-permute-start | bytes 393224 | tf_op jit(solution)/shard_map/ppermute | solution.py:520
  20.6 0.4 collective-permute-start.3
  21.0 2.6 %shard_map.160 = (bf16[8,256,128]{2,1,0:T(8,128)(2,1)S(1)}, f32[8,256,128]{2,1,0:T(8,128)S(1)}) custom-call(s32[1]{0:T(128)} %bitcast.4.refs_0_, bf16[2,256,512]{2,1,0:T(8,128)(2,1)S(1)} %fusion.5.refs_3_.refs_2_.refs_1_, bf16[8,2048]{1,0:T(8,128)(2,1)S(1)} %collective-permute-done.refs_4_.refs_2_, bf16[3,2,512]{2,1,0:T(2,128)(2,1)S(1)} %copy-done.4, ...), custom_call_target="tpu_custom_call" | custom-call | flops 99999997952 | bytes 6291456 | tf_op jit(solution)/shard_map/pallas_call | solution.py:86
  23.6 1.5 %collective-permute-done.2.refs_3_.refs_4_ = bf16[2,128,256]{2,1,0:T(8,128)(2,1)S(1)} collective-permute-done((bf16[2,128,256]{2,1,0:T(8,128)(2,1)S(1)}, bf16[2,128,256]{2,1,0:T(8,128)(2,1)S(1)}, u32[]{:S(2)}, u32[]{:S(2)}) %collective-permute-start.2) | collective-permute-done | bytes 131104 | tf_op jit(solution)/shard_map/ppermute | solution.py:520
  25.1 1.6 %collective-permute-done.3.refs_4_.refs_5_ = bf16[2,128,256]{2,1,0:T(8,128)(2,1)S(1)} collective-permute-done((bf16[2,128,256]{2,1,0:T(8,128)(2,1)S(1)}, bf16[2,128,256]{2,1,0:T(8,128)(2,1)S(1)}, u32[]{:S(2)}, u32[]{:S(2)}) %collective-permute-start.3) | collective-permute-done | bytes 131104 | tf_op jit(solution)/shard_map/ppermute | solution.py:520
  26.7 0.8 %shard_map.161 = bf16[2,128,128]{2,1,0:T(8,128)(2,1)S(1)} custom-call(s32[1]{0:T(128)} %bitcast.refs_1_.refs_0_, bf16[8,128,256]{2,1,0:T(8,128)(2,1)S(1)} %get-tuple-element.40.refs_1_.refs_2_.refs_6_, bf16[2,128,256]{2,1,0:T(8,128)(2,1)S(1)} %collective-permute-done.1.refs_2_.refs_3_, bf16[2,128,256]{2,1,0:T(8,128)(2,1)S(1)} %collective-permute-done.2.refs_3_.refs_4_, ...), custom_call_target="tpu_custom_call" | custom-call | flops 24000000000 | bytes 50331648 | tf_op jit(solution)/shard_map/pallas_call | solution.py:86
  27.5 2.4 %collective-permute-start.4 = (bf16[2,128,128]{2,1,0:T(8,128)(2,1)S(1)}, bf16[2,128,128]{2,1,0:T(8,128)(2,1)S(1)}, u32[]{:S(2)}, u32[]{:S(2)}) collective-permute-start(bf16[2,128,128]{2,1,0:T(8,128)(2,1)S(1)} %shard_map.161), channel_id=1, source_target_pairs={{0,16},{4,20},{8,24},{12,28},{16,0},{20,4},{24,8},{28,12},{1,17},{... | collective-permute-start | bytes 196616 | tf_op jit(solution)/shard_map/ppermute | solution.py:520
  29.9 1.3 %convolution_convert_fusion.refs_8_.refs_6_ = bf16[256,1024]{1,0:T(8,128)(2,1)S(1)} fusion(bf16[256,2048]{1,0:T(8,128)(2,1)S(1)} %copy-done, bf16[2048,1024]{1,0:T(8,128)(2,1)S(1)} %copy-done.16), kind=kOutput, calls=%fused_computation.3 | convolution fusion | flops 1074003968 | bytes 5767168 | tf_op jit(solution)/shard_map/dot_general | solution.py:641
  31.2 1.6 %collective-permute-done.4.refs_7_ = bf16[2,128,128]{2,1,0:T(8,128)(2,1)S(1)} collective-permute-done((bf16[2,128,128]{2,1,0:T(8,128)(2,1)S(1)}, bf16[2,128,128]{2,1,0:T(8,128)(2,1)S(1)}, u32[]{:S(2)}, u32[]{:S(2)}) %collective-permute-start.4) | collective-permute-done | bytes 65568 | tf_op jit(solution)/shard_map/ppermute | solution.py:520
  32.8 1.1 %shard_map.162 = (bf16[2,128,128]{2,1,0:T(8,128)(2,1)S(1)}, bf16[2,128,128]{2,1,0:T(8,128)(2,1)S(1)}, bf16[2,128,128]{2,1,0:T(8,128)(2,1)S(1)}, bf16[2,128,128]{2,1,0:T(8,128)(2,1)}) custom-call(s32[1]{0:T(128)} %bitcast.refs_1_.refs_0_, s32[1]{0:T(128)} %bitcast.3.refs_1_, bf16[8,128,256]{2,1,0:T(8,128)(2,1)S(1)} %get-tuple-element.40.refs_1_.refs_2_.refs_6_, ...), custom_call_target="tpu_custom_call" | custom-call | flops 600000000 | bytes 25165824 | tf_op jit(solution)/shard_map/pallas_call | solution.py:86
  33.9 2.3 %collective-permute-start.5 = (bf16[2,128,128]{2,1,0:T(8,128)(2,1)}, bf16[2,128,128]{2,1,0:T(8,128)(2,1)S(1)}, u32[]{:S(2)}, u32[]{:S(2)}) collective-permute-start(bf16[2,128,128]{2,1,0:T(8,128)(2,1)} %get-tuple-element.58), channel_id=1, source_target_pairs={{0,12},{4,8},{8,4},{12,0},{16,28},{20,24},{24,20},{28,16},{1,13},{... | collective-permute-start | bytes 196616 | tf_op jit(solution)/shard_map/ppermute | solution.py:520
  36.1 0.5 collective-permute-start.6
  36.6 0.7 %collective-permute-start.7 = (bf16[2,128,128]{2,1,0:T(8,128)(2,1)S(1)}, bf16[2,128,128]{2,1,0:T(8,128)(2,1)S(1)}, u32[]{:S(2)}, u32[]{:S(2)}) collective-permute-start(bf16[2,128,128]{2,1,0:T(8,128)(2,1)S(1)} %get-tuple-element.63), channel_id=1, source_target_pairs={{0,8},{4,12},{8,0},{12,4},{16,24},{20,28},{24,16},{28,20},{1,9},{5... | collective-permute-start | bytes 196616 | tf_op jit(solution)/shard_map/ppermute | solution.py:520
  37.4 1.9 %collective-permute-done.5.refs_4_.refs_10_ = bf16[2,128,128]{2,1,0:T(8,128)(2,1)S(1)} collective-permute-done((bf16[2,128,128]{2,1,0:T(8,128)(2,1)}, bf16[2,128,128]{2,1,0:T(8,128)(2,1)S(1)}, u32[]{:S(2)}, u32[]{:S(2)}) %collective-permute-start.5) | collective-permute-done | bytes 65568 | tf_op jit(solution)/shard_map/ppermute | solution.py:520
  39.2 1.2 %collective-permute-done.6.refs_5_.refs_8_ = bf16[2,128,128]{2,1,0:T(8,128)(2,1)S(1)} collective-permute-done((bf16[2,128,128]{2,1,0:T(8,128)(2,1)S(1)}, bf16[2,128,128]{2,1,0:T(8,128)(2,1)S(1)}, u32[]{:S(2)}, u32[]{:S(2)}) %collective-permute-start.6) | collective-permute-done | bytes 65568 | tf_op jit(solution)/shard_map/ppermute | solution.py:520
  40.4 0.6 %shard_map.163.refs_8_.refs_3_ = bf16[3,256,256]{2,1,0:T(8,128)(2,1)S(1)} custom-call(s32[1]{0:T(128)} %bitcast.refs_1_.refs_0_, s32[1]{0:T(128)} %bitcast.1.refs_1_, s32[1]{0:T(128)} %bitcast.2.refs_2_, bf16[2,128,128]{2,1,0:T(8,128)(2,1)S(1)} %get-tuple-element.57.refs_3_.refs_7_, bf16[2,128,128]{2,1,0:T(8,128)(2,1)S(1)} %collective-permute-done.5.refs_4_.refs_10_, ...), custom_call_target="tpu_custom_call" | custom-call | flops 1000000 | bytes 25165824 | tf_op jit(solution)/shard_map/pallas_call | solution.py:86
  41.0 2.2 %copy-done.9 = bf16[1024,2048]{1,0:T(8,128)(2,1)S(1)} copy-done((bf16[1024,2048]{1,0:T(8,128)(2,1)S(1)}, bf16[1024,2048]{1,0:T(8,128)(2,1)}, u32[]{:S(2)}) %copy-start.9) | copy-done | bytes 4194328
  43.2 0.8 %shard_map.164 = (bf16[1,256,256]{2,1,0:T(8,128)(2,1)S(1)}, bf16[1,256,512]{2,1,0:T(8,128)(2,1)S(1)}, bf16[1,256,512]{2,1,0:T(8,128)(2,1)S(1)}) custom-call(s32[1]{0:T(128)} %bitcast.refs_1_.refs_0_, s32[1]{0:T(128)} %bitcast.1.refs_1_, s32[1]{0:T(128)} %bitcast.2.refs_2_, bf16[2,128,128]{2,1,0:T(8,128)(2,1)S(1)} %collective-permute-done.7.refs_3_.refs_9_, ...), custom_call_target="tpu_custom_call" | custom-call | flops 99999997952 | bytes 50331648 | tf_op jit(solution)/shard_map/pallas_call | solution.py:86
  44.1 1.3 %copy-done.10 = bf16[1024,2048]{1,0:T(8,128)(2,1)S(1)} copy-done((bf16[1024,2048]{1,0:T(8,128)(2,1)S(1)}, bf16[1024,2048]{1,0:T(8,128)(2,1)}, u32[]{:S(2)}) %copy-start.10) | copy-done | bytes 4194328
  45.4 0.1 copy-done.13
  45.5 1.6 %shard_map.165 = (bf16[1,256,512]{2,1,0:T(8,128)(2,1)S(1)}, bf16[1,256,512]{2,1,0:T(8,128)(2,1)S(1)}, f32[1,8,128,128]{3,2,1,0:T(8,128)}) custom-call(s32[1]{0:T(128)} %bitcast.refs_1_.refs_0_, s32[1]{0:T(128)} %bitcast.1.refs_1_, s32[1]{0:T(128)} %bitcast.2.refs_2_, bf16[3,256,256]{2,1,0:T(8,128)(2,1)S(1)} %shard_map.163.refs_8_.refs_3_, ...), custom_call_target="tpu_custom_call" | custom-call | flops 6000000000 | bytes 25165824 | tf_op jit(solution)/shard_map/pallas_call | solution.py:86
  47.2 1.6 %collective-permute-start.10 = (bf16[1,256,512]{2,1,0:T(8,128)(2,1)S(1)}, bf16[1,256,512]{2,1,0:T(8,128)(2,1)S(1)}, u32[]{:S(2)}, u32[]{:S(2)}) collective-permute-start(bf16[1,256,512]{2,1,0:T(8,128)(2,1)S(1)} %add_convert_fusion.1), channel_id=1, source_target_pairs={{0,2},{1,3},{2,0},{3,1},{4,6},{5,7},{6,4},{7,5},{8,10},{9,11},{10,... | collective-permute-start | bytes 786440 | tf_op jit(solution)/shard_map/ppermute | solution.py:520
  48.8 7.2 %collective-permute-done.10 = bf16[1,256,512]{2,1,0:T(8,128)(2,1)S(1)} collective-permute-done((bf16[1,256,512]{2,1,0:T(8,128)(2,1)S(1)}, bf16[1,256,512]{2,1,0:T(8,128)(2,1)S(1)}, u32[]{:S(2)}, u32[]{:S(2)}) %collective-permute-start.10) | collective-permute-done | bytes 262176 | tf_op jit(solution)/shard_map/ppermute | solution.py:520
  55.9 0.8 %fusion.10 = bf16[256,512]{1,0:T(8,128)(2,1)} fusion(bf16[1,256,512]{2,1,0:T(8,128)(2,1)S(1)} %collective-permute-done.10, bf16[1,256,512]{2,1,0:T(8,128)(2,1)S(1)} %collective-permute-done.8, bf16[1,256,512]{2,1,0:T(8,128)(2,1)S(1)} %get-tuple-element.65), kind=kLoop, calls=%fused_computation.11 | loop fusion | flops 786432 | bytes 1048576 | tf_op jit(solution)/shard_map/convert_element_type | solution.py:697
  (41 shorter events, 0.3 us)
Async XLA Ops:
  0.6 1.2 %copy-start = (bf16[256,2048]{1,0:T(8,128)(2,1)S(1)}, bf16[256,2048]{1,0:T(8,128)(2,1)}, u32[]{:S(2)}) copy-start(bf16[256,2048]{1,0:T(8,128)(2,1)} %param.15) | copy-start | bytes 3145732
  0.6 5.0 %copy-start.15 = (bf16[2048,1024]{1,0:T(8,128)(2,1)S(1)}, bf16[2048,1024]{1,0:T(8,128)(2,1)}, u32[]{:S(2)}) copy-start(bf16[2048,1024]{1,0:T(8,128)(2,1)} %param.17) | copy-start | bytes 12582916
  5.6 4.4 %copy-start.14 = (bf16[2048,2,8]{0,2,1:T(8,128)(2,1)S(1)}, bf16[2048,2,8]{0,2,1:T(8,128)(2,1)}, u32[]{:S(2)}) copy-start(bf16[2048,2,8]{0,2,1:T(8,128)(2,1)} %param.19) | copy-start | bytes 196612
  5.7 4.8 %copy-start.1 = (bf16[4,1024]{1,0:T(4,128)(2,1)S(1)}, bf16[4,1024]{1,0:T(4,128)(2,1)}, u32[]{:S(2)}) copy-start(bf16[4,1024]{1,0:T(4,128)(2,1)} %refs_8_.1) | copy-start | bytes 24580
  5.7 4.8 %copy-start.2 = (bf16[4,2,512]{2,1,0:T(2,128)(2,1)S(1)}, bf16[4,2,512]{2,1,0:T(2,128)(2,1)}, u32[]{:S(2)}) copy-start(bf16[4,2,512]{2,1,0:T(2,128)(2,1)} %refs_4_.1) | copy-start | bytes 24580
  5.7 4.8 %copy-start.5 = (f32[8]{0:T(128)S(1)}, f32[8]{0:T(128)}, u32[]{:S(2)}) copy-start(f32[8]{0:T(128)} %param.24) | copy-start | bytes 100
  5.7 4.8 %copy-start.6 = (f32[8]{0:T(128)S(1)}, f32[8]{0:T(128)}, u32[]{:S(2)}) copy-start(f32[8]{0:T(128)} %param.25) | copy-start | bytes 100
  5.7 4.8 %copy-start.7 = (f32[8]{0:T(128)S(1)}, f32[8]{0:T(128)}, u32[]{:S(2)}) copy-start(f32[8]{0:T(128)} %param.26) | copy-start | bytes 100
  5.7 10.6 %copy-start.3 = (bf16[3,1024]{1,0:T(4,128)(2,1)S(1)}, bf16[3,1024]{1,0:T(4,128)(2,1)}, u32[]{:S(2)}) copy-start(bf16[3,1024]{1,0:T(4,128)(2,1)} %refs_6_.4) | copy-start | bytes 18436
  5.7 10.6 %copy-start.4 = (bf16[3,2,512]{2,1,0:T(2,128)(2,1)S(1)}, bf16[3,2,512]{2,1,0:T(2,128)(2,1)}, u32[]{:S(2)}) copy-start(bf16[3,2,512]{2,1,0:T(2,128)(2,1)} %refs_3_.1) | copy-start | bytes 18436
  7.1 9.3 %collective-permute-start = (bf16[8,2048]{1,0:T(8,128)(2,1)S(1)}, bf16[8,2048]{1,0:T(8,128)(2,1)S(1)}, u32[]{:S(2)}, u32[]{:S(2)}) collective-permute-start(bf16[8,2048]{1,0:T(8,128)(2,1)S(1)} %pad_maximum_fusion), channel_id=1, source_target_pairs={{0,4},{4,8},{8,12},{12,16},{16,20},{20,24},{24,28},{28,0},{1,5},{5... | collective-permute-start | bytes 98312 | tf_op jit(solution)/shard_map/ppermute | solution.py:557
  17.4 15.4 %copy-start.12 = (bf16[8,128,256]{2,1,0:T(8,128)(2,1)}, bf16[8,128,256]{2,1,0:T(8,128)(2,1)S(1)}, u32[]{:S(2)}) copy-start(bf16[8,128,256]{2,1,0:T(8,128)(2,1)S(1)} %get-tuple-element.40.refs_1_.refs_2_.refs_6_) | copy-start | bytes 1572868
  17.4 6.2 %collective-permute-start.1 = (bf16[2,128,256]{2,1,0:T(8,128)(2,1)S(1)}, bf16[2,128,256]{2,1,0:T(8,128)(2,1)S(1)}, u32[]{:S(2)}, u32[]{:S(2)}) collective-permute-start(bf16[2,128,256]{2,1,0:T(8,128)(2,1)S(1)} %get-tuple-element.41), channel_id=1, source_target_pairs={{0,4},{4,0},{8,12},{12,8},{16,20},{20,16},{24,28},{28,24},{1,5},{5... | collective-permute-start | bytes 393224 | tf_op jit(solution)/shard_map/ppermute | solution.py:520
  19.0 6.1 %collective-permute-start.2 = (bf16[2,128,256]{2,1,0:T(8,128)(2,1)S(1)}, bf16[2,128,256]{2,1,0:T(8,128)(2,1)S(1)}, u32[]{:S(2)}, u32[]{:S(2)}) collective-permute-start(bf16[2,128,256]{2,1,0:T(8,128)(2,1)S(1)} %get-tuple-element.42), channel_id=1, source_target_pairs={{0,8},{4,12},{8,0},{12,4},{16,24},{20,28},{24,16},{28,20},{1,9},{5... | collective-permute-start | bytes 393224 | tf_op jit(solution)/shard_map/ppermute | solution.py:520
  20.6 6.1 %collective-permute-start.3 = (bf16[2,128,256]{2,1,0:T(8,128)(2,1)S(1)}, bf16[2,128,256]{2,1,0:T(8,128)(2,1)S(1)}, u32[]{:S(2)}, u32[]{:S(2)}) collective-permute-start(bf16[2,128,256]{2,1,0:T(8,128)(2,1)S(1)} %get-tuple-element.43), channel_id=1, source_target_pairs={{0,12},{4,8},{8,4},{12,0},{16,28},{20,24},{24,20},{28,16},{1,13},{... | collective-permute-start | bytes 393224 | tf_op jit(solution)/shard_map/ppermute | solution.py:520
  21.0 5.8 %copy-start.11 = (f32[8,128,128]{2,1,0:T(8,128)S(1)}, f32[8,128,128]{2,1,0:T(8,128)}, u32[]{:S(2)}) copy-start(f32[8,128,128]{2,1,0:T(8,128)} %refs_6_.5) | copy-start | bytes 1572868
  26.7 3.2 %copy-start.16 = (bf16[2048,1024]{1,0:T(8,128)(2,1)S(1)}, bf16[2048,1024]{1,0:T(8,128)(2,1)}, u32[]{:S(2)}) copy-start(bf16[2048,1024]{1,0:T(8,128)(2,1)} %param.18) | copy-start | bytes 12582916
  27.5 12.9 %copy-start.8 = (f32[128]{0:T(128)S(1)}, f32[128]{0:T(128)}, u32[]{:S(2)}) copy-start(f32[128]{0:T(128)} %param.28) | copy-start | bytes 1540
  27.5 5.2 %collective-permute-start.4 = (bf16[2,128,128]{2,1,0:T(8,128)(2,1)S(1)}, bf16[2,128,128]{2,1,0:T(8,128)(2,1)S(1)}, u32[]{:S(2)}, u32[]{:S(2)}) collective-permute-start(bf16[2,128,128]{2,1,0:T(8,128)(2,1)S(1)} %shard_map.161), channel_id=1, source_target_pairs={{0,16},{4,20},{8,24},{12,28},{16,0},{20,4},{24,8},{28,12},{1,17},{... | collective-permute-start | bytes 196616 | tf_op jit(solution)/shard_map/ppermute | solution.py:520
  33.9 5.4 %collective-permute-start.5 = (bf16[2,128,128]{2,1,0:T(8,128)(2,1)}, bf16[2,128,128]{2,1,0:T(8,128)(2,1)S(1)}, u32[]{:S(2)}, u32[]{:S(2)}) collective-permute-start(bf16[2,128,128]{2,1,0:T(8,128)(2,1)} %get-tuple-element.58), channel_id=1, source_target_pairs={{0,12},{4,8},{8,4},{12,0},{16,28},{20,24},{24,20},{28,16},{1,13},{... | collective-permute-start | bytes 196616 | tf_op jit(solution)/shard_map/ppermute | solution.py:520
  36.1 4.3 %collective-permute-start.6 = (bf16[2,128,128]{2,1,0:T(8,128)(2,1)S(1)}, bf16[2,128,128]{2,1,0:T(8,128)(2,1)S(1)}, u32[]{:S(2)}, u32[]{:S(2)}) collective-permute-start(bf16[2,128,128]{2,1,0:T(8,128)(2,1)S(1)} %get-tuple-element.59), channel_id=1, source_target_pairs={{0,4},{4,0},{8,12},{12,8},{16,20},{20,16},{24,28},{28,24},{1,5},{5... | collective-permute-start | bytes 196616 | tf_op jit(solution)/shard_map/ppermute | solution.py:520
  36.6 4.4 %collective-permute-start.7 = (bf16[2,128,128]{2,1,0:T(8,128)(2,1)S(1)}, bf16[2,128,128]{2,1,0:T(8,128)(2,1)S(1)}, u32[]{:S(2)}, u32[]{:S(2)}) collective-permute-start(bf16[2,128,128]{2,1,0:T(8,128)(2,1)S(1)} %get-tuple-element.63), channel_id=1, source_target_pairs={{0,8},{4,12},{8,0},{12,4},{16,24},{20,28},{24,16},{28,20},{1,9},{5... | collective-permute-start | bytes 196616 | tf_op jit(solution)/shard_map/ppermute | solution.py:520
  41.0 2.2 %copy-start.9 = (bf16[1024,2048]{1,0:T(8,128)(2,1)S(1)}, bf16[1024,2048]{1,0:T(8,128)(2,1)}, u32[]{:S(2)}) copy-start(bf16[1024,2048]{1,0:T(8,128)(2,1)} %refs_5_.5) | copy-start | bytes 12582916
  43.2 2.2 %copy-start.10 = (bf16[1024,2048]{1,0:T(8,128)(2,1)S(1)}, bf16[1024,2048]{1,0:T(8,128)(2,1)}, u32[]{:S(2)}) copy-start(bf16[1024,2048]{1,0:T(8,128)(2,1)} %refs_5_.5) | copy-start | bytes 12582916
  43.2 2.3 %copy-start.13 = (bf16[8,128,256]{2,1,0:T(8,128)(2,1)S(1)}, bf16[8,128,256]{2,1,0:T(8,128)(2,1)}, u32[]{:S(2)}) copy-start(bf16[8,128,256]{2,1,0:T(8,128)(2,1)} %copy-done.12) | copy-start | bytes 1572868
  44.0 3.1 %collective-permute-start.9 = (bf16[1,256,512]{2,1,0:T(8,128)(2,1)S(1)}, bf16[1,256,512]{2,1,0:T(8,128)(2,1)S(1)}, u32[]{:S(2)}, u32[]{:S(2)}) collective-permute-start(bf16[1,256,512]{2,1,0:T(8,128)(2,1)S(1)} %get-tuple-element.68), channel_id=1, source_target_pairs={{0,1},{1,0},{2,3},{3,2},{4,5},{5,4},{6,7},{7,6},{8,9},{9,8},{10,11... | collective-permute-start | bytes 786440 | tf_op jit(solution)/shard_map/ppermute | solution.py:520
  47.1 1.7 %collective-permute-start.8 = (bf16[1,256,512]{2,1,0:T(8,128)(2,1)S(1)}, bf16[1,256,512]{2,1,0:T(8,128)(2,1)S(1)}, u32[]{:S(2)}, u32[]{:S(2)}) collective-permute-start(bf16[1,256,512]{2,1,0:T(8,128)(2,1)S(1)} %get-tuple-element.66), channel_id=1, source_target_pairs={{0,1},{1,0},{2,3},{3,2},{4,5},{5,4},{6,7},{7,6},{8,9},{9,8},{10,11... | collective-permute-start | bytes 786440 | tf_op jit(solution)/shard_map/ppermute | solution.py:520
  47.2 8.8 %collective-permute-start.10 = (bf16[1,256,512]{2,1,0:T(8,128)(2,1)S(1)}, bf16[1,256,512]{2,1,0:T(8,128)(2,1)S(1)}, u32[]{:S(2)}, u32[]{:S(2)}) collective-permute-start(bf16[1,256,512]{2,1,0:T(8,128)(2,1)S(1)} %add_convert_fusion.1), channel_id=1, source_target_pairs={{0,2},{1,3},{2,0},{3,1},{4,6},{5,7},{6,4},{7,5},{8,10},{9,11},{10,... | collective-permute-start | bytes 786440 | tf_op jit(solution)/shard_map/ppermute | solution.py:520
